TPU v7x, 256 devices: a whole 4x4x8 slice. The times are simulated.
256 devices in a mesh: grp: 4 (over y_hi, core), dp: 64 (over x, y_lo, z).
Axes of the slice: x: 4, y: 4 (y_hi: 2, y_lo: 2; y = y_hi * 2 + y_lo), z: 8, core: 2. Of those that a mesh axis runs over, the one named last changes fastest.
Arguments:
- normed: bfloat16 [32768, 704], P(('grp', 'dp')), may hold values from -6 to 6
- pre_gelu: bfloat16 [32768, 2816], P(('grp', 'dp')), may hold values from -45 to 45
- out_grad: bfloat16 [32768, 2816], P(('grp', 'dp')), may hold values from -24 to 24
- grn_gain: float32 [2816], replicated, may hold values from -4 to 4
Outputs:
- pre_grad: bfloat16 [32768, 2816], P(('grp', 'dp'))
- w_up_grad: float32 [2816, 704], P(('grp', 'dp'))
- gain_grad: float32 [2816], P(('grp', 'dp'))
- shift_grad: float32 [2816], P(('grp', 'dp'))
- bias_grad: float32 [2816], P(('grp', 'dp'))
All inputs are finite; a program needn't handle non-finite values.
Results may differ from a plain program's by a relative error of at most 0.007.
Values sent between devices are 32-bit elements; how exact they have to be, the bound alone decides.
No kernel may reach another device: no remote copies, remote signals or barrier semaphores. Data moves between devices by JAX's collectives and lax.ppermute only.
A program may use at most 64 MiB of HBM per device.

v0:
```python
import jax
import jax.numpy as jnp
from jax import lax
from jax.sharding import PartitionSpec as P

root_half = 0.7071067811865476
inv_root_two_pi = 0.3989422804014327


def partner(x, axis, distance):
    return lax.ppermute(x, axis, [(i, i ^ 1 << distance) for i in range(lax.axis_size(axis))])


def gelu_pair(pre_gelu):
    values = pre_gelu.astype(jnp.float32)
    cdf = 0.5 * (1.0 + jax.scipy.special.erf(values * root_half))
    gelu_out = values * cdf
    gelu_slope = cdf + values * jnp.exp(-0.5 * values * values) * inv_root_two_pi
    return (gelu_out, gelu_slope)


def on_device(normed, pre_gelu, out_grad, grn_gain):
    units = grn_gain.shape[0]
    gelu_out, gelu_slope = gelu_pair(pre_gelu)
    upstream = out_grad.astype(jnp.float32)
    own_squares = jnp.sum(gelu_out * gelu_out, axis=0)
    own_response = jnp.sum(upstream * gelu_out, axis=0)
    other_squares, other_response = partner((own_squares, own_response), "dp", 0)
    squares = own_squares + other_squares
    response = own_response + other_response
    channel_norm = jnp.sqrt(squares + 1e-06)
    norm_mean = jnp.mean(channel_norm) + 1e-06
    scaled = channel_norm / norm_mean
    scaled_grad = grn_gain * response
    norm_grad = scaled_grad / norm_mean - jnp.sum(scaled_grad * channel_norm) / (
        units * norm_mean * norm_mean
    )
    act_grad = upstream * (grn_gain * scaled + 1.0) + gelu_out * (norm_grad / channel_norm)
    pre_grad = (act_grad * gelu_slope).astype(jnp.bfloat16)
    gain_term = own_response * scaled
    shift_term = jnp.sum(upstream, axis=0)
    bias_term = jnp.sum(pre_grad.astype(jnp.float32), axis=0)
    gain_grad, shift_grad, bias_grad = (
        lax.psum_scatter(gain_term, ("grp", "dp"), scatter_dimension=0, tiled=True),
        lax.psum_scatter(shift_term, ("grp", "dp"), scatter_dimension=0, tiled=True),
        lax.psum_scatter(bias_term, ("grp", "dp"), scatter_dimension=0, tiled=True),
    )
    w_up_grad = lax.psum_scatter(
        lax.dot_general(
            pre_grad, normed, (((0,), (0,)), ((), ())), preferred_element_type=jnp.float32
        ),
        ("grp", "dp"),
        scatter_dimension=0,
        tiled=True,
    )
    return (pre_grad, w_up_grad, gain_grad, shift_grad, bias_grad)


def solution(mesh):
    in_specs = (P(("grp", "dp"), None), P(("grp", "dp"), None), P(("grp", "dp"), None), P())
    out_specs = (
        P(("grp", "dp"), None),
        P(("grp", "dp"), None),
        P(("grp", "dp")),
        P(("grp", "dp")),
        P(("grp", "dp")),
    )
    return jax.shard_map(
        on_device, mesh=mesh, in_specs=in_specs, out_specs=out_specs, check_vma=False
    )
```

profile of v0, /device:TPU:8, one launch (start us, length us, event | category | flops | bytes accessed | tf_op | source)
XLA Modules:
  0.0 312.5 jit_solution(14334698664945266833)
XLA Ops:
  7.2 0.0 copy-start
  7.2 0.0 copy-start.2
  7.2 0.0 copy-start.3
  7.2 0.0 all-reduce.7.cloned.1.call-start
  7.2 2.1 fusion.3
  9.4 2.0 collective-permute-start
  11.4 0.1 collective-permute-start.1
  11.5 1.7 collective-permute-done
  13.2 1.9 collective-permute-done.1
  15.1 0.0 copy-done.3
  15.1 0.6 fusion.11
  17.0 0.0 copy-done.2
  17.0 1.9 convert_reduce_fusion.1
  18.9 0.0 copy-start.1
  18.9 0.0 copy-done
  18.9 4.6 %fusion.14 = f32[2816,704]{1,0:T(8,128)} fusion(bf16[128,2816]{1,0:T(8,128)(2,1)S(1)} %get-tuple-element.14, bf16[128,704]{0,1:T(8,128)(2,1)S(1)} %copy-done), kind=kOutput, calls=%fused_computation.29 | convolution fusion | flops 507510784 | bytes 8830976 | tf_op jit(solution)/shard_map/dot_general | solution.py:49
  23.6 0.0 copy-done.1
  23.6 0.0 all-reduce.7.cloned.1.call-update
  23.6 78.9 %all-reduce.4 = (f32[2816]{0:T(1024)S(1)}, f32[2816]{0:T(1024)S(1)}, f32[2816]{0:T(1024)S(1)}) all-reduce(f32[2816]{0:T(1024)S(1)} %get-tuple-element.17, f32[2816]{0:T(1024)S(1)} %get-tuple-element.7, f32[2816]{0:T(1024)S(1)} %get-tuple-element.13), channel_id=3, replica_groups=mesh['grp'=4,'dp'=64] {'grp','dp'}, use_global_device_ids=true, to_apply=%region_5.0.clone | all-reduce | flops 8448 | bytes 67584
  102.5 0.6 dynamic-slice.1
  103.1 0.6 dynamic-slice.2
  103.7 0.6 dynamic-slice.3
  104.2 199.9 %all-reduce.7.cloned.1.call-done = f32[2816,704]{1,0:T(8,128)} async-done(((f32[2816,704]{1,0:T(8,128)}), f32[2816,704]{1,0:T(8,128)}) %all-reduce.7.cloned.1.call-update) | async-done | bytes 7929872
  304.2 1.5 constant_dynamic-slice_fusion
  (1 shorter events, 0.0 us)
Async XLA Ops:
  7.2 11.8 %copy-start = (bf16[128,704]{0,1:T(8,128)(2,1)S(1)}, bf16[128,704]{0,1:T(8,128)(2,1)}, u32[]{:S(2)}) copy-start(bf16[128,704]{0,1:T(8,128)(2,1)} %param.4) | copy-start | bytes 540676
  7.2 9.8 %copy-start.2 = (bf16[128,2816]{1,0:T(8,128)(2,1)S(1)}, bf16[128,2816]{1,0:T(8,128)(2,1)}, u32[]{:S(2)}) copy-start(bf16[128,2816]{1,0:T(8,128)(2,1)} %param.6) | copy-start | bytes 2162692
  7.2 7.9 %copy-start.3 = (f32[2816]{0:T(1024)S(1)}, f32[2816]{0:T(1024)}, u32[]{:S(2)}) copy-start(f32[2816]{0:T(1024)} %param.7) | copy-start | bytes 33796
  7.2 296.9 %all-reduce.7.cloned.1.call-start = ((), (), s32[]{:S(2)}) async-start(), calls=%async_computation | async-start | bytes 17301504
  9.4 3.8 %collective-permute-start = (f32[2816]{0:T(1024)S(1)}, f32[2816]{0:T(1024)S(1)}, u32[]{:S(2)}, u32[]{:S(2)}) collective-permute-start(f32[2816]{0:T(1024)S(1)} %get-tuple-element.6), channel_id=1, source_target_pairs={{0,1},{1,0},{2,3},{3,2},{4,5},{5,4},{6,7},{7,6},{8,9},{9,8},{10,11... | collective-permute-start | bytes 33800 | tf_op jit(solution)/shard_map/ppermute | solution.py:11
  11.4 3.7 %collective-permute-start.1 = (f32[2816]{0:T(1024)S(1)}, f32[2816]{0:T(1024)S(1)}, u32[]{:S(2)}, u32[]{:S(2)}) collective-permute-start(f32[2816]{0:T(1024)S(1)} %get-tuple-element.5), channel_id=1, source_target_pairs={{0,1},{1,0},{2,3},{3,2},{4,5},{5,4},{6,7},{7,6},{8,9},{9,8},{10,11... | collective-permute-start | bytes 33800 | tf_op jit(solution)/shard_map/ppermute | solution.py:11
  18.9 4.7 %copy-start.1 = (bf16[128,2816]{1,0:T(8,128)(2,1)}, bf16[128,2816]{1,0:T(8,128)(2,1)S(1)}, u32[]{:S(2)}) copy-start(bf16[128,2816]{1,0:T(8,128)(2,1)S(1)} %get-tuple-element.14) | copy-start | bytes 2162692
Sparse Core Ops, SparseCore 0:
  23.7 280.4 all-reduce.6
where the time goes:
time: 313 us
  waiting for transfers between devices  204 us (65%)
  blocking collectives  78.9 us (25%)
  between operations  15.4 us (5%)
  matrix products  4.63 us (1%)
  other arithmetic  4.62 us (1%)
  local copies, waits for them, and re-layouts  3.29 us (1%)
    unnamed x2, waiting for transfers between devices  200 us
    unnamed x1, blocking collectives  78.9 us
  transfers between devices with their start and end apart: 3, of which 3 were waited for; matrix products, arithmetic and copies ran while one was open for 1% of the time, Pallas kernels for 0%

commit v1 on v0

v1 whole, which is shorter than its diff:
```python
import jax
import jax.numpy as jnp
import numpy as np
from jax import lax
from jax.experimental import pallas as pl
from jax.experimental.pallas import tpu as pltpu
from jax.sharding import Mesh, PartitionSpec as P

root_half = 0.7071067811865476
inv_root_two_pi = 0.3989422804014327

AXES = ("yh", "core", "x", "yl", "z")
SIZES = (2, 2, 4, 2, 8)
ROWS = 128
C = 704
H = 2816
BLOCK = 88
OWN = 11
LANES = 128
MIB = 1 << 20


def pairs(target):
    found = []
    for i in range(256):
        yh, core, x, yl, z = (int(v) for v in np.unravel_index(i, SIZES))
        core2, x2, y2, z2 = target(core, x, 2 * yh + yl, z)
        place = (y2 // 2 % 2, core2 % 2, x2 % 4, y2 % 2, z2 % 8)
        found.append((i, int(np.ravel_multi_index(place, SIZES))))
    return found


def send(value, target):
    return lax.ppermute(value, AXES, pairs(target))


def other_core(core, x, y, z):
    return 1 - core, x, y, z


def other_half(core, x, y, z):
    return core, x, y, z ^ 1


def along(k):
    return lambda core, x, y, z: (core, x + k, y, z) if core == 0 else (core, x, y + k, z)


def across(k):
    return lambda core, x, y, z: (1, x, y + k, z) if core == 0 else (0, x + k, y, z)


def beside(k):
    return lambda core, x, y, z: (core, x, y + k, z) if core == 0 else (core, x + k, y, z)


def call(body, out_shape, scratch=(), flops=0, moved=0, limit=24):
    return pl.pallas_call(
        body,
        out_shape=out_shape,
        scratch_shapes=scratch,
        compiler_params=pltpu.CompilerParams(vmem_limit_bytes=limit * MIB),
        cost_estimate=pl.CostEstimate(flops=flops, bytes_accessed=moved, transcendentals=0),
    )


def f32(*shape):
    return jax.ShapeDtypeStruct(shape, jnp.float32)


def widen(normed, wide):
    for k in range(5):
        wide[k * ROWS : (k + 1) * ROWS, :] = normed[:, k * LANES : (k + 1) * LANES].astype(jnp.float32)
    last = normed[:, 5 * LANES : C].astype(jnp.float32)
    wide[5 * ROWS : C, :] = jnp.concatenate([last[: ROWS // 2], last[ROWS // 2 :]], axis=1)


def narrow(*refs):
    *wides, out = refs
    lane = lax.broadcasted_iota(jnp.int32, (ROWS, LANES - 64), 1)
    ones = jnp.where(lane == 0, 1.0, 0.0)
    for s, wide in enumerate(wides):
        rows = slice(s * ROWS, (s + 1) * ROWS)
        for k in range(5):
            out[rows, k * LANES : (k + 1) * LANES] = wide[k * ROWS : (k + 1) * ROWS, :].astype(jnp.bfloat16)
        last = wide[5 * ROWS : C, :]
        both = jnp.concatenate([last[:, :64], last[:, 64:]], axis=0)
        out[rows, 5 * LANES :] = jnp.concatenate([both, ones], axis=1).astype(jnp.bfloat16)


def statistics(pre_gelu, out_grad, sums, shift, gelu, slope):
    for k in range(H // LANES):
        cols = slice(k * LANES, (k + 1) * LANES)
        values = pre_gelu[:, cols].astype(jnp.float32)
        upstream = out_grad[:, cols].astype(jnp.float32)
        cdf = 0.5 * (1.0 + lax.erf(values * root_half))
        gelu_out = values * cdf
        gelu[:, cols] = gelu_out
        slope[:, cols] = cdf + values * jnp.exp(-0.5 * values * values) * inv_root_two_pi
        sums[0:1, cols] = jnp.sum(gelu_out * gelu_out, axis=0, keepdims=True)
        sums[1:2, cols] = jnp.sum(upstream * gelu_out, axis=0, keepdims=True)
        shift[0:1, cols] = jnp.sum(upstream, axis=0, keepdims=True)


def gradient(sums, other, shift, gain, out_grad, gelu, slope, pre_grad, *rest):
    chunks, (turned, gains, shifts) = rest[:8], rest[8:]
    squares = sums[0:1, :] + other[0:1, :]
    response = sums[1:2, :] + other[1:2, :]
    channel_norm = jnp.sqrt(squares + 1e-06)
    norm_mean = jnp.sum(channel_norm, axis=1, keepdims=True) * (1.0 / H) + 1e-06
    scaled = channel_norm / norm_mean
    scaled_grad = gain[...] * response
    norm_grad = scaled_grad / norm_mean - jnp.sum(scaled_grad * channel_norm, axis=1, keepdims=True) / (
        H * norm_mean * norm_mean
    )
    of_upstream = gain[...] * scaled + 1.0
    of_gelu = norm_grad / channel_norm
    gain_term = sums[1:2, :] * scaled
    shift_term = shift[...]
    for k in range(H // LANES):
        cols = slice(k * LANES, (k + 1) * LANES)
        upstream = out_grad[:, cols].astype(jnp.float32)
        act_grad = upstream * of_upstream[:, cols] + gelu[:, cols] * of_gelu[:, cols]
        rounded = (act_grad * slope[:, cols]).astype(jnp.bfloat16)
        pre_grad[:, cols] = rounded
        turned[cols, :] = rounded.astype(jnp.float32).T
    both = jnp.concatenate([gain_term, shift_term, jnp.zeros((6, H), jnp.float32)], axis=0)
    for b in range(H // BLOCK):
        tile, start = divmod(b * BLOCK, LANES)
        window = both[:, tile * LANES : min((tile + 2) * LANES, H)]
        if start:
            window = pltpu.roll(window, window.shape[1] - start, 1)
        gains[b : b + 1, :] = window[0:1, :LANES]
        shifts[b : b + 1, :] = window[1:2, :LANES]
    core, x = lax.axis_index("core"), lax.axis_index("x")
    y = 2 * lax.axis_index("yh") + lax.axis_index("yl")
    for of_other in range(2):
        to = core if of_other == 0 else 1 - core
        mine, beside_mine = jnp.where(to == 0, x, y), jnp.where(to == 0, y, x)
        for j in range(4):
            chunk = chunks[of_other * 4 + j]
            d = lax.rem(mine + j, 4)
            for i in range(4):
                e = lax.rem(beside_mine + i, 4)
                block_x, block_y = jnp.where(to == 0, d, e), jnp.where(to == 0, e, d)
                b = (block_y // 2) * 16 + to * 8 + block_x * 2 + lax.rem(block_y, 2)
                start = pl.multiple_of(b * BLOCK, 8)
                chunk[i * BLOCK : (i + 1) * BLOCK, :] = turned[pl.ds(start, BLOCK), :]
                chunk[4 * BLOCK + i : 4 * BLOCK + i + 1, :] = gains[pl.ds(b, 1), :]
                chunk[4 * BLOCK + 4 + i : 4 * BLOCK + 5 + i, :] = shifts[pl.ds(b, 1), :]


def product(*refs):
    parts, right, outs, left = refs[:8], refs[8], refs[9:13], refs[13]
    for s, part in enumerate(parts):
        left[:, s * ROWS : (s + 1) * ROWS] = part[: 4 * BLOCK, :].astype(jnp.bfloat16)
    small = parts[0][4 * BLOCK :, :]
    for part in parts[1:]:
        small = small + part[4 * BLOCK :, :]
    small = small.T
    lane = lax.broadcasted_iota(jnp.int32, (BLOCK, LANES), 1)
    for k in range(3):
        cols = slice(2 * k * LANES, 2 * (k + 1) * LANES)
        total = jnp.dot(left[...], right[:, cols], preferred_element_type=jnp.float32)
        for i, out in enumerate(outs):
            rows = total[i * BLOCK : (i + 1) * BLOCK, :]
            if k < 2:
                out[:, cols] = rows
            else:
                out[:, 4 * LANES : 5 * LANES] = rows[:, :LANES]
                last = rows[:, LANES:]
                last = jnp.where(lane == 65, small[:BLOCK, i : i + 1], last)
                last = jnp.where(lane == 66, small[:BLOCK, 4 + i : 5 + i], last)
                out[:, 5 * LANES :] = last


PACKED = 72


def gather_rows(a, b, c, d, out):
    for k in range(6):
        cols = slice(k * LANES, (k + 1) * LANES)
        total = (a[:, cols] + b[:, cols]) + (c[:, cols] + d[:, cols])
        for z in range(8):
            out[z, k * OWN : (k + 1) * OWN, :] = total[z * OWN : (z + 1) * OWN, :]
    out[:, 6 * OWN :, :] = jnp.zeros((8, PACKED - 6 * OWN, LANES), jnp.float32)


def finish(parts, weight, gain, shift, bias):
    total = parts[0]
    for z in range(1, 8):
        total = total + parts[z]
    for k in range(6):
        rows = total[k * OWN : (k + 1) * OWN, :]
        if k < 5:
            weight[:, k * LANES : (k + 1) * LANES] = rows
        else:
            weight[:, 5 * LANES :] = rows[:, :64]
            turned = jnp.concatenate([rows, jnp.zeros((5, LANES), jnp.float32)], axis=0).T
            bias[...] = turned[64:65, :OWN]
            gain[...] = turned[65:66, :OWN]
            shift[...] = turned[66:67, :OWN]


def on_device(normed, pre_gelu, out_grad, grn_gain):
    wide = call(widen, f32(C, LANES), moved=540_000)(normed)
    sums, shift, gelu, slope = call(
        statistics,
        [f32(2, H), f32(1, H), f32(ROWS, H), f32(ROWS, H)],
        flops=60 * ROWS * H,
        moved=4_400_000,
    )(pre_gelu, out_grad)
    other = send(sums, other_half)

    near = send(wide, other_core)
    from_below = send(wide, along(1))
    from_above = send(wide, along(-1))
    below_across = send(wide, across(1))
    above_across = send(wide, across(-1))
    far = send(from_below, along(1))
    far_across = send(above_across, along(-1))
    right = call(narrow, jax.ShapeDtypeStruct((8 * ROWS, 6 * LANES), jnp.bfloat16), moved=4_400_000)(
        wide, near, from_below, below_across, from_above, above_across, far, far_across
    )

    pre_grad, *chunks = call(
        gradient,
        [jax.ShapeDtypeStruct((ROWS, H), jnp.bfloat16)] + [f32(4 * BLOCK + 8, LANES)] * 8,
        scratch=[
            pltpu.VMEM((H, LANES), jnp.float32),
            pltpu.VMEM((H // BLOCK, LANES), jnp.float32),
            pltpu.VMEM((H // BLOCK, LANES), jnp.float32),
        ],
        flops=30 * ROWS * H,
        moved=6_000_000,
    )(sums, other, shift, grn_gain.reshape(1, H), out_grad, gelu, slope)
    keep, cross = chunks[:4], chunks[4:]
    parts = [
        keep[0],
        send(cross[0], other_core),
        send(keep[1], along(1)),
        send(cross[1], across(1)),
        send(keep[3], along(-1)),
        send(cross[3], across(-1)),
        send(keep[2], along(2)),
        send(cross[2], across(2)),
    ]
    own, *away = call(
        product,
        [f32(BLOCK, 6 * LANES)] * 4,
        scratch=[pltpu.VMEM((4 * BLOCK, 8 * ROWS), jnp.bfloat16)],
        flops=2 * 352 * 1024 * 768,
        moved=4_000_000,
    )(*parts, right)
    stage = [send(away[0], beside(1)), send(away[2], beside(-1)), send(away[1], beside(2))]
    rows = call(gather_rows, f32(8, PACKED, LANES), moved=1_400_000)(own, *stage)
    rows = lax.all_to_all(rows, "z", 0, 0, tiled=True)
    weight, gain, shift, bias = call(
        finish, [f32(OWN, C), f32(1, OWN), f32(1, OWN), f32(1, OWN)], moved=330_000
    )(rows)
    return pre_grad, weight, gain.reshape(OWN), shift.reshape(OWN), bias.reshape(OWN)


def solution(mesh):
    split = Mesh(mesh.devices.reshape(SIZES), AXES)
    return jax.shard_map(
        on_device,
        mesh=split,
        in_specs=(P(AXES, None), P(AXES, None), P(AXES, None), P()),
        out_specs=(P(AXES, None), P(AXES, None), P(AXES), P(AXES), P(AXES)),
        check_vma=False,
    )
```

time: 313 us -> 73.2 us (0.23)
  waiting for transfers between devices: 204 us -> 28.5 us
  blocking collectives: 78.9 us -> 19 us
  between operations: 15.4 us -> 0.7 us
  starting transfers between devices: 2.15 us -> 16.6 us
  matrix products: 4.63 us -> 0 us
  other arithmetic: 4.62 us -> 0 us
  Pallas kernels: 0 us -> 4.5 us
    unnamed x2 -> x0, waiting for transfers between devices: 200 us -> none
    unnamed x1 -> x0, blocking collectives: 78.9 us -> none
    ppermute x2 -> x18, waiting for transfers between devices: 3.59 us -> 28.5 us  [send(): return lax.ppermute(value, AXES, pairs(target))]
    all_to_all x0 -> x1, blocking collectives: none -> 19 us  [on_device(): rows = lax.all_to_all(rows, 'z', 0, 0, tiled=True)]
    ppermute x2 -> x18, starting transfers between devices: 2.11 us -> 16.6 us  [send(): return lax.ppermute(value, AXES, pairs(target))]
    dot_general x1 -> x0, matrix products: 4.63 us -> none  [on_device(): lax.dot_general(pre_grad, normed, (((0,), (0,)), ((), ())), preferred_ele...]
    reduce_sum x3 -> x0, other arithmetic: 4.61 us -> none  [the longest x1 2.13 us: on_device(): own_response = jnp.sum(upstream * gelu_out, axis=0)]
    pallas_call x0 -> x7, Pallas kernels: none -> 4.5 us  [the longest x1 1.74 us: on_device(): call(gradient, [jax.ShapeDtypeStruct((ROWS, H), jnp.bfloat16)] + [f32(4 *...]
  transfers between devices with their start and end apart: 3 -> 18, of which waited for: 3 -> 11; matrix products, arithmetic and copies ran while one was open for 1% -> 0% of each run, Pallas kernels for 0% -> 4%
where the time goes in v1:
time: 73.2 us; the launch traced here: 72.7 us
  waiting for transfers between devices  28.5 us (39%)
  blocking collectives  19 us (26%)
  starting transfers between devices  16.6 us (23%)
  Pallas kernels  4.5 us (6%)
  local copies, waits for them, and re-layouts  3.37 us (5%)
    ppermute x18, waiting for transfers between devices, send(): return lax.ppermute(value, AXES, pairs(target))  28.5 us
    all_to_all x1, blocking collectives, on_device(): rows = lax.all_to_all(rows, 'z', 0, 0, tiled=True)  19 us
    ppermute x18, starting transfers between devices, send(): return lax.ppermute(value, AXES, pairs(target))  16.6 us
    unnamed x9, local copies, waits for them, and re-layouts  3.36 us
    pallas_call x1, Pallas kernels, on_device(): call(gradient, [jax.ShapeDtypeStruct((ROWS, H), jnp.bfloat16)] + [f32(4 *...  1.74 us
  transfers between devices with their start and end apart: 18, of which 11 were waited for; matrix products, arithmetic and copies ran while one was open for 0% of the time, Pallas kernels for 4%

profile of v1, /device:TPU:8, one launch (start us, length us, event | category | flops | bytes accessed | tf_op | source)
XLA Modules:
  0.0 72.7 jit_solution(15513868121159674749)
XLA Ops:
  0.7 1.1 %copy.9.normed = bf16[128,704]{1,0:T(8,128)(2,1)S(1)} copy(bf16[128,704]{0,1:T(8,128)(2,1)} %param.4) | data formatting | bytes 360448 | tf_op args[0]
  1.9 1.5 %collective-permute-start.9 = (f32[704,128]{1,0:T(8,128)S(1)}, f32[704,128]{1,0:T(8,128)S(1)}, u32[]{:S(2)}, u32[]{:S(2)}) collective-permute-start(f32[704,128]{1,0:T(8,128)S(1)} %shard_map.85.refs_0_), channel_id=1, source_target_pairs={{0,16},{1,17},{2,18},{3,19},{4,20},{5,21},{6,22},{7,23},{8,24},{9,... | collective-permute-start | bytes 1081352 | tf_op jit(solution)/shard_map/ppermute | solution.py:34
  3.4 1.1 %copy-done = bf16[128,2816]{1,0:T(8,128)(2,1)S(1)} copy-done((bf16[128,2816]{1,0:T(8,128)(2,1)S(1)}, bf16[128,2816]{1,0:T(8,128)(2,1)}, u32[]{:S(2)}) %copy-start) | copy-done | bytes 720920
  4.5 1.1 %copy-done.2 = bf16[128,2816]{1,0:T(8,128)(2,1)S(1)} copy-done((bf16[128,2816]{1,0:T(8,128)(2,1)S(1)}, bf16[128,2816]{1,0:T(8,128)(2,1)}, u32[]{:S(2)}) %copy-start.2) | copy-done | bytes 720920
  5.6 0.9 %shard_map.83 = (f32[2,2816]{1,0:T(2,128)S(1)}, f32[1,2816]{1,0:T(1,128)S(1)}, f32[128,2816]{1,0:T(8,128)S(1)}, f32[128,2816]{1,0:T(8,128)S(1)}) custom-call(bf16[128,2816]{1,0:T(8,128)(2,1)S(1)} %copy-done.2, bf16[128,2816]{1,0:T(8,128)(2,1)S(1)} %copy-done), custom_call_target="tpu_custom_call" | custom-call | flops 21626880 | bytes 4400000 | tf_op jit(solution)/shard_map/pallas_call | solution.py:207
  6.6 2.0 %collective-permute-start = (f32[2,2816]{1,0:T(2,128)S(1)}, f32[2,2816]{1,0:T(2,128)S(1)}, u32[]{:S(2)}, u32[]{:S(2)}) collective-permute-start(f32[2,2816]{1,0:T(2,128)S(1)} %get-tuple-element.26.sums), channel_id=1, source_target_pairs={{0,1},{1,0},{2,3},{3,2},{4,5},{5,4},{6,7},{7,6},{8,9},{9,8},{10,11... | collective-permute-start | bytes 67592 | tf_op jit(solution)/shard_map/ppermute | solution.py:34
  8.6 1.9 %collective-permute-done.other = f32[2,2816]{1,0:T(2,128)S(1)} collective-permute-done((f32[2,2816]{1,0:T(2,128)S(1)}, f32[2,2816]{1,0:T(2,128)S(1)}, u32[]{:S(2)}, u32[]{:S(2)}) %collective-permute-start) | collective-permute-done | bytes 22560 | tf_op jit(solution)/shard_map/ppermute | solution.py:34
  10.4 1.7 %shard_map.84 = (bf16[128,2816]{1,0:T(8,128)(2,1)}, f32[360,128]{1,0:T(8,128)S(1)}, f32[360,128]{1,0:T(8,128)S(1)}, f32[360,128]{1,0:T(8,128)S(1)}, f32[360,128]...) custom-call(f32[2,2816]{1,0:T(2,128)S(1)} %get-tuple-element.26.sums, ...), custom_call_target="tpu_custom_call" | custom-call | flops 10813440 | bytes 6000000 | tf_op jit(solution)/shard_map/pallas_call | solution.py:226
  14.4 1.3 %collective-permute-start.10 = (f32[704,128]{1,0:T(8,128)S(1)}, f32[704,128]{1,0:T(8,128)S(1)}, u32[]{:S(2)}, u32[]{:S(2)}) collective-permute-start(f32[704,128]{1,0:T(8,128)S(1)} %shard_map.85.refs_0_), channel_id=1, source_target_pairs={{0,72},{1,73},{2,74},{3,75},{4,76},{5,77},{6,78},{7,79},{8,192},{9... | collective-permute-start | bytes 1081352 | tf_op jit(solution)/shard_map/ppermute | solution.py:34
  15.7 5.4 %collective-permute-done.2.refs_2_ = f32[360,128]{1,0:T(8,128)S(1)} collective-permute-done((f32[360,128]{1,0:T(8,128)S(1)}, f32[360,128]{1,0:T(8,128)S(1)}, u32[]{:S(2)}, u32[]{:S(2)}) %collective-permute-start.2) | collective-permute-done | bytes 184352 | tf_op jit(solution)/shard_map/ppermute | solution.py:34
  21.6 1.6 %collective-permute-start.13 = (f32[704,128]{1,0:T(8,128)S(1)}, f32[704,128]{1,0:T(8,128)S(1)}, u32[]{:S(2)}, u32[]{:S(2)}) collective-permute-start(f32[704,128]{1,0:T(8,128)S(1)} %collective-permute-done.9.refs_2_), channel_id=1, source_target_pairs={{0,16},{1,17},{2,18},{3,19},{4,20},{5,21},{6,22},{7,23},{8,24},{9,... | collective-permute-start | bytes 1081352 | tf_op jit(solution)/shard_map/ppermute | solution.py:34
  23.1 1.7 %collective-permute-start.14 = (f32[704,128]{1,0:T(8,128)S(1)}, f32[704,128]{1,0:T(8,128)S(1)}, u32[]{:S(2)}, u32[]{:S(2)}) collective-permute-start(f32[704,128]{1,0:T(8,128)S(1)} %collective-permute-done.12.refs_5_), channel_id=1, source_target_pairs={{0,48},{1,49},{2,50},{3,51},{4,52},{5,53},{6,54},{7,55},{8,56},{9,... | collective-permute-start | bytes 1081352 | tf_op jit(solution)/shard_map/ppermute | solution.py:34
  25.0 3.5 %collective-permute-done.11.refs_4_ = f32[704,128]{1,0:T(8,128)S(1)} collective-permute-done((f32[704,128]{1,0:T(8,128)S(1)}, f32[704,128]{1,0:T(8,128)S(1)}, u32[]{:S(2)}, u32[]{:S(2)}) %collective-permute-start.11) | collective-permute-done | bytes 360480 | tf_op jit(solution)/shard_map/ppermute | solution.py:34
  28.5 2.8 %collective-permute-done.13.refs_6_ = f32[704,128]{1,0:T(8,128)S(1)} collective-permute-done((f32[704,128]{1,0:T(8,128)S(1)}, f32[704,128]{1,0:T(8,128)S(1)}, u32[]{:S(2)}, u32[]{:S(2)}) %collective-permute-start.13) | collective-permute-done | bytes 360480 | tf_op jit(solution)/shard_map/ppermute | solution.py:34
  31.3 1.3 %collective-permute-start.6 = (f32[360,128]{1,0:T(8,128)S(1)}, f32[360,128]{1,0:T(8,128)S(1)}, u32[]{:S(2)}, u32[]{:S(2)}) collective-permute-start(f32[360,128]{1,0:T(8,128)S(1)} %get-tuple-element.37), channel_id=1, source_target_pairs={{0,32},{1,33},{2,34},{3,35},{4,36},{5,37},{6,38},{7,39},{8,40},{9,... | collective-permute-start | bytes 552968 | tf_op jit(solution)/shard_map/ppermute | solution.py:34
  33.5 2.9 %collective-permute-done.4.refs_4_ = f32[360,128]{1,0:T(8,128)S(1)} collective-permute-done((f32[360,128]{1,0:T(8,128)S(1)}, f32[360,128]{1,0:T(8,128)S(1)}, u32[]{:S(2)}, u32[]{:S(2)}) %collective-permute-start.4) | collective-permute-done | bytes 184352 | tf_op jit(solution)/shard_map/ppermute | solution.py:34
  36.3 2.6 %collective-permute-done.6.refs_6_ = f32[360,128]{1,0:T(8,128)S(1)} collective-permute-done((f32[360,128]{1,0:T(8,128)S(1)}, f32[360,128]{1,0:T(8,128)S(1)}, u32[]{:S(2)}, u32[]{:S(2)}) %collective-permute-start.6) | collective-permute-done | bytes 184352 | tf_op jit(solution)/shard_map/ppermute | solution.py:34
  39.0 1.3 %collective-permute-done.7.refs_7_ = f32[360,128]{1,0:T(8,128)S(1)} collective-permute-done((f32[360,128]{1,0:T(8,128)S(1)}, f32[360,128]{1,0:T(8,128)S(1)}, u32[]{:S(2)}, u32[]{:S(2)}) %collective-permute-start.7) | collective-permute-done | bytes 184352 | tf_op jit(solution)/shard_map/ppermute | solution.py:34
  41.1 1.9 %collective-permute-start.15 = (f32[88,768]{1,0:T(8,128)S(1)}, f32[88,768]{1,0:T(8,128)S(1)}, u32[]{:S(2)}, u32[]{:S(2)}) collective-permute-start(f32[88,768]{1,0:T(8,128)S(1)} %get-tuple-element.40), channel_id=1, source_target_pairs={{0,8},{1,9},{2,10},{3,11},{4,12},{5,13},{6,14},{7,15},{8,128},{9,1... | collective-permute-start | bytes 811016 | tf_op jit(solution)/shard_map/ppermute | solution.py:34
  43.2 2.4 %collective-permute-start.17 = (f32[88,768]{1,0:T(8,128)S(1)}, f32[88,768]{1,0:T(8,128)S(1)}, u32[]{:S(2)}, u32[]{:S(2)}) collective-permute-start(f32[88,768]{1,0:T(8,128)S(1)} %get-tuple-element.42), channel_id=1, source_target_pairs={{0,128},{1,129},{2,130},{3,131},{4,132},{5,133},{6,134},{7,135},{8... | collective-permute-start | bytes 811016 | tf_op jit(solution)/shard_map/ppermute | solution.py:34
  45.6 2.1 %collective-permute-done.15.b = f32[88,768]{1,0:T(8,128)S(1)} collective-permute-done((f32[88,768]{1,0:T(8,128)S(1)}, f32[88,768]{1,0:T(8,128)S(1)}, u32[]{:S(2)}, u32[]{:S(2)}) %collective-permute-start.15) | collective-permute-done | bytes 270368 | tf_op jit(solution)/shard_map/ppermute | solution.py:34
  47.7 1.8 %collective-permute-done.16.c = f32[88,768]{1,0:T(8,128)S(1)} collective-permute-done((f32[88,768]{1,0:T(8,128)S(1)}, f32[88,768]{1,0:T(8,128)S(1)}, u32[]{:S(2)}, u32[]{:S(2)}) %collective-permute-start.16) | collective-permute-done | bytes 270368 | tf_op jit(solution)/shard_map/ppermute | solution.py:34
  49.5 3.5 %collective-permute-done.17.d = f32[88,768]{1,0:T(8,128)S(1)} collective-permute-done((f32[88,768]{1,0:T(8,128)S(1)}, f32[88,768]{1,0:T(8,128)S(1)}, u32[]{:S(2)}, u32[]{:S(2)}) %collective-permute-start.17) | collective-permute-done | bytes 270368 | tf_op jit(solution)/shard_map/ppermute | solution.py:34
  53.0 19.0 %all_to_all.5.parts = f32[8,72,128]{2,1,0:T(8,128)S(1)} all-to-all(f32[8,72,128]{2,1,0:T(8,128)S(1)} %shard_map.88), channel_id=1, replica_groups=mesh['yh'=2,'core'=2,'x'=4,'yl'=2,'z'=8] {'z'}, dimensions={0} | all-to-all | bytes 589824 | tf_op jit(solution)/shard_map/all_to_all | solution.py:257
  (30 shorter events, 5.5 us)
Async XLA Ops:
  0.6 9.8 %copy-start.1 = (bf16[128,2816]{1,0:T(8,128)(2,1)S(1)}, bf16[128,2816]{1,0:T(8,128)(2,1)}, u32[]{:S(2)}) copy-start(bf16[128,2816]{1,0:T(8,128)(2,1)} %out_grad.3) | copy-start | bytes 2162692
  0.6 7.9 %copy-start.3 = (f32[2816]{0:T(1024)S(1)}, f32[2816]{0:T(1024)}, u32[]{:S(2)}) copy-start(f32[2816]{0:T(1024)} %param.7) | copy-start | bytes 33796
  1.9 19.7 %collective-permute-start.9 = (f32[704,128]{1,0:T(8,128)S(1)}, f32[704,128]{1,0:T(8,128)S(1)}, u32[]{:S(2)}, u32[]{:S(2)}) collective-permute-start(f32[704,128]{1,0:T(8,128)S(1)} %shard_map.85.refs_0_), channel_id=1, source_target_pairs={{0,16},{1,17},{2,18},{3,19},{4,20},{5,21},{6,22},{7,23},{8,24},{9,... | collective-permute-start | bytes 1081352 | tf_op jit(solution)/shard_map/ppermute | solution.py:34
  3.4 19.7 %collective-permute-start.12 = (f32[704,128]{1,0:T(8,128)S(1)}, f32[704,128]{1,0:T(8,128)S(1)}, u32[]{:S(2)}, u32[]{:S(2)}) collective-permute-start(f32[704,128]{1,0:T(8,128)S(1)} %shard_map.85.refs_0_), channel_id=1, source_target_pairs={{0,200},{1,201},{2,202},{3,203},{4,204},{5,205},{6,206},{7,207},{8... | collective-permute-start | bytes 1081352 | tf_op jit(solution)/shard_map/ppermute | solution.py:34
  3.4 1.1 %copy-start = (bf16[128,2816]{1,0:T(8,128)(2,1)S(1)}, bf16[128,2816]{1,0:T(8,128)(2,1)}, u32[]{:S(2)}) copy-start(bf16[128,2816]{1,0:T(8,128)(2,1)} %out_grad.3) | copy-start | bytes 2162692
  4.5 1.1 %copy-start.2 = (bf16[128,2816]{1,0:T(8,128)(2,1)S(1)}, bf16[128,2816]{1,0:T(8,128)(2,1)}, u32[]{:S(2)}) copy-start(bf16[128,2816]{1,0:T(8,128)(2,1)} %pre_gelu.1) | copy-start | bytes 2162692
  6.6 3.9 %collective-permute-start = (f32[2,2816]{1,0:T(2,128)S(1)}, f32[2,2816]{1,0:T(2,128)S(1)}, u32[]{:S(2)}, u32[]{:S(2)}) collective-permute-start(f32[2,2816]{1,0:T(2,128)S(1)} %get-tuple-element.26.sums), channel_id=1, source_target_pairs={{0,1},{1,0},{2,3},{3,2},{4,5},{5,4},{6,7},{7,6},{8,9},{9,8},{10,11... | collective-permute-start | bytes 67592 | tf_op jit(solution)/shard_map/ppermute | solution.py:34
  12.2 2.2 %collective-permute-start.1 = (f32[360,128]{1,0:T(8,128)S(1)}, f32[360,128]{1,0:T(8,128)S(1)}, u32[]{:S(2)}, u32[]{:S(2)}) collective-permute-start(f32[360,128]{1,0:T(8,128)S(1)} %get-tuple-element.32), channel_id=1, source_target_pairs={{0,64},{1,65},{2,66},{3,67},{4,68},{5,69},{6,70},{7,71},{8,72},{9,... | collective-permute-start | bytes 552968 | tf_op jit(solution)/shard_map/ppermute | solution.py:34
  13.1 8.0 %collective-permute-start.2 = (f32[360,128]{1,0:T(8,128)S(1)}, f32[360,128]{1,0:T(8,128)S(1)}, u32[]{:S(2)}, u32[]{:S(2)}) collective-permute-start(f32[360,128]{1,0:T(8,128)S(1)} %get-tuple-element.33), channel_id=1, source_target_pairs={{0,16},{1,17},{2,18},{3,19},{4,20},{5,21},{6,22},{7,23},{8,24},{9,... | collective-permute-start | bytes 552968 | tf_op jit(solution)/shard_map/ppermute | solution.py:34
  13.8 11.0 %collective-permute-start.8 = (f32[704,128]{1,0:T(8,128)S(1)}, f32[704,128]{1,0:T(8,128)S(1)}, u32[]{:S(2)}, u32[]{:S(2)}) collective-permute-start(f32[704,128]{1,0:T(8,128)S(1)} %shard_map.85.refs_0_), channel_id=1, source_target_pairs={{0,64},{1,65},{2,66},{3,67},{4,68},{5,69},{6,70},{7,71},{8,72},{9,... | collective-permute-start | bytes 1081352 | tf_op jit(solution)/shard_map/ppermute | solution.py:34
  14.4 10.4 %collective-permute-start.10 = (f32[704,128]{1,0:T(8,128)S(1)}, f32[704,128]{1,0:T(8,128)S(1)}, u32[]{:S(2)}, u32[]{:S(2)}) collective-permute-start(f32[704,128]{1,0:T(8,128)S(1)} %shard_map.85.refs_0_), channel_id=1, source_target_pairs={{0,72},{1,73},{2,74},{3,75},{4,76},{5,77},{6,78},{7,79},{8,192},{9... | collective-permute-start | bytes 1081352 | tf_op jit(solution)/shard_map/ppermute | solution.py:34
  21.1 7.4 %collective-permute-start.11 = (f32[704,128]{1,0:T(8,128)S(1)}, f32[704,128]{1,0:T(8,128)S(1)}, u32[]{:S(2)}, u32[]{:S(2)}) collective-permute-start(f32[704,128]{1,0:T(8,128)S(1)} %shard_map.85.refs_0_), channel_id=1, source_target_pairs={{0,48},{1,49},{2,50},{3,51},{4,52},{5,53},{6,54},{7,55},{8,56},{9,... | collective-permute-start | bytes 1081352 | tf_op jit(solution)/shard_map/ppermute | solution.py:34
  21.6 9.8 %collective-permute-start.13 = (f32[704,128]{1,0:T(8,128)S(1)}, f32[704,128]{1,0:T(8,128)S(1)}, u32[]{:S(2)}, u32[]{:S(2)}) collective-permute-start(f32[704,128]{1,0:T(8,128)S(1)} %collective-permute-done.9.refs_2_), channel_id=1, source_target_pairs={{0,16},{1,17},{2,18},{3,19},{4,20},{5,21},{6,22},{7,23},{8,24},{9,... | collective-permute-start | bytes 1081352 | tf_op jit(solution)/shard_map/ppermute | solution.py:34
  23.1 10.1 %collective-permute-start.14 = (f32[704,128]{1,0:T(8,128)S(1)}, f32[704,128]{1,0:T(8,128)S(1)}, u32[]{:S(2)}, u32[]{:S(2)}) collective-permute-start(f32[704,128]{1,0:T(8,128)S(1)} %collective-permute-done.12.refs_5_), channel_id=1, source_target_pairs={{0,48},{1,49},{2,50},{3,51},{4,52},{5,53},{6,54},{7,55},{8,56},{9,... | collective-permute-start | bytes 1081352 | tf_op jit(solution)/shard_map/ppermute | solution.py:34
  24.8 8.7 %collective-permute-start.3 = (f32[360,128]{1,0:T(8,128)S(1)}, f32[360,128]{1,0:T(8,128)S(1)}, u32[]{:S(2)}, u32[]{:S(2)}) collective-permute-start(f32[360,128]{1,0:T(8,128)S(1)} %get-tuple-element.34), channel_id=1, source_target_pairs={{0,72},{1,73},{2,74},{3,75},{4,76},{5,77},{6,78},{7,79},{8,192},{9... | collective-permute-start | bytes 552968 | tf_op jit(solution)/shard_map/ppermute | solution.py:34
  24.8 11.5 %collective-permute-start.4 = (f32[360,128]{1,0:T(8,128)S(1)}, f32[360,128]{1,0:T(8,128)S(1)}, u32[]{:S(2)}, u32[]{:S(2)}) collective-permute-start(f32[360,128]{1,0:T(8,128)S(1)} %get-tuple-element.35), channel_id=1, source_target_pairs={{0,48},{1,49},{2,50},{3,51},{4,52},{5,53},{6,54},{7,55},{8,56},{9,... | collective-permute-start | bytes 552968 | tf_op jit(solution)/shard_map/ppermute | solution.py:34
  28.5 7.8 %collective-permute-start.5 = (f32[360,128]{1,0:T(8,128)S(1)}, f32[360,128]{1,0:T(8,128)S(1)}, u32[]{:S(2)}, u32[]{:S(2)}) collective-permute-start(f32[360,128]{1,0:T(8,128)S(1)} %get-tuple-element.36), channel_id=1, source_target_pairs={{0,200},{1,201},{2,202},{3,203},{4,204},{5,205},{6,206},{7,207},{8... | collective-permute-start | bytes 552968 | tf_op jit(solution)/shard_map/ppermute | solution.py:34
  31.3 7.7 %collective-permute-start.6 = (f32[360,128]{1,0:T(8,128)S(1)}, f32[360,128]{1,0:T(8,128)S(1)}, u32[]{:S(2)}, u32[]{:S(2)}) collective-permute-start(f32[360,128]{1,0:T(8,128)S(1)} %get-tuple-element.37), channel_id=1, source_target_pairs={{0,32},{1,33},{2,34},{3,35},{4,36},{5,37},{6,38},{7,39},{8,40},{9,... | collective-permute-start | bytes 552968 | tf_op jit(solution)/shard_map/ppermute | solution.py:34
  33.2 7.1 %collective-permute-start.7 = (f32[360,128]{1,0:T(8,128)S(1)}, f32[360,128]{1,0:T(8,128)S(1)}, u32[]{:S(2)}, u32[]{:S(2)}) collective-permute-start(f32[360,128]{1,0:T(8,128)S(1)} %get-tuple-element.38), channel_id=1, source_target_pairs={{0,192},{1,193},{2,194},{3,195},{4,196},{5,197},{6,198},{7,199},{8... | collective-permute-start | bytes 552968 | tf_op jit(solution)/shard_map/ppermute | solution.py:34
  41.1 6.5 %collective-permute-start.15 = (f32[88,768]{1,0:T(8,128)S(1)}, f32[88,768]{1,0:T(8,128)S(1)}, u32[]{:S(2)}, u32[]{:S(2)}) collective-permute-start(f32[88,768]{1,0:T(8,128)S(1)} %get-tuple-element.40), channel_id=1, source_target_pairs={{0,8},{1,9},{2,10},{3,11},{4,12},{5,13},{6,14},{7,15},{8,128},{9,1... | collective-permute-start | bytes 811016 | tf_op jit(solution)/shard_map/ppermute | solution.py:34
  43.0 6.5 %collective-permute-start.16 = (f32[88,768]{1,0:T(8,128)S(1)}, f32[88,768]{1,0:T(8,128)S(1)}, u32[]{:S(2)}, u32[]{:S(2)}) collective-permute-start(f32[88,768]{1,0:T(8,128)S(1)} %get-tuple-element.41), channel_id=1, source_target_pairs={{0,136},{1,137},{2,138},{3,139},{4,140},{5,141},{6,142},{7,143},{8... | collective-permute-start | bytes 811016 | tf_op jit(solution)/shard_map/ppermute | solution.py:34
  43.2 9.7 %collective-permute-start.17 = (f32[88,768]{1,0:T(8,128)S(1)}, f32[88,768]{1,0:T(8,128)S(1)}, u32[]{:S(2)}, u32[]{:S(2)}) collective-permute-start(f32[88,768]{1,0:T(8,128)S(1)} %get-tuple-element.42), channel_id=1, source_target_pairs={{0,128},{1,129},{2,130},{3,131},{4,132},{5,133},{6,134},{7,135},{8... | collective-permute-start | bytes 811016 | tf_op jit(solution)/shard_map/ppermute | solution.py:34

commit v2 on v1

v2 whole, which is shorter than its diff:
```python
import jax
import jax.numpy as jnp
import numpy as np
from jax import lax
from jax.experimental import pallas as pl
from jax.experimental.pallas import tpu as pltpu
from jax.sharding import Mesh, PartitionSpec as P

root_half = 0.7071067811865476
inv_root_two_pi = 0.3989422804014327

AXES = ("yh", "core", "x", "yl", "z")
SIZES = (2, 2, 4, 2, 8)
ROWS = 128
C = 704
H = 2816
BLOCK = 88
OWN = 11
PART = 4 * BLOCK + 8
LANES = 128
MIB = 1 << 20
GUIDE = 20_000_000_000


def pairs(target):
    found = []
    for i in range(256):
        yh, core, x, yl, z = (int(v) for v in np.unravel_index(i, SIZES))
        core2, x2, y2, z2 = target(core, x, 2 * yh + yl, z)
        place = (y2 // 2 % 2, core2 % 2, x2 % 4, y2 % 2, z2 % 8)
        found.append((i, int(np.ravel_multi_index(place, SIZES))))
    return found


def send(value, target):
    return lax.ppermute(value, AXES, pairs(target))


def other_core(core, x, y, z):
    return 1 - core, x, y, z


def other_half(core, x, y, z):
    return core, x, y, z ^ 1


def along(k):
    return lambda core, x, y, z: (core, x + k, y, z) if core == 0 else (core, x, y + k, z)


def across(k):
    return lambda core, x, y, z: (1, x, y + k, z) if core == 0 else (0, x + k, y, z)


def beside(k):
    return lambda core, x, y, z: (core, x, y + k, z) if core == 0 else (core, x + k, y, z)


def call(body, out_shape, scratch=(), flops=0, moved=0, limit=24, **specs):
    return pl.pallas_call(
        body,
        out_shape=out_shape,
        **specs,
        scratch_shapes=scratch,
        compiler_params=pltpu.CompilerParams(vmem_limit_bytes=limit * MIB),
        cost_estimate=pl.CostEstimate(flops=flops, bytes_accessed=moved, transcendentals=0),
    )


def f32(*shape):
    return jax.ShapeDtypeStruct(shape, jnp.float32)


def narrow(*refs):
    *wides, out = refs
    for s, wide in enumerate(wides):
        top = wide.shape[0] - C
        out[:, s * ROWS : (s + 1) * ROWS] = wide[top:, :].astype(jnp.bfloat16)


CUTS = (0, 6, 12, 17, 22)


def statistics(
    normed_hbm, pre_gelu_hbm, out_grad_hbm, wide, sums, shift, gelu, slope, out_grad, pre_gelu, normed, sems, normed_sem
):
    copies = []
    for p, (start, stop) in enumerate(zip(CUTS[:-1], CUTS[1:])):
        cols = pl.ds(start * LANES, (stop - start) * LANES)
        for n, (source, target) in enumerate(((pre_gelu_hbm, pre_gelu), (out_grad_hbm, out_grad))):
            copies.append(pltpu.make_async_copy(source.at[:, cols], target.at[:, cols], sems.at[n, p]))
            copies[-1].start()
    last = pltpu.make_async_copy(normed_hbm, normed, normed_sem)
    last.start()
    for p, (start, stop) in enumerate(zip(CUTS[:-1], CUTS[1:])):
        copies[2 * p].wait()
        copies[2 * p + 1].wait()
        for k in range(start, stop):
            cols = slice(k * LANES, (k + 1) * LANES)
            values = pre_gelu[:, cols].astype(jnp.float32)
            upstream = out_grad[:, cols].astype(jnp.float32)
            cdf = 0.5 * (1.0 + lax.erf(values * root_half))
            gelu_out = values * cdf
            gelu[:, cols] = gelu_out
            slope[:, cols] = cdf + values * jnp.exp(-0.5 * values * values) * inv_root_two_pi
            sums[0:1, cols] = jnp.sum(gelu_out * gelu_out, axis=0, keepdims=True)
            sums[1:2, cols] = jnp.sum(upstream * gelu_out, axis=0, keepdims=True)
            shift[0:1, cols] = jnp.sum(upstream, axis=0, keepdims=True)
    last.wait()
    wide[...] = normed[...].astype(jnp.float32)


def gradient(sums, other, shift, gain, out_grad, gelu, slope, wide, result, keep, cross, *scratch):
    pre_grad, turned, gains, shifts, sems = scratch
    squares = sums[0:1, :] + other[0:1, :]
    response = sums[1:2, :] + other[1:2, :]
    channel_norm = jnp.sqrt(squares + 1e-06)
    norm_mean = jnp.sum(channel_norm, axis=1, keepdims=True) * (1.0 / H) + 1e-06
    scaled = channel_norm / norm_mean
    scaled_grad = gain[...] * response
    norm_grad = scaled_grad / norm_mean - jnp.sum(scaled_grad * channel_norm, axis=1, keepdims=True) / (
        H * norm_mean * norm_mean
    )
    of_upstream = gain[...] * scaled + 1.0
    of_gelu = norm_grad / channel_norm
    gain_term = sums[1:2, :] * scaled
    shift_term = shift[...]
    copies = []
    for p, (start, stop) in enumerate(zip(CUTS[:-1], CUTS[1:])):
        for k in range(start, stop):
            cols = slice(k * LANES, (k + 1) * LANES)
            upstream = out_grad[:, cols].astype(jnp.float32)
            act_grad = upstream * of_upstream[:, cols] + gelu[:, cols] * of_gelu[:, cols]
            rounded = (act_grad * slope[:, cols]).astype(jnp.bfloat16)
            pre_grad[:, cols] = rounded
            turned[cols, :] = rounded.astype(jnp.float32).T
        cols = pl.ds(start * LANES, (stop - start) * LANES)
        copies.append(pltpu.make_async_copy(pre_grad.at[:, cols], result.at[:, cols], sems.at[p]))
        copies[-1].start()
    both = jnp.concatenate([gain_term, shift_term, jnp.zeros((6, H), jnp.float32)], axis=0)
    for b in range(H // BLOCK):
        tile, start = divmod(b * BLOCK, LANES)
        window = both[:, tile * LANES : min((tile + 2) * LANES, H)]
        if start:
            window = pltpu.roll(window, window.shape[1] - start, 1)
        gains[b : b + 1, :] = window[0:1, :LANES]
        shifts[b : b + 1, :] = window[1:2, :LANES]
    core, x = lax.axis_index("core"), lax.axis_index("x")
    y = 2 * lax.axis_index("yh") + lax.axis_index("yl")
    for of_other in range(2):
        to = core if of_other == 0 else 1 - core
        mine, beside_mine = jnp.where(to == 0, x, y), jnp.where(to == 0, y, x)
        for j in range(4):
            chunk, top = (cross if of_other else keep), j * PART
            d = lax.rem(mine + j, 4)
            for i in range(4):
                e = lax.rem(beside_mine + i, 4)
                block_x, block_y = jnp.where(to == 0, d, e), jnp.where(to == 0, e, d)
                b = (block_y // 2) * 16 + to * 8 + block_x * 2 + lax.rem(block_y, 2)
                start = pl.multiple_of(b * BLOCK, 8)
                chunk[top + i * BLOCK : top + (i + 1) * BLOCK, :] = turned[pl.ds(start, BLOCK), :]
                row = top + 4 * BLOCK + i
                chunk[row : row + 1, :] = gains[pl.ds(b, 1), :]
                chunk[row + 4 : row + 5, :] = shifts[pl.ds(b, 1), :]
    cross[4 * PART :, :] = wide[...]
    for copy in copies:
        copy.wait()


def merge(keep, arrived, *outs):
    for j, out in enumerate(outs):
        out[:PART, :] = keep[j * PART : (j + 1) * PART, :]
        out[PART:, :] = arrived[j * PART : (j + 1) * PART, :]


def product(here, above, below, opposite, right_first, right_second, right_rest, *rest):
    outs, (left_first, left_second, left_rest) = rest[:4], rest[4:]
    one, two = slice(0, 4 * BLOCK), slice(PART, PART + 4 * BLOCK)
    sources = (
        (left_first, (here[one, :], below[one, :])),
        (left_second, (above[two, :], above[one, :], below[two, :])),
        (left_rest, (here[two, :], opposite[one, :], opposite[two, :])),
    )
    for left, values in sources:
        for s, value in enumerate(values):
            left[:, s * ROWS : (s + 1) * ROWS] = value.astype(jnp.bfloat16)
    rights = (right_first, right_second, right_rest)
    across_pixels = (((1,), (1,)), ((), ()))
    small = jnp.zeros((8, LANES), jnp.float32)
    for pair in (here, above, below, opposite):
        small = small + (pair[4 * BLOCK : PART, :] + pair[PART + 4 * BLOCK :, :])
    bias = 0.0
    for left, _ in sources:
        ones = jnp.ones((8, left.shape[1]), jnp.bfloat16)
        bias = bias + lax.dot_general(ones, left[...], across_pixels, preferred_element_type=jnp.float32)
    bias = jnp.concatenate([bias, jnp.zeros((8, 4 * LANES - 4 * BLOCK), jnp.float32)], axis=1)
    rows = []
    for i in range(4):
        tile, start = divmod(i * BLOCK, LANES)
        window = bias[:, tile * LANES : (tile + 2) * LANES]
        rows.append((pltpu.roll(window, 2 * LANES - start, 1) if start else window)[0:1, :LANES])
    small = jnp.concatenate([small, *rows, *rows], axis=0)
    for z in range(8):
        turned = pltpu.roll(small, LANES - z * OWN, 1) if z else small
        for i, out in enumerate(outs):
            row = z * PACKED + 61
            out[row : row + 1, :] = turned[8 + i : 9 + i, :]
            out[row + 1 : row + 2, :] = turned[i : i + 1, :]
            out[row + 2 : row + 3, :] = turned[4 + i : 5 + i, :]
    for group in range(3):
        cols = slice(2 * group * LANES, min(2 * (group + 1) * LANES, C))
        total = 0.0
        for (left, _), right in zip(sources, rights):
            total = total + lax.dot_general(
                left[...], right[cols, :], across_pixels, preferred_element_type=jnp.float32
            )
        if group == 2:
            last = total[:, LANES:]
            last = jnp.concatenate([last, last], axis=1)
            last = jnp.concatenate([last, jnp.zeros((8, LANES), jnp.float32)], axis=0)
            left_half = lax.broadcasted_iota(jnp.int32, (6, LANES), 1) < 64
        for i, out in enumerate(outs):
            for z in range(8):
                unit = i * BLOCK + z * OWN
                for k in range(2 * group, min(2 * group + 2, 5)):
                    row, col = z * PACKED + k * OWN, (k - 2 * group) * LANES
                    out[row : row + OWN, :] = total[unit : unit + OWN, col : col + LANES]
                if group == 2:
                    row = z * PACKED + 5 * OWN
                    out[row : row + 6, :] = jnp.where(left_half, last[unit : unit + 6], last[unit + 6 : unit + 12])


PACKED = 64


def add(a, b, c, d, out):
    out[...] = (a[...] + b[...]) + (c[...] + d[...])


def finish(parts, weight, gain, shift, bias):
    total = parts[0]
    for z in range(1, 8):
        total = total + parts[z]
    for k in range(5):
        weight[:, k * LANES : (k + 1) * LANES] = total[k * OWN : (k + 1) * OWN, :]
    last = total[5 * OWN : 5 * OWN + 6, :]
    weight[:6, 5 * LANES :] = last[:, :64]
    weight[6:, 5 * LANES :] = last[:5, 64:]
    bias[...] = total[61:62, :OWN]
    gain[...] = total[62:63, :OWN]
    shift[...] = total[63:64, :OWN]


def on_device(normed, pre_gelu, out_grad, grn_gain):
    bf16 = jnp.bfloat16
    wide, sums, shift, gelu, slope, upstream = call(
        statistics,
        [f32(C, ROWS), f32(2, H), f32(1, H), f32(ROWS, H), f32(ROWS, H), jax.ShapeDtypeStruct((ROWS, H), bf16)],
        scratch=[
            pltpu.VMEM((ROWS, H), bf16),
            pltpu.VMEM((C, ROWS), bf16),
            pltpu.SemaphoreType.DMA((2, 4)),
            pltpu.SemaphoreType.DMA,
        ],
        flops=60 * ROWS * H,
        moved=4_400_000,
        in_specs=[pl.BlockSpec(memory_space=pl.ANY)] * 3,
    )(*(pltpu.with_memory_space_constraint(v, pltpu.HBM) for v in (normed.T, pre_gelu, out_grad)))
    other = send(sums, other_half)

    from_below = send(wide, along(1))
    from_above = send(wide, along(-1))
    below_across = send(wide, across(1))
    above_across = send(wide, across(-1))

    def right_of(*wides, flops=GUIDE):
        shape = jax.ShapeDtypeStruct((C, len(wides) * ROWS), bf16)
        return call(narrow, shape, flops=flops, moved=4_400_000)(*wides)

    pre_grad, keep, cross = call(
        gradient,
        [jax.ShapeDtypeStruct((ROWS, H), bf16), f32(4 * PART, LANES), f32(4 * PART + C, LANES)],
        out_specs=[pl.BlockSpec(memory_space=pl.ANY)] + [pl.BlockSpec(memory_space=pltpu.VMEM)] * 2,
        scratch=[
            pltpu.VMEM((ROWS, H), bf16),
            pltpu.VMEM((H, LANES), jnp.float32),
            pltpu.VMEM((H // BLOCK, LANES), jnp.float32),
            pltpu.VMEM((H // BLOCK, LANES), jnp.float32),
            pltpu.SemaphoreType.DMA((4,)),
        ],
        flops=GUIDE // 5,
        moved=6_000_000,
    )(sums, other, shift, grn_gain.reshape(1, H), upstream, gelu, slope, wide)
    arrived = send(cross, other_core)
    right_first = right_of(wide, from_above, flops=GUIDE)
    arrived, right_first = lax.optimization_barrier((arrived, right_first))
    here, next_one, next_two, next_three = call(merge, [f32(2 * PART, LANES)] * 4, moved=4_400_000)(keep, arrived)
    far = send(from_below, along(1))
    far_across = send(above_across, along(-1))
    next_one, below_across, from_below = lax.optimization_barrier((next_one, below_across, from_below))
    right_second = right_of(below_across, from_below, above_across, flops=GUIDE)
    right_rest = right_of(arrived, far, far_across, flops=GUIDE)
    above = send(next_one, along(1))
    below = send(next_three, along(-1))
    opposite = send(next_two, along(2))
    own, *away = call(
        product,
        [f32(8 * PACKED, LANES)] * 4,
        scratch=[pltpu.VMEM((4 * BLOCK, n * ROWS), bf16) for n in (2, 3, 3)],
        flops=2 * 352 * 1024 * 768,
        moved=4_000_000,
    )(here, above, below, opposite, right_first, right_second, right_rest)
    stage = [send(away[1], beside(2)), send(away[0], beside(1)), send(away[2], beside(-1))]
    rows = call(add, f32(8 * PACKED, LANES), moved=1_400_000)(own, *stage)
    rows = lax.all_to_all(rows.reshape(8, PACKED, LANES), "z", 0, 0, tiled=True)
    weight, gain, shift, bias = call(
        finish, [f32(OWN, C), f32(1, OWN), f32(1, OWN), f32(1, OWN)], moved=330_000
    )(rows)
    return pre_grad, weight, gain.reshape(OWN), shift.reshape(OWN), bias.reshape(OWN)


def solution(mesh):
    split = Mesh(mesh.devices.reshape(SIZES), AXES)
    return jax.shard_map(
        on_device,
        mesh=split,
        in_specs=(P(AXES, None), P(AXES, None), P(AXES, None), P()),
        out_specs=(P(AXES, None), P(AXES, None), P(AXES), P(AXES), P(AXES)),
        check_vma=False,
    )
```

time: 73.2 us -> 65 us (0.89)
  waiting for transfers between devices: 28.5 us -> 19 us
  starting transfers between devices: 16.6 us -> 20.6 us
  local copies, waits for them, and re-layouts: 3.37 us -> 0.01 us
  Pallas kernels: 4.5 us -> 6.07 us
  blocking collectives: 19 us -> 17.8 us
    ppermute x18 -> x14, waiting for transfers between devices: 28.5 us -> 19 us  [send(): return lax.ppermute(value, AXES, pairs(target))]
    ppermute x18 -> x14, starting transfers between devices: 16.6 us -> 20.6 us  [send(): return lax.ppermute(value, AXES, pairs(target))]
    unnamed x9 -> x2, local copies, waits for them, and re-layouts: 3.36 us -> 0.01 us
    pallas_call x6 -> x8, Pallas kernels: 3.86 us -> 5.37 us  [the longest x1 2.1 us: on_device(): call(statistics, [f32(C, ROWS), f32(2, H), f32(1, H), f32(ROWS, H), f32(R...]
    all_to_all x1, blocking collectives: 19 us -> 17.8 us  [on_device(): rows = lax.all_to_all(rows.reshape(8, PACKED, LANES), 'z', 0, 0, tiled=True)]
  transfers between devices with their start and end apart: 18 -> 14, of which waited for: 11 -> 8; matrix products, arithmetic and copies ran while one was open for 0% -> 0% of each run, Pallas kernels for 4% -> 3%
where the time goes in v2:
time: 65 us; the launch traced here: 64.2 us
  starting transfers between devices  20.6 us (32%)
  waiting for transfers between devices  19 us (29%)
  blocking collectives  17.8 us (27%)
  Pallas kernels  6.07 us (9%)
  between operations  0.75 us (1%)
    ppermute x14, starting transfers between devices, send(): return lax.ppermute(value, AXES, pairs(target))  20.6 us
    ppermute x14, waiting for transfers between devices, send(): return lax.ppermute(value, AXES, pairs(target))  19 us
    all_to_all x1, blocking collectives, on_device(): rows = lax.all_to_all(rows.reshape(8, PACKED, LANES), 'z', 0, 0, tiled=True)  17.8 us
    pallas_call x1, Pallas kernels, on_device(): call(statistics, [f32(C, ROWS), f32(2, H), f32(1, H), f32(ROWS, H), f32(R...  2.1 us
    pallas_call x1, Pallas kernels, on_device(): call(gradient, [jax.ShapeDtypeStruct((ROWS, H), bf16), f32(4 * PART, LANE...  1.76 us
  transfers between devices with their start and end apart: 14, of which 8 were waited for; matrix products, arithmetic and copies ran while one was open for 0% of the time, Pallas kernels for 3%

profile of v2, /device:TPU:8, one launch (start us, length us, event | category | flops | bytes accessed | tf_op | source)
XLA Modules:
  0.0 64.2 jit_solution(11388916148041460536)
XLA Ops:
  0.6 2.1 %shard_map.83 = (f32[704,128]{1,0:T(8,128)S(1)}, f32[2,2816]{1,0:T(2,128)S(1)}, f32[1,2816]{1,0:T(1,128)S(1)}, f32[128,2816]{1,0:T(8,128)S(1)}, f32[128,2816]{1,0:T(8,128)S(1)}, /*index=5*/bf16[128,2816]{1,0:T(8,128)(2,1)S(1)}) custom-call(bf16[704,128]{1,0:T(8,128)(2,1)} %bitcast.6, bf16[128,2816]{1,0:T(8,128)(2,1)} %pre_gelu_hbm.1, ...), custom_call_target="tpu_custom_call" | custom-call | flops 21626880 | bytes 4400000 | tf_op jit(solution)/shard_map/pallas_call | solution.py:256
  2.8 2.0 %collective-permute-start = (f32[2,2816]{1,0:T(2,128)S(1)}, f32[2,2816]{1,0:T(2,128)S(1)}, u32[]{:S(2)}, u32[]{:S(2)}) collective-permute-start(f32[2,2816]{1,0:T(2,128)S(1)} %get-tuple-element.31.sums), channel_id=1, source_target_pairs={{0,1},{1,0},{2,3},{3,2},{4,5},{5,4},{6,7},{7,6},{8,9},{9,8},{10,11... | collective-permute-start | bytes 67592 | tf_op jit(solution)/shard_map/ppermute | solution.py:36
  4.8 1.5 %collective-permute-start.4 = (f32[704,128]{1,0:T(8,128)S(1)}, f32[704,128]{1,0:T(8,128)S(1)}, u32[]{:S(2)}, u32[]{:S(2)}) collective-permute-start(f32[704,128]{1,0:T(8,128)S(1)} %get-tuple-element.36.wide.refs_0_), channel_id=1, source_target_pairs={{0,16},{1,17},{2,18},{3,19},{4,20},{5,21},{6,22},{7,23},{8,24},{9,... | collective-permute-start | bytes 1081352 | tf_op jit(solution)/shard_map/ppermute | solution.py:36
  6.3 3.6 %collective-permute-start.3 = (f32[704,128]{1,0:T(8,128)S(1)}, f32[704,128]{1,0:T(8,128)S(1)}, u32[]{:S(2)}, u32[]{:S(2)}) collective-permute-start(f32[704,128]{1,0:T(8,128)S(1)} %get-tuple-element.36.wide.refs_0_), channel_id=1, source_target_pairs={{0,72},{1,73},{2,74},{3,75},{4,76},{5,77},{6,78},{7,79},{8,192},{9... | collective-permute-start | bytes 1081352 | tf_op jit(solution)/shard_map/ppermute | solution.py:36
  9.8 0.8 %collective-permute-start.2 = (f32[704,128]{1,0:T(8,128)S(1)}, f32[704,128]{1,0:T(8,128)S(1)}, u32[]{:S(2)}, u32[]{:S(2)}) collective-permute-start(f32[704,128]{1,0:T(8,128)S(1)} %get-tuple-element.36.wide.refs_0_), channel_id=1, source_target_pairs={{0,48},{1,49},{2,50},{3,51},{4,52},{5,53},{6,54},{7,55},{8,56},{9,... | collective-permute-start | bytes 1081352 | tf_op jit(solution)/shard_map/ppermute | solution.py:36
  10.7 1.8 %shard_map.84 = (bf16[128,2816]{1,0:T(8,128)(2,1)}, f32[1440,128]{1,0:T(8,128)S(1)}, f32[2144,128]{1,0:T(8,128)S(1)}) custom-call(f32[2,2816]{1,0:T(2,128)S(1)} %get-tuple-element.31.sums, f32[2,2816]{1,0:T(2,128)S(1)} %collective-permute-done.other, f32[1,2816]{1,0:T(1,128)S(1)} %get-tuple-element.32.shift, f32[1,2816]{1,0:T(1,128)S(1)} %reshape.25.gain, ...), custom_call_target="tpu_custom_call" | custom-call | flops 4000000000 | bytes 6000000 | tf_op jit(solution)/shard_map/pallas_call | solution.py:280
  12.5 3.1 %collective-permute-start.10 = (f32[704,128]{1,0:T(8,128)S(1)}, f32[704,128]{1,0:T(8,128)S(1)}, u32[]{:S(2)}, u32[]{:S(2)}) collective-permute-start(f32[704,128]{1,0:T(8,128)S(1)} %collective-permute-done.8.refs_2_), channel_id=1, source_target_pairs={{0,48},{1,49},{2,50},{3,51},{4,52},{5,53},{6,54},{7,55},{8,56},{9,... | collective-permute-start | bytes 1081352 | tf_op jit(solution)/shard_map/ppermute | solution.py:36
  15.7 0.5 collective-permute-done.4.refs_1_
  16.2 1.1 %collective-permute-done.2.refs_1_ = f32[704,128]{1,0:T(8,128)S(1)} collective-permute-done((f32[704,128]{1,0:T(8,128)S(1)}, f32[704,128]{1,0:T(8,128)S(1)}, u32[]{:S(2)}, u32[]{:S(2)}) %collective-permute-start.2) | collective-permute-done | bytes 360480 | tf_op jit(solution)/shard_map/ppermute | solution.py:36
  17.4 1.3 %collective-permute-start.5 = (f32[720,128]{1,0:T(8,128)S(1)}, f32[720,128]{1,0:T(8,128)S(1)}, u32[]{:S(2)}, u32[]{:S(2)}) collective-permute-start(f32[720,128]{1,0:T(8,128)S(1)} %get-tuple-element.43), channel_id=1, source_target_pairs={{0,16},{1,17},{2,18},{3,19},{4,20},{5,21},{6,22},{7,23},{8,24},{9,... | collective-permute-start | bytes 1105928 | tf_op jit(solution)/shard_map/ppermute | solution.py:36
  18.7 2.0 %collective-permute-start.6 = (f32[720,128]{1,0:T(8,128)S(1)}, f32[720,128]{1,0:T(8,128)S(1)}, u32[]{:S(2)}, u32[]{:S(2)}) collective-permute-start(f32[720,128]{1,0:T(8,128)S(1)} %get-tuple-element.44), channel_id=1, source_target_pairs={{0,48},{1,49},{2,50},{3,51},{4,52},{5,53},{6,54},{7,55},{8,56},{9,... | collective-permute-start | bytes 1105928 | tf_op jit(solution)/shard_map/ppermute | solution.py:36
  20.7 1.8 %collective-permute-start.7 = (f32[720,128]{1,0:T(8,128)S(1)}, f32[720,128]{1,0:T(8,128)S(1)}, u32[]{:S(2)}, u32[]{:S(2)}) collective-permute-start(f32[720,128]{1,0:T(8,128)S(1)} %get-tuple-element.45), channel_id=1, source_target_pairs={{0,32},{1,33},{2,34},{3,35},{4,36},{5,37},{6,38},{7,39},{8,40},{9,... | collective-permute-start | bytes 1105928 | tf_op jit(solution)/shard_map/ppermute | solution.py:36
  22.5 2.3 %collective-permute-done.9.refs_1_ = f32[704,128]{1,0:T(8,128)S(1)} collective-permute-done((f32[704,128]{1,0:T(8,128)S(1)}, f32[704,128]{1,0:T(8,128)S(1)}, u32[]{:S(2)}, u32[]{:S(2)}) %collective-permute-start.9) | collective-permute-done | bytes 360480 | tf_op jit(solution)/shard_map/ppermute | solution.py:36
  25.0 3.8 %collective-permute-done.5.above = f32[720,128]{1,0:T(8,128)S(1)} collective-permute-done((f32[720,128]{1,0:T(8,128)S(1)}, f32[720,128]{1,0:T(8,128)S(1)}, u32[]{:S(2)}, u32[]{:S(2)}) %collective-permute-start.5) | collective-permute-done | bytes 368672 | tf_op jit(solution)/shard_map/ppermute | solution.py:36
  28.8 1.0 %collective-permute-done.6.below = f32[720,128]{1,0:T(8,128)S(1)} collective-permute-done((f32[720,128]{1,0:T(8,128)S(1)}, f32[720,128]{1,0:T(8,128)S(1)}, u32[]{:S(2)}, u32[]{:S(2)}) %collective-permute-start.6) | collective-permute-done | bytes 368672 | tf_op jit(solution)/shard_map/ppermute | solution.py:36
  29.8 3.8 %collective-permute-done.7.opposite = f32[720,128]{1,0:T(8,128)S(1)} collective-permute-done((f32[720,128]{1,0:T(8,128)S(1)}, f32[720,128]{1,0:T(8,128)S(1)}, u32[]{:S(2)}, u32[]{:S(2)}) %collective-permute-start.7) | collective-permute-done | bytes 368672 | tf_op jit(solution)/shard_map/ppermute | solution.py:36
  33.5 1.2 %shard_map.89 = (f32[512,128]{1,0:T(8,128)S(1)}, f32[512,128]{1,0:T(8,128)S(1)}, f32[512,128]{1,0:T(8,128)S(1)}, f32[512,128]{1,0:T(8,128)S(1)}) custom-call(f32[720,128]{1,0:T(8,128)S(1)} %get-tuple-element.41.here, f32[720,128]{1,0:T(8,128)S(1)} %collective-permute-done.5.above, f32[720,128]{1,0:T(8,128)S(1)} %collective-permute-done.6.below, ...), custom_call_target="tpu_custom_call" | custom-call | flops 553648128 | bytes 4000000 | tf_op jit(solution)/shard_map/pallas_call | solution.py:306
  34.7 2.3 %collective-permute-start.11 = (f32[512,128]{1,0:T(8,128)S(1)}, f32[512,128]{1,0:T(8,128)S(1)}, u32[]{:S(2)}, u32[]{:S(2)}) collective-permute-start(f32[512,128]{1,0:T(8,128)S(1)} %get-tuple-element.50), channel_id=1, source_target_pairs={{0,128},{1,129},{2,130},{3,131},{4,132},{5,133},{6,134},{7,135},{8... | collective-permute-start | bytes 786440 | tf_op jit(solution)/shard_map/ppermute | solution.py:36
  37.0 1.8 %collective-permute-start.12 = (f32[512,128]{1,0:T(8,128)S(1)}, f32[512,128]{1,0:T(8,128)S(1)}, u32[]{:S(2)}, u32[]{:S(2)}) collective-permute-start(f32[512,128]{1,0:T(8,128)S(1)} %get-tuple-element.51), channel_id=1, source_target_pairs={{0,8},{1,9},{2,10},{3,11},{4,12},{5,13},{6,14},{7,15},{8,128},{9,1... | collective-permute-start | bytes 786440 | tf_op jit(solution)/shard_map/ppermute | solution.py:36
  38.8 0.2 collective-permute-start.13
  39.1 3.6 %collective-permute-done.11.b = f32[512,128]{1,0:T(8,128)S(1)} collective-permute-done((f32[512,128]{1,0:T(8,128)S(1)}, f32[512,128]{1,0:T(8,128)S(1)}, u32[]{:S(2)}, u32[]{:S(2)}) %collective-permute-start.11) | collective-permute-done | bytes 262176 | tf_op jit(solution)/shard_map/ppermute | solution.py:36
  42.7 2.9 %collective-permute-done.12.c = f32[512,128]{1,0:T(8,128)S(1)} collective-permute-done((f32[512,128]{1,0:T(8,128)S(1)}, f32[512,128]{1,0:T(8,128)S(1)}, u32[]{:S(2)}, u32[]{:S(2)}) %collective-permute-start.12) | collective-permute-done | bytes 262176 | tf_op jit(solution)/shard_map/ppermute | solution.py:36
  45.6 17.8 %all_to_all.5.parts = f32[8,64,128]{2,1,0:T(8,128)S(1)} all-to-all(f32[8,64,128]{2,1,0:T(8,128)S(1)} %bitcast.5), channel_id=1, replica_groups=mesh['yh'=2,'core'=2,'x'=4,'yl'=2,'z'=8] {'z'}, dimensions={0} | all-to-all | bytes 524288 | tf_op jit(solution)/shard_map/all_to_all | solution.py:315
  63.5 0.7 %shard_map.91 = (f32[11,704]{1,0:T(8,128)}, f32[1,11]{1,0:T(1,128)}, f32[1,11]{1,0:T(1,128)}, f32[1,11]{1,0:T(1,128)}) custom-call(f32[8,64,128]{2,1,0:T(8,128)S(1)} %all_to_all.5.parts), custom_call_target="tpu_custom_call" | custom-call | bytes 330000 | tf_op jit(solution)/shard_map/pallas_call | solution.py:316
  (17 shorter events, 0.5 us)
Async XLA Ops:
  0.6 10.0 %copy-start = (f32[2816]{0:T(1024)S(1)}, f32[2816]{0:T(1024)}, u32[]{:S(2)}) copy-start(f32[2816]{0:T(1024)} %param.7) | copy-start | bytes 33796
  2.8 7.9 %collective-permute-start = (f32[2,2816]{1,0:T(2,128)S(1)}, f32[2,2816]{1,0:T(2,128)S(1)}, u32[]{:S(2)}, u32[]{:S(2)}) collective-permute-start(f32[2,2816]{1,0:T(2,128)S(1)} %get-tuple-element.31.sums), channel_id=1, source_target_pairs={{0,1},{1,0},{2,3},{3,2},{4,5},{5,4},{6,7},{7,6},{8,9},{9,8},{10,11... | collective-permute-start | bytes 67592 | tf_op jit(solution)/shard_map/ppermute | solution.py:36
  4.8 7.8 %collective-permute-start.8 = (f32[704,128]{1,0:T(8,128)S(1)}, f32[704,128]{1,0:T(8,128)S(1)}, u32[]{:S(2)}, u32[]{:S(2)}) collective-permute-start(f32[704,128]{1,0:T(8,128)S(1)} %get-tuple-element.36.wide.refs_0_), channel_id=1, source_target_pairs={{0,200},{1,201},{2,202},{3,203},{4,204},{5,205},{6,206},{7,207},{8... | collective-permute-start | bytes 1081352 | tf_op jit(solution)/shard_map/ppermute | solution.py:36
  4.8 11.4 %collective-permute-start.4 = (f32[704,128]{1,0:T(8,128)S(1)}, f32[704,128]{1,0:T(8,128)S(1)}, u32[]{:S(2)}, u32[]{:S(2)}) collective-permute-start(f32[704,128]{1,0:T(8,128)S(1)} %get-tuple-element.36.wide.refs_0_), channel_id=1, source_target_pairs={{0,16},{1,17},{2,18},{3,19},{4,20},{5,21},{6,22},{7,23},{8,24},{9,... | collective-permute-start | bytes 1081352 | tf_op jit(solution)/shard_map/ppermute | solution.py:36
  6.3 11.2 %collective-permute-start.3 = (f32[704,128]{1,0:T(8,128)S(1)}, f32[704,128]{1,0:T(8,128)S(1)}, u32[]{:S(2)}, u32[]{:S(2)}) collective-permute-start(f32[704,128]{1,0:T(8,128)S(1)} %get-tuple-element.36.wide.refs_0_), channel_id=1, source_target_pairs={{0,72},{1,73},{2,74},{3,75},{4,76},{5,77},{6,78},{7,79},{8,192},{9... | collective-permute-start | bytes 1081352 | tf_op jit(solution)/shard_map/ppermute | solution.py:36
  9.8 7.4 %collective-permute-start.2 = (f32[704,128]{1,0:T(8,128)S(1)}, f32[704,128]{1,0:T(8,128)S(1)}, u32[]{:S(2)}, u32[]{:S(2)}) collective-permute-start(f32[704,128]{1,0:T(8,128)S(1)} %get-tuple-element.36.wide.refs_0_), channel_id=1, source_target_pairs={{0,48},{1,49},{2,50},{3,51},{4,52},{5,53},{6,54},{7,55},{8,56},{9,... | collective-permute-start | bytes 1081352 | tf_op jit(solution)/shard_map/ppermute | solution.py:36
  12.4 4.9 %collective-permute-start.1 = (f32[2144,128]{1,0:T(8,128)S(1)}, f32[2144,128]{1,0:T(8,128)S(1)}, u32[]{:S(2)}, u32[]{:S(2)}) collective-permute-start(f32[2144,128]{1,0:T(8,128)S(1)} %get-tuple-element.39), channel_id=1, source_target_pairs={{0,64},{1,65},{2,66},{3,67},{4,68},{5,69},{6,70},{7,71},{8,72},{9,... | collective-permute-start | bytes 3293192 | tf_op jit(solution)/shard_map/ppermute | solution.py:36
  12.5 10.0 %collective-permute-start.10 = (f32[704,128]{1,0:T(8,128)S(1)}, f32[704,128]{1,0:T(8,128)S(1)}, u32[]{:S(2)}, u32[]{:S(2)}) collective-permute-start(f32[704,128]{1,0:T(8,128)S(1)} %collective-permute-done.8.refs_2_), channel_id=1, source_target_pairs={{0,48},{1,49},{2,50},{3,51},{4,52},{5,53},{6,54},{7,55},{8,56},{9,... | collective-permute-start | bytes 1081352 | tf_op jit(solution)/shard_map/ppermute | solution.py:36
  16.2 8.6 %collective-permute-start.9 = (f32[704,128]{1,0:T(8,128)S(1)}, f32[704,128]{1,0:T(8,128)S(1)}, u32[]{:S(2)}, u32[]{:S(2)}) collective-permute-start(f32[704,128]{1,0:T(8,128)S(1)} %collective-permute-done.4.refs_1_), channel_id=1, source_target_pairs={{0,16},{1,17},{2,18},{3,19},{4,20},{5,21},{6,22},{7,23},{8,24},{9,... | collective-permute-start | bytes 1081352 | tf_op jit(solution)/shard_map/ppermute | solution.py:36
  17.4 11.3 %collective-permute-start.5 = (f32[720,128]{1,0:T(8,128)S(1)}, f32[720,128]{1,0:T(8,128)S(1)}, u32[]{:S(2)}, u32[]{:S(2)}) collective-permute-start(f32[720,128]{1,0:T(8,128)S(1)} %get-tuple-element.43), channel_id=1, source_target_pairs={{0,16},{1,17},{2,18},{3,19},{4,20},{5,21},{6,22},{7,23},{8,24},{9,... | collective-permute-start | bytes 1105928 | tf_op jit(solution)/shard_map/ppermute | solution.py:36
  18.7 11.0 %collective-permute-start.6 = (f32[720,128]{1,0:T(8,128)S(1)}, f32[720,128]{1,0:T(8,128)S(1)}, u32[]{:S(2)}, u32[]{:S(2)}) collective-permute-start(f32[720,128]{1,0:T(8,128)S(1)} %get-tuple-element.44), channel_id=1, source_target_pairs={{0,48},{1,49},{2,50},{3,51},{4,52},{5,53},{6,54},{7,55},{8,56},{9,... | collective-permute-start | bytes 1105928 | tf_op jit(solution)/shard_map/ppermute | solution.py:36
  20.7 12.8 %collective-permute-start.7 = (f32[720,128]{1,0:T(8,128)S(1)}, f32[720,128]{1,0:T(8,128)S(1)}, u32[]{:S(2)}, u32[]{:S(2)}) collective-permute-start(f32[720,128]{1,0:T(8,128)S(1)} %get-tuple-element.45), channel_id=1, source_target_pairs={{0,32},{1,33},{2,34},{3,35},{4,36},{5,37},{6,38},{7,39},{8,40},{9,... | collective-permute-start | bytes 1105928 | tf_op jit(solution)/shard_map/ppermute | solution.py:36
  34.7 8.0 %collective-permute-start.11 = (f32[512,128]{1,0:T(8,128)S(1)}, f32[512,128]{1,0:T(8,128)S(1)}, u32[]{:S(2)}, u32[]{:S(2)}) collective-permute-start(f32[512,128]{1,0:T(8,128)S(1)} %get-tuple-element.50), channel_id=1, source_target_pairs={{0,128},{1,129},{2,130},{3,131},{4,132},{5,133},{6,134},{7,135},{8... | collective-permute-start | bytes 786440 | tf_op jit(solution)/shard_map/ppermute | solution.py:36
  37.0 8.5 %collective-permute-start.12 = (f32[512,128]{1,0:T(8,128)S(1)}, f32[512,128]{1,0:T(8,128)S(1)}, u32[]{:S(2)}, u32[]{:S(2)}) collective-permute-start(f32[512,128]{1,0:T(8,128)S(1)} %get-tuple-element.51), channel_id=1, source_target_pairs={{0,8},{1,9},{2,10},{3,11},{4,12},{5,13},{6,14},{7,15},{8,128},{9,1... | collective-permute-start | bytes 786440 | tf_op jit(solution)/shard_map/ppermute | solution.py:36
  38.8 6.8 %collective-permute-start.13 = (f32[512,128]{1,0:T(8,128)S(1)}, f32[512,128]{1,0:T(8,128)S(1)}, u32[]{:S(2)}, u32[]{:S(2)}) collective-permute-start(f32[512,128]{1,0:T(8,128)S(1)} %get-tuple-element.52), channel_id=1, source_target_pairs={{0,136},{1,137},{2,138},{3,139},{4,140},{5,141},{6,142},{7,143},{8... | collective-permute-start | bytes 786440 | tf_op jit(solution)/shard_map/ppermute | solution.py:36

commit v3 on v2

--- a/solution.py
+++ b/solution.py
@@ -1,3 +1,5 @@
+import functools
+
 import jax
 import jax.numpy as jnp
 import numpy as np
@@ -16,7 +18,10 @@
 H = 2816
 BLOCK = 88
 OWN = 11
-PART = 4 * BLOCK + 8
+HALF = BLOCK // 2
+FIRST = 4 * HALF + 8
+SECOND = 4 * HALF
+PART = FIRST + SECOND
 LANES = 128
 MIB = 1 << 20
 GUIDE = 20_000_000_000
@@ -81,17 +86,27 @@
 CUTS = (0, 6, 12, 17, 22)
 
 
-def statistics(
-    normed_hbm, pre_gelu_hbm, out_grad_hbm, wide, sums, shift, gelu, slope, out_grad, pre_gelu, normed, sems, normed_sem
-):
+def widen(normed_hbm, wide, normed, sems):
+    half = C // 2
+    copies = [
+        pltpu.make_async_copy(normed_hbm.at[pl.ds(p * half, half)], normed.at[pl.ds(p * half, half)], sems.at[p])
+        for p in range(2)
+    ]
+    for copy in copies:
+        copy.start()
+    for p, copy in enumerate(copies):
+        copy.wait()
+        rows = slice(p * half, (p + 1) * half)
+        wide[rows, :] = normed[rows, :].astype(jnp.float32)
+
+
+def statistics(pre_gelu_hbm, out_grad_hbm, sums, shift, gelu, slope, out_grad, pre_gelu, sems):
     copies = []
     for p, (start, stop) in enumerate(zip(CUTS[:-1], CUTS[1:])):
         cols = pl.ds(start * LANES, (stop - start) * LANES)
         for n, (source, target) in enumerate(((pre_gelu_hbm, pre_gelu), (out_grad_hbm, out_grad))):
             copies.append(pltpu.make_async_copy(source.at[:, cols], target.at[:, cols], sems.at[n, p]))
             copies[-1].start()
-    last = pltpu.make_async_copy(normed_hbm, normed, normed_sem)
-    last.start()
     for p, (start, stop) in enumerate(zip(CUTS[:-1], CUTS[1:])):
         copies[2 * p].wait()
         copies[2 * p + 1].wait()
@@ -106,8 +121,6 @@
             sums[0:1, cols] = jnp.sum(gelu_out * gelu_out, axis=0, keepdims=True)
             sums[1:2, cols] = jnp.sum(upstream * gelu_out, axis=0, keepdims=True)
             shift[0:1, cols] = jnp.sum(upstream, axis=0, keepdims=True)
-    last.wait()
-    wide[...] = normed[...].astype(jnp.float32)
 
 
 def gradient(sums, other, shift, gain, out_grad, gelu, slope, wide, result, keep, cross, *scratch):
@@ -158,8 +171,10 @@
                 block_x, block_y = jnp.where(to == 0, d, e), jnp.where(to == 0, e, d)
                 b = (block_y // 2) * 16 + to * 8 + block_x * 2 + lax.rem(block_y, 2)
                 start = pl.multiple_of(b * BLOCK, 8)
-                chunk[top + i * BLOCK : top + (i + 1) * BLOCK, :] = turned[pl.ds(start, BLOCK), :]
-                row = top + 4 * BLOCK + i
+                units = turned[pl.ds(start, BLOCK), :]
+                chunk[top + i * HALF : top + (i + 1) * HALF, :] = units[:HALF]
+                chunk[top + FIRST + i * HALF : top + FIRST + (i + 1) * HALF, :] = units[HALF:]
+                row = top + 4 * HALF + i
                 chunk[row : row + 1, :] = gains[pl.ds(b, 1), :]
                 chunk[row + 4 : row + 5, :] = shifts[pl.ds(b, 1), :]
     cross[4 * PART :, :] = wide[...]
@@ -168,49 +183,62 @@
 
 
 def merge(keep, arrived, *outs):
-    for j, out in enumerate(outs):
-        out[:PART, :] = keep[j * PART : (j + 1) * PART, :]
-        out[PART:, :] = arrived[j * PART : (j + 1) * PART, :]
-
-
-def product(here, above, below, opposite, right_first, right_second, right_rest, *rest):
-    outs, (left_first, left_second, left_rest) = rest[:4], rest[4:]
-    one, two = slice(0, 4 * BLOCK), slice(PART, PART + 4 * BLOCK)
+    for j in range(4):
+        first, second = outs[j], outs[4 + j]
+        for n, source in enumerate((keep, arrived)):
+            middle = j * PART + FIRST
+            first[n * FIRST : (n + 1) * FIRST, :] = source[j * PART : middle, :]
+            second[n * SECOND : (n + 1) * SECOND, :] = source[middle : middle + SECOND, :]
+
+
+def product(half, here, above, below, opposite, right_first, right_second, right_rest, *rest):
+    if half == 0:
+        outs, terms, lefts = rest[:4], rest[4], rest[5:]
+    else:
+        terms, outs, lefts = rest[0], rest[1:5], rest[5:]
+    step = FIRST if half == 0 else SECOND
+    one, two = slice(0, 4 * HALF), slice(step, step + 4 * HALF)
     sources = (
-        (left_first, (here[one, :], below[one, :])),
-        (left_second, (above[two, :], above[one, :], below[two, :])),
-        (left_rest, (here[two, :], opposite[one, :], opposite[two, :])),
-    )
-    for left, values in sources:
+        (here[one, :], above[one, :], below[two, :]),
+        (above[two, :], below[one, :]),
+        (here[two, :], opposite[one, :], opposite[two, :]),
+    )
+    for left, values in zip(lefts, sources):
         for s, value in enumerate(values):
             left[:, s * ROWS : (s + 1) * ROWS] = value.astype(jnp.bfloat16)
     rights = (right_first, right_second, right_rest)
     across_pixels = (((1,), (1,)), ((), ()))
-    small = jnp.zeros((8, LANES), jnp.float32)
-    for pair in (here, above, below, opposite):
-        small = small + (pair[4 * BLOCK : PART, :] + pair[PART + 4 * BLOCK :, :])
+    if half == 0:
+        small = jnp.zeros((8, LANES), jnp.float32)
+        for pair in (here, above, below, opposite):
+            small = small + (pair[4 * HALF : FIRST, :] + pair[FIRST + 4 * HALF :, :])
+        terms[...] = small
+    else:
+        small = terms[...]
     bias = 0.0
-    for left, _ in sources:
+    for left in lefts:
         ones = jnp.ones((8, left.shape[1]), jnp.bfloat16)
         bias = bias + lax.dot_general(ones, left[...], across_pixels, preferred_element_type=jnp.float32)
-    bias = jnp.concatenate([bias, jnp.zeros((8, 4 * LANES - 4 * BLOCK), jnp.float32)], axis=1)
+    bias = jnp.concatenate([bias, jnp.zeros((8, 3 * LANES - 4 * HALF), jnp.float32)], axis=1)
     rows = []
     for i in range(4):
-        tile, start = divmod(i * BLOCK, LANES)
+        tile, start = divmod(i * HALF, LANES)
         window = bias[:, tile * LANES : (tile + 2) * LANES]
         rows.append((pltpu.roll(window, 2 * LANES - start, 1) if start else window)[0:1, :LANES])
-    small = jnp.concatenate([small, *rows, *rows], axis=0)
-    for z in range(8):
-        turned = pltpu.roll(small, LANES - z * OWN, 1) if z else small
+    bias = jnp.concatenate([*rows, *rows], axis=0)
+    for z in range(4):
+        skip = (4 * half + z) * OWN
+        turned = pltpu.roll(small, LANES - skip, 1) if skip else small
+        turned_bias = pltpu.roll(bias, LANES - z * OWN, 1) if z else bias
         for i, out in enumerate(outs):
             row = z * PACKED + 61
-            out[row : row + 1, :] = turned[8 + i : 9 + i, :]
+            out[row : row + 1, :] = turned_bias[i : i + 1, :]
             out[row + 1 : row + 2, :] = turned[i : i + 1, :]
             out[row + 2 : row + 3, :] = turned[4 + i : 5 + i, :]
     for group in range(3):
         cols = slice(2 * group * LANES, min(2 * (group + 1) * LANES, C))
         total = 0.0
-        for (left, _), right in zip(sources, rights):
+        for left, right in zip(lefts, rights):
             total = total + lax.dot_general(
                 left[...], right[cols, :], across_pixels, preferred_element_type=jnp.float32
             )
@@ -220,8 +248,8 @@
             last = jnp.concatenate([last, jnp.zeros((8, LANES), jnp.float32)], axis=0)
             left_half = lax.broadcasted_iota(jnp.int32, (6, LANES), 1) < 64
         for i, out in enumerate(outs):
-            for z in range(8):
-                unit = i * BLOCK + z * OWN
+            for z in range(4):
+                unit = i * HALF + z * OWN
                 for k in range(2 * group, min(2 * group + 2, 5)):
                     row, col = z * PACKED + k * OWN, (k - 2 * group) * LANES
                     out[row : row + OWN, :] = total[unit : unit + OWN, col : col + LANES]
@@ -235,6 +263,11 @@
 
 def add(a, b, c, d, out):
     out[...] = (a[...] + b[...]) + (c[...] + d[...])
+
+
+def add_below(above, a, b, c, d, out):
+    out[:4] = above[...].reshape(4, PACKED, LANES)
+    out[4:] = ((a[...] + b[...]) + (c[...] + d[...])).reshape(4, PACKED, LANES)
 
 
 def finish(parts, weight, gain, shift, bias):
@@ -253,19 +286,24 @@
 
 def on_device(normed, pre_gelu, out_grad, grn_gain):
     bf16 = jnp.bfloat16
-    wide, sums, shift, gelu, slope, upstream = call(
+    normed, pre_gelu, out_grad = (
+        pltpu.with_memory_space_constraint(v, pltpu.HBM) for v in (normed.T, pre_gelu, out_grad)
+    )
+    wide = call(
+        widen,
+        f32(C, ROWS),
+        scratch=[pltpu.VMEM((C, ROWS), bf16), pltpu.SemaphoreType.DMA((2,))],
+        moved=540_000,
+        in_specs=[pl.BlockSpec(memory_space=pl.ANY)],
+    )(normed)
+    sums, shift, gelu, slope, upstream = call(
         statistics,
-        [f32(C, ROWS), f32(2, H), f32(1, H), f32(ROWS, H), f32(ROWS, H), jax.ShapeDtypeStruct((ROWS, H), bf16)],
-        scratch=[
-            pltpu.VMEM((ROWS, H), bf16),
-            pltpu.VMEM((C, ROWS), bf16),
-            pltpu.SemaphoreType.DMA((2, 4)),
-            pltpu.SemaphoreType.DMA,
-        ],
-        flops=60 * ROWS * H,
+        [f32(2, H), f32(1, H), f32(ROWS, H), f32(ROWS, H), jax.ShapeDtypeStruct((ROWS, H), bf16)],
+        scratch=[pltpu.VMEM((ROWS, H), bf16), pltpu.SemaphoreType.DMA((2, 4))],
+        flops=0,
         moved=4_400_000,
-        in_specs=[pl.BlockSpec(memory_space=pl.ANY)] * 3,
-    )(*(pltpu.with_memory_space_constraint(v, pltpu.HBM) for v in (normed.T, pre_gelu, out_grad)))
+        in_specs=[pl.BlockSpec(memory_space=pl.ANY)] * 2,
+    )(pre_gelu, out_grad)
     other = send(sums, other_half)
 
     from_below = send(wide, along(1))
@@ -288,31 +326,44 @@
             pltpu.VMEM((H // BLOCK, LANES), jnp.float32),
             pltpu.SemaphoreType.DMA((4,)),
         ],
-        flops=GUIDE // 5,
+        flops=0,
         moved=6_000_000,
     )(sums, other, shift, grn_gain.reshape(1, H), upstream, gelu, slope, wide)
     arrived = send(cross, other_core)
-    right_first = right_of(wide, from_above, flops=GUIDE)
+    right_first = right_of(wide, from_below, above_across, flops=GUIDE)
     arrived, right_first = lax.optimization_barrier((arrived, right_first))
-    here, next_one, next_two, next_three = call(merge, [f32(2 * PART, LANES)] * 4, moved=4_400_000)(keep, arrived)
+    firsts_and_seconds = call(
+        merge, [f32(2 * FIRST, LANES)] * 4 + [f32(2 * SECOND, LANES)] * 4, moved=4_400_000
+    )(keep, arrived)
     far = send(from_below, along(1))
     far_across = send(above_across, along(-1))
-    next_one, below_across, from_below = lax.optimization_barrier((next_one, below_across, from_below))
-    right_second = right_of(below_across, from_below, above_across, flops=GUIDE)
+    firsts, seconds = list(firsts_and_seconds[:4]), list(firsts_and_seconds[4:])
+    firsts[1], from_above, below_across = lax.optimization_barrier((firsts[1], from_above, below_across))
+    right_second = right_of(below_across, from_above, flops=GUIDE)
     right_rest = right_of(arrived, far, far_across, flops=GUIDE)
-    above = send(next_one, along(1))
-    below = send(next_three, along(-1))
-    opposite = send(next_two, along(2))
-    own, *away = call(
-        product,
-        [f32(8 * PACKED, LANES)] * 4,
-        scratch=[pltpu.VMEM((4 * BLOCK, n * ROWS), bf16) for n in (2, 3, 3)],
-        flops=2 * 352 * 1024 * 768,
-        moved=4_000_000,
-    )(here, above, below, opposite, right_first, right_second, right_rest)
-    stage = [send(away[1], beside(2)), send(away[0], beside(1)), send(away[2], beside(-1))]
-    rows = call(add, f32(8 * PACKED, LANES), moved=1_400_000)(own, *stage)
-    rows = lax.all_to_all(rows.reshape(8, PACKED, LANES), "z", 0, 0, tiled=True)
+
+    def around(own, one, two, three):
+        return own, send(one, along(1)), send(three, along(-1)), send(two, along(2))
+
+    def multiply(half, parts, terms=(), flops=0):
+        outs = [f32(4 * PACKED, LANES)] * 4 + ([f32(8, LANES)] if half == 0 else [])
+        return call(
+            functools.partial(product, half),
+            outs,
+            scratch=[pltpu.VMEM((4 * HALF, n * ROWS), bf16) for n in (3, 2, 3)],
+            flops=flops,
+            moved=4_000_000,
+        )(*parts, right_first, right_second, right_rest, *terms)
+
+    def reduce_beside(own, one, two, three):
+        return own, send(two, beside(2)), send(one, beside(1)), send(three, beside(-1))
+
+    *products, terms = multiply(0, around(*firsts), flops=GUIDE)
+    rows = reduce_beside(*products)
+    rows = call(add, f32(4 * PACKED, LANES), flops=GUIDE//10, moved=700_000)(*rows)
+    others = reduce_beside(*multiply(1, around(*seconds), (terms,), flops=GUIDE))
+    rows = call(add_below, f32(8, PACKED, LANES), moved=1_000_000)(rows, *others)
+    rows = lax.all_to_all(rows, "z", 0, 0, tiled=True)
     weight, gain, shift, bias = call(
         finish, [f32(OWN, C), f32(1, OWN), f32(1, OWN), f32(1, OWN)], moved=330_000
     )(rows)

time: 65 us -> 62.5 us (0.962)
  waiting for transfers between devices: 19 us -> 11 us
  starting transfers between devices: 20.6 us -> 25 us
  Pallas kernels: 6.07 us -> 7.49 us
    ppermute x14 -> x20, waiting for transfers between devices: 19 us -> 11 us  [send(): return lax.ppermute(value, AXES, pairs(target))]
    ppermute x14 -> x20, starting transfers between devices: 20.6 us -> 25 us  [send(): return lax.ppermute(value, AXES, pairs(target))]
    pallas_call x4 -> x7, Pallas kernels: 3.42 us -> 4.82 us  [the longest x1 2.06 us: on_device(): call(statistics, [f32(2, H), f32(1, H), f32(ROWS, H), f32(ROWS, H), jax.S...]
  transfers between devices with their start and end apart: 14 -> 20, of which waited for: 8 -> 8; matrix products, arithmetic and copies ran while one was open for 0% -> 0% of each run, Pallas kernels for 3% -> 9%
where the time goes in v3:
time: 62.5 us; the launch traced here: 62.1 us
  starting transfers between devices  25 us (40%)
  blocking collectives  17.8 us (28%)
  waiting for transfers between devices  11 us (18%)
  Pallas kernels  7.49 us (12%)
  between operations  0.76 us (1%)
    ppermute x20, starting transfers between devices, send(): return lax.ppermute(value, AXES, pairs(target))  25 us
    all_to_all x1, blocking collectives, on_device(): rows = lax.all_to_all(rows, 'z', 0, 0, tiled=True)  17.8 us
    ppermute x20, waiting for transfers between devices, send(): return lax.ppermute(value, AXES, pairs(target))  11 us
    pallas_call x1, Pallas kernels, on_device(): call(statistics, [f32(2, H), f32(1, H), f32(ROWS, H), f32(ROWS, H), jax.S...  2.06 us
    pallas_call x1, Pallas kernels, on_device(): call(gradient, [jax.ShapeDtypeStruct((ROWS, H), bf16), f32(4 * PART, LANE...  1.77 us
    pallas_call x2, Pallas kernels, multiply(): call(functools.partial(product, half), outs, scratch=[pltpu.VMEM((4 * HAL...  1.63 us
  transfers between devices with their start and end apart: 20, of which 8 were waited for; matrix products, arithmetic and copies ran while one was open for 0% of the time, Pallas kernels for 9%

profile of v3, /device:TPU:8, one launch (start us, length us, event | category | flops | bytes accessed | tf_op | source)
XLA Modules:
  0.0 62.1 jit_solution(5134092959729152771)
XLA Ops:
  0.6 1.0 %shard_map.84.wide.refs_0_ = f32[704,128]{1,0:T(8,128)S(1)} custom-call(bf16[704,128]{1,0:T(8,128)(2,1)} %bitcast.4), custom_call_target="tpu_custom_call" | custom-call | bytes 540000 | tf_op jit(solution)/shard_map/pallas_call | solution.py:292
  1.7 1.6 %collective-permute-start.2 = (f32[704,128]{1,0:T(8,128)S(1)}, f32[704,128]{1,0:T(8,128)S(1)}, u32[]{:S(2)}, u32[]{:S(2)}) collective-permute-start(f32[704,128]{1,0:T(8,128)S(1)} %shard_map.84.wide.refs_0_), channel_id=1, source_target_pairs={{0,16},{1,17},{2,18},{3,19},{4,20},{5,21},{6,22},{7,23},{8,24},{9,... | collective-permute-start | bytes 1081352 | tf_op jit(solution)/shard_map/ppermute | solution.py:41
  3.3 2.1 %shard_map.83 = (f32[2,2816]{1,0:T(2,128)S(1)}, f32[1,2816]{1,0:T(1,128)S(1)}, f32[128,2816]{1,0:T(8,128)S(1)}, f32[128,2816]{1,0:T(8,128)S(1)}, bf16[128,2816]{1,0:T(8,128)(2,1)S(1)}) custom-call(bf16[128,2816]{1,0:T(8,128)(2,1)} %pre_gelu_hbm.1, bf16[128,2816]{1,0:T(8,128)(2,1)} %out_grad_hbm.1), custom_call_target="tpu_custom_call" | custom-call | bytes 4400000 | tf_op jit(solution)/shard_map/pallas_call | solution.py:299
  5.3 2.0 %collective-permute-start = (f32[2,2816]{1,0:T(2,128)S(1)}, f32[2,2816]{1,0:T(2,128)S(1)}, u32[]{:S(2)}, u32[]{:S(2)}) collective-permute-start(f32[2,2816]{1,0:T(2,128)S(1)} %get-tuple-element.39.sums), channel_id=1, source_target_pairs={{0,1},{1,0},{2,3},{3,2},{4,5},{5,4},{6,7},{7,6},{8,9},{9,8},{10,11... | collective-permute-start | bytes 67592 | tf_op jit(solution)/shard_map/ppermute | solution.py:41
  7.4 1.7 %collective-permute-start.4 = (f32[704,128]{1,0:T(8,128)S(1)}, f32[704,128]{1,0:T(8,128)S(1)}, u32[]{:S(2)}, u32[]{:S(2)}) collective-permute-start(f32[704,128]{1,0:T(8,128)S(1)} %shard_map.84.wide.refs_0_), channel_id=1, source_target_pairs={{0,48},{1,49},{2,50},{3,51},{4,52},{5,53},{6,54},{7,55},{8,56},{9,... | collective-permute-start | bytes 1081352 | tf_op jit(solution)/shard_map/ppermute | solution.py:41
  9.1 1.9 %collective-permute-start.5 = (f32[704,128]{1,0:T(8,128)S(1)}, f32[704,128]{1,0:T(8,128)S(1)}, u32[]{:S(2)}, u32[]{:S(2)}) collective-permute-start(f32[704,128]{1,0:T(8,128)S(1)} %shard_map.84.wide.refs_0_), channel_id=1, source_target_pairs={{0,72},{1,73},{2,74},{3,75},{4,76},{5,77},{6,78},{7,79},{8,192},{9... | collective-permute-start | bytes 1081352 | tf_op jit(solution)/shard_map/ppermute | solution.py:41
  11.0 1.8 %shard_map.85 = (bf16[128,2816]{1,0:T(8,128)(2,1)}, f32[1440,128]{1,0:T(8,128)S(1)}, f32[2144,128]{1,0:T(8,128)S(1)}) custom-call(f32[2,2816]{1,0:T(2,128)S(1)} %get-tuple-element.39.sums, f32[2,2816]{1,0:T(2,128)S(1)} %collective-permute-done.other, f32[1,2816]{1,0:T(1,128)S(1)} %get-tuple-element.40.shift, f32[1,2816]{1,0:T(1,128)S(1)} %reshape.22.gain, ...), custom_call_target="tpu_custom_call" | custom-call | bytes 6000000 | tf_op jit(solution)/shard_map/pallas_call | solution.py:318
  13.0 1.3 %collective-permute-start.10 = (f32[704,128]{1,0:T(8,128)S(1)}, f32[704,128]{1,0:T(8,128)S(1)}, u32[]{:S(2)}, u32[]{:S(2)}) collective-permute-start(f32[704,128]{1,0:T(8,128)S(1)} %collective-permute-done.3.refs_2_), channel_id=1, source_target_pairs={{0,48},{1,49},{2,50},{3,51},{4,52},{5,53},{6,54},{7,55},{8,56},{9,... | collective-permute-start | bytes 1081352 | tf_op jit(solution)/shard_map/ppermute | solution.py:41
  15.7 1.4 %collective-permute-done.5.refs_0_ = f32[704,128]{1,0:T(8,128)S(1)} collective-permute-done((f32[704,128]{1,0:T(8,128)S(1)}, f32[704,128]{1,0:T(8,128)S(1)}, u32[]{:S(2)}, u32[]{:S(2)}) %collective-permute-start.5) | collective-permute-done | bytes 360480 | tf_op jit(solution)/shard_map/ppermute | solution.py:41
  17.2 3.2 %collective-permute-start.7 = (f32[368,128]{1,0:T(8,128)S(1)}, f32[368,128]{1,0:T(8,128)S(1)}, u32[]{:S(2)}, u32[]{:S(2)}) collective-permute-start(f32[368,128]{1,0:T(8,128)S(1)} %get-tuple-element.51), channel_id=1, source_target_pairs={{0,48},{1,49},{2,50},{3,51},{4,52},{5,53},{6,54},{7,55},{8,56},{9,... | collective-permute-start | bytes 565256 | tf_op jit(solution)/shard_map/ppermute | solution.py:41
  20.5 0.9 %collective-permute-start.14 = (f32[352,128]{1,0:T(8,128)S(1)}, f32[352,128]{1,0:T(8,128)S(1)}, u32[]{:S(2)}, u32[]{:S(2)}) collective-permute-start(f32[352,128]{1,0:T(8,128)S(1)} %get-tuple-element.61), channel_id=1, source_target_pairs={{0,16},{1,17},{2,18},{3,19},{4,20},{5,21},{6,22},{7,23},{8,24},{9,... | collective-permute-start | bytes 540680 | tf_op jit(solution)/shard_map/ppermute | solution.py:41
  21.4 1.7 %collective-permute-done.9.refs_1_ = f32[704,128]{1,0:T(8,128)S(1)} collective-permute-done((f32[704,128]{1,0:T(8,128)S(1)}, f32[704,128]{1,0:T(8,128)S(1)}, u32[]{:S(2)}, u32[]{:S(2)}) %collective-permute-start.9) | collective-permute-done | bytes 360480 | tf_op jit(solution)/shard_map/ppermute | solution.py:41
  23.9 1.3 %collective-permute-done.6.above = f32[368,128]{1,0:T(8,128)S(1)} collective-permute-done((f32[368,128]{1,0:T(8,128)S(1)}, f32[368,128]{1,0:T(8,128)S(1)}, u32[]{:S(2)}, u32[]{:S(2)}) %collective-permute-start.6) | collective-permute-done | bytes 188448 | tf_op jit(solution)/shard_map/ppermute | solution.py:41
  25.2 1.3 %collective-permute-start.16 = (f32[352,128]{1,0:T(8,128)S(1)}, f32[352,128]{1,0:T(8,128)S(1)}, u32[]{:S(2)}, u32[]{:S(2)}) collective-permute-start(f32[352,128]{1,0:T(8,128)S(1)} %get-tuple-element.63), channel_id=1, source_target_pairs={{0,32},{1,33},{2,34},{3,35},{4,36},{5,37},{6,38},{7,39},{8,40},{9,... | collective-permute-start | bytes 540680 | tf_op jit(solution)/shard_map/ppermute | solution.py:41
  26.5 1.1 %collective-permute-done.8.opposite = f32[368,128]{1,0:T(8,128)S(1)} collective-permute-done((f32[368,128]{1,0:T(8,128)S(1)}, f32[368,128]{1,0:T(8,128)S(1)}, u32[]{:S(2)}, u32[]{:S(2)}) %collective-permute-start.8) | collective-permute-done | bytes 188448 | tf_op jit(solution)/shard_map/ppermute | solution.py:41
  27.6 0.8 %shard_map.90 = (f32[256,128]{1,0:T(8,128)S(1)}, f32[256,128]{1,0:T(8,128)S(1)}, f32[256,128]{1,0:T(8,128)S(1)}, f32[256,128]{1,0:T(8,128)S(1)}, f32[8,128]{1,0:T(8,128)S(1)}) custom-call(f32[368,128]{1,0:T(8,128)S(1)} %get-tuple-element.48.here, f32[368,128]{1,0:T(8,128)S(1)} %collective-permute-done.6.above, f32[368,128]{1,0:T(8,128)S(1)} %collective-permute-done.7.below, ...), custom_call_target="tpu_custom_call" | custom-call | flops 20000000000 | bytes 4000000 | tf_op jit(solution)/shard_map/pallas_call | solution.py:350
  28.4 2.5 %collective-permute-start.11 = (f32[256,128]{1,0:T(8,128)S(1)}, f32[256,128]{1,0:T(8,128)S(1)}, u32[]{:S(2)}, u32[]{:S(2)}) collective-permute-start(f32[256,128]{1,0:T(8,128)S(1)} %get-tuple-element.57), channel_id=1, source_target_pairs={{0,128},{1,129},{2,130},{3,131},{4,132},{5,133},{6,134},{7,135},{8... | collective-permute-start | bytes 393224 | tf_op jit(solution)/shard_map/ppermute | solution.py:41
  30.9 1.9 %collective-permute-start.12 = (f32[256,128]{1,0:T(8,128)S(1)}, f32[256,128]{1,0:T(8,128)S(1)}, u32[]{:S(2)}, u32[]{:S(2)}) collective-permute-start(f32[256,128]{1,0:T(8,128)S(1)} %get-tuple-element.58), channel_id=1, source_target_pairs={{0,8},{1,9},{2,10},{3,11},{4,12},{5,13},{6,14},{7,15},{8,128},{9,1... | collective-permute-start | bytes 393224 | tf_op jit(solution)/shard_map/ppermute | solution.py:41
  33.7 1.7 %collective-permute-start.17 = (f32[256,128]{1,0:T(8,128)S(1)}, f32[256,128]{1,0:T(8,128)S(1)}, u32[]{:S(2)}, u32[]{:S(2)}) collective-permute-start(f32[256,128]{1,0:T(8,128)S(1)} %get-tuple-element.66), channel_id=1, source_target_pairs={{0,128},{1,129},{2,130},{3,131},{4,132},{5,133},{6,134},{7,135},{8... | collective-permute-start | bytes 393224 | tf_op jit(solution)/shard_map/ppermute | solution.py:41
  35.4 3.1 %collective-permute-start.18 = (f32[256,128]{1,0:T(8,128)S(1)}, f32[256,128]{1,0:T(8,128)S(1)}, u32[]{:S(2)}, u32[]{:S(2)}) collective-permute-start(f32[256,128]{1,0:T(8,128)S(1)} %get-tuple-element.67), channel_id=1, source_target_pairs={{0,8},{1,9},{2,10},{3,11},{4,12},{5,13},{6,14},{7,15},{8,128},{9,1... | collective-permute-start | bytes 393224 | tf_op jit(solution)/shard_map/ppermute | solution.py:41
  38.6 1.7 %collective-permute-done.17.b = f32[256,128]{1,0:T(8,128)S(1)} collective-permute-done((f32[256,128]{1,0:T(8,128)S(1)}, f32[256,128]{1,0:T(8,128)S(1)}, u32[]{:S(2)}, u32[]{:S(2)}) %collective-permute-start.17) | collective-permute-done | bytes 131104 | tf_op jit(solution)/shard_map/ppermute | solution.py:41
  40.3 1.8 %collective-permute-done.18.c = f32[256,128]{1,0:T(8,128)S(1)} collective-permute-done((f32[256,128]{1,0:T(8,128)S(1)}, f32[256,128]{1,0:T(8,128)S(1)}, u32[]{:S(2)}, u32[]{:S(2)}) %collective-permute-start.18) | collective-permute-done | bytes 131104 | tf_op jit(solution)/shard_map/ppermute | solution.py:41
  42.1 1.4 %collective-permute-done.19.d = f32[256,128]{1,0:T(8,128)S(1)} collective-permute-done((f32[256,128]{1,0:T(8,128)S(1)}, f32[256,128]{1,0:T(8,128)S(1)}, u32[]{:S(2)}, u32[]{:S(2)}) %collective-permute-start.19) | collective-permute-done | bytes 131104 | tf_op jit(solution)/shard_map/ppermute | solution.py:41
  43.6 17.8 %all_to_all.5.parts = f32[8,64,128]{2,1,0:T(8,128)S(1)} all-to-all(f32[8,64,128]{2,1,0:T(8,128)S(1)} %shard_map.93), channel_id=1, replica_groups=mesh['yh'=2,'core'=2,'x'=4,'yl'=2,'z'=8] {'z'}, dimensions={0} | all-to-all | bytes 524288 | tf_op jit(solution)/shard_map/all_to_all | solution.py:366
  (32 shorter events, 4.2 us)
Async XLA Ops:
  0.6 10.4 %copy-start = (f32[2816]{0:T(1024)S(1)}, f32[2816]{0:T(1024)}, u32[]{:S(2)}) copy-start(f32[2816]{0:T(1024)} %param.7) | copy-start | bytes 33796
  1.6 11.4 %collective-permute-start.3 = (f32[704,128]{1,0:T(8,128)S(1)}, f32[704,128]{1,0:T(8,128)S(1)}, u32[]{:S(2)}, u32[]{:S(2)}) collective-permute-start(f32[704,128]{1,0:T(8,128)S(1)} %shard_map.84.wide.refs_0_), channel_id=1, source_target_pairs={{0,200},{1,201},{2,202},{3,203},{4,204},{5,205},{6,206},{7,207},{8... | collective-permute-start | bytes 1081352 | tf_op jit(solution)/shard_map/ppermute | solution.py:41
  1.7 12.6 %collective-permute-start.2 = (f32[704,128]{1,0:T(8,128)S(1)}, f32[704,128]{1,0:T(8,128)S(1)}, u32[]{:S(2)}, u32[]{:S(2)}) collective-permute-start(f32[704,128]{1,0:T(8,128)S(1)} %shard_map.84.wide.refs_0_), channel_id=1, source_target_pairs={{0,16},{1,17},{2,18},{3,19},{4,20},{5,21},{6,22},{7,23},{8,24},{9,... | collective-permute-start | bytes 1081352 | tf_op jit(solution)/shard_map/ppermute | solution.py:41
  5.3 5.7 %collective-permute-start = (f32[2,2816]{1,0:T(2,128)S(1)}, f32[2,2816]{1,0:T(2,128)S(1)}, u32[]{:S(2)}, u32[]{:S(2)}) collective-permute-start(f32[2,2816]{1,0:T(2,128)S(1)} %get-tuple-element.39.sums), channel_id=1, source_target_pairs={{0,1},{1,0},{2,3},{3,2},{4,5},{5,4},{6,7},{7,6},{8,9},{9,8},{10,11... | collective-permute-start | bytes 67592 | tf_op jit(solution)/shard_map/ppermute | solution.py:41
  7.4 8.4 %collective-permute-start.4 = (f32[704,128]{1,0:T(8,128)S(1)}, f32[704,128]{1,0:T(8,128)S(1)}, u32[]{:S(2)}, u32[]{:S(2)}) collective-permute-start(f32[704,128]{1,0:T(8,128)S(1)} %shard_map.84.wide.refs_0_), channel_id=1, source_target_pairs={{0,48},{1,49},{2,50},{3,51},{4,52},{5,53},{6,54},{7,55},{8,56},{9,... | collective-permute-start | bytes 1081352 | tf_op jit(solution)/shard_map/ppermute | solution.py:41
  9.1 8.1 %collective-permute-start.5 = (f32[704,128]{1,0:T(8,128)S(1)}, f32[704,128]{1,0:T(8,128)S(1)}, u32[]{:S(2)}, u32[]{:S(2)}) collective-permute-start(f32[704,128]{1,0:T(8,128)S(1)} %shard_map.84.wide.refs_0_), channel_id=1, source_target_pairs={{0,72},{1,73},{2,74},{3,75},{4,76},{5,77},{6,78},{7,79},{8,192},{9... | collective-permute-start | bytes 1081352 | tf_op jit(solution)/shard_map/ppermute | solution.py:41
  12.8 2.8 %collective-permute-start.1 = (f32[2144,128]{1,0:T(8,128)S(1)}, f32[2144,128]{1,0:T(8,128)S(1)}, u32[]{:S(2)}, u32[]{:S(2)}) collective-permute-start(f32[2144,128]{1,0:T(8,128)S(1)} %get-tuple-element.46), channel_id=1, source_target_pairs={{0,64},{1,65},{2,66},{3,67},{4,68},{5,69},{6,70},{7,71},{8,72},{9,... | collective-permute-start | bytes 3293192 | tf_op jit(solution)/shard_map/ppermute | solution.py:41
  13.0 7.4 %collective-permute-start.10 = (f32[704,128]{1,0:T(8,128)S(1)}, f32[704,128]{1,0:T(8,128)S(1)}, u32[]{:S(2)}, u32[]{:S(2)}) collective-permute-start(f32[704,128]{1,0:T(8,128)S(1)} %collective-permute-done.3.refs_2_), channel_id=1, source_target_pairs={{0,48},{1,49},{2,50},{3,51},{4,52},{5,53},{6,54},{7,55},{8,56},{9,... | collective-permute-start | bytes 1081352 | tf_op jit(solution)/shard_map/ppermute | solution.py:41
  14.4 8.7 %collective-permute-start.9 = (f32[704,128]{1,0:T(8,128)S(1)}, f32[704,128]{1,0:T(8,128)S(1)}, u32[]{:S(2)}, u32[]{:S(2)}) collective-permute-start(f32[704,128]{1,0:T(8,128)S(1)} %collective-permute-done.2.refs_1_), channel_id=1, source_target_pairs={{0,16},{1,17},{2,18},{3,19},{4,20},{5,21},{6,22},{7,23},{8,24},{9,... | collective-permute-start | bytes 1081352 | tf_op jit(solution)/shard_map/ppermute | solution.py:41
  17.2 8.0 %collective-permute-start.6 = (f32[368,128]{1,0:T(8,128)S(1)}, f32[368,128]{1,0:T(8,128)S(1)}, u32[]{:S(2)}, u32[]{:S(2)}) collective-permute-start(f32[368,128]{1,0:T(8,128)S(1)} %get-tuple-element.50), channel_id=1, source_target_pairs={{0,16},{1,17},{2,18},{3,19},{4,20},{5,21},{6,22},{7,23},{8,24},{9,... | collective-permute-start | bytes 565256 | tf_op jit(solution)/shard_map/ppermute | solution.py:41
  17.2 9.3 %collective-permute-start.7 = (f32[368,128]{1,0:T(8,128)S(1)}, f32[368,128]{1,0:T(8,128)S(1)}, u32[]{:S(2)}, u32[]{:S(2)}) collective-permute-start(f32[368,128]{1,0:T(8,128)S(1)} %get-tuple-element.51), channel_id=1, source_target_pairs={{0,48},{1,49},{2,50},{3,51},{4,52},{5,53},{6,54},{7,55},{8,56},{9,... | collective-permute-start | bytes 565256 | tf_op jit(solution)/shard_map/ppermute | solution.py:41
  20.4 7.2 %collective-permute-start.8 = (f32[368,128]{1,0:T(8,128)S(1)}, f32[368,128]{1,0:T(8,128)S(1)}, u32[]{:S(2)}, u32[]{:S(2)}) collective-permute-start(f32[368,128]{1,0:T(8,128)S(1)} %get-tuple-element.52), channel_id=1, source_target_pairs={{0,32},{1,33},{2,34},{3,35},{4,36},{5,37},{6,38},{7,39},{8,40},{9,... | collective-permute-start | bytes 565256 | tf_op jit(solution)/shard_map/ppermute | solution.py:41
  20.5 12.3 %collective-permute-start.14 = (f32[352,128]{1,0:T(8,128)S(1)}, f32[352,128]{1,0:T(8,128)S(1)}, u32[]{:S(2)}, u32[]{:S(2)}) collective-permute-start(f32[352,128]{1,0:T(8,128)S(1)} %get-tuple-element.61), channel_id=1, source_target_pairs={{0,16},{1,17},{2,18},{3,19},{4,20},{5,21},{6,22},{7,23},{8,24},{9,... | collective-permute-start | bytes 540680 | tf_op jit(solution)/shard_map/ppermute | solution.py:41
  23.1 9.8 %collective-permute-start.15 = (f32[352,128]{1,0:T(8,128)S(1)}, f32[352,128]{1,0:T(8,128)S(1)}, u32[]{:S(2)}, u32[]{:S(2)}) collective-permute-start(f32[352,128]{1,0:T(8,128)S(1)} %get-tuple-element.62), channel_id=1, source_target_pairs={{0,48},{1,49},{2,50},{3,51},{4,52},{5,53},{6,54},{7,55},{8,56},{9,... | collective-permute-start | bytes 540680 | tf_op jit(solution)/shard_map/ppermute | solution.py:41
  25.2 7.8 %collective-permute-start.16 = (f32[352,128]{1,0:T(8,128)S(1)}, f32[352,128]{1,0:T(8,128)S(1)}, u32[]{:S(2)}, u32[]{:S(2)}) collective-permute-start(f32[352,128]{1,0:T(8,128)S(1)} %get-tuple-element.63), channel_id=1, source_target_pairs={{0,32},{1,33},{2,34},{3,35},{4,36},{5,37},{6,38},{7,39},{8,40},{9,... | collective-permute-start | bytes 540680 | tf_op jit(solution)/shard_map/ppermute | solution.py:41
  28.4 10.1 %collective-permute-start.11 = (f32[256,128]{1,0:T(8,128)S(1)}, f32[256,128]{1,0:T(8,128)S(1)}, u32[]{:S(2)}, u32[]{:S(2)}) collective-permute-start(f32[256,128]{1,0:T(8,128)S(1)} %get-tuple-element.57), channel_id=1, source_target_pairs={{0,128},{1,129},{2,130},{3,131},{4,132},{5,133},{6,134},{7,135},{8... | collective-permute-start | bytes 393224 | tf_op jit(solution)/shard_map/ppermute | solution.py:41
  30.9 7.7 %collective-permute-start.12 = (f32[256,128]{1,0:T(8,128)S(1)}, f32[256,128]{1,0:T(8,128)S(1)}, u32[]{:S(2)}, u32[]{:S(2)}) collective-permute-start(f32[256,128]{1,0:T(8,128)S(1)} %get-tuple-element.58), channel_id=1, source_target_pairs={{0,8},{1,9},{2,10},{3,11},{4,12},{5,13},{6,14},{7,15},{8,128},{9,1... | collective-permute-start | bytes 393224 | tf_op jit(solution)/shard_map/ppermute | solution.py:41
  32.8 5.8 %collective-permute-start.13 = (f32[256,128]{1,0:T(8,128)S(1)}, f32[256,128]{1,0:T(8,128)S(1)}, u32[]{:S(2)}, u32[]{:S(2)}) collective-permute-start(f32[256,128]{1,0:T(8,128)S(1)} %get-tuple-element.59), channel_id=1, source_target_pairs={{0,136},{1,137},{2,138},{3,139},{4,140},{5,141},{6,142},{7,143},{8... | collective-permute-start | bytes 393224 | tf_op jit(solution)/shard_map/ppermute | solution.py:41
  33.7 6.6 %collective-permute-start.17 = (f32[256,128]{1,0:T(8,128)S(1)}, f32[256,128]{1,0:T(8,128)S(1)}, u32[]{:S(2)}, u32[]{:S(2)}) collective-permute-start(f32[256,128]{1,0:T(8,128)S(1)} %get-tuple-element.66), channel_id=1, source_target_pairs={{0,128},{1,129},{2,130},{3,131},{4,132},{5,133},{6,134},{7,135},{8... | collective-permute-start | bytes 393224 | tf_op jit(solution)/shard_map/ppermute | solution.py:41
  35.4 6.7 %collective-permute-start.18 = (f32[256,128]{1,0:T(8,128)S(1)}, f32[256,128]{1,0:T(8,128)S(1)}, u32[]{:S(2)}, u32[]{:S(2)}) collective-permute-start(f32[256,128]{1,0:T(8,128)S(1)} %get-tuple-element.67), channel_id=1, source_target_pairs={{0,8},{1,9},{2,10},{3,11},{4,12},{5,13},{6,14},{7,15},{8,128},{9,1... | collective-permute-start | bytes 393224 | tf_op jit(solution)/shard_map/ppermute | solution.py:41
  38.6 5.0 %collective-permute-start.19 = (f32[256,128]{1,0:T(8,128)S(1)}, f32[256,128]{1,0:T(8,128)S(1)}, u32[]{:S(2)}, u32[]{:S(2)}) collective-permute-start(f32[256,128]{1,0:T(8,128)S(1)} %get-tuple-element.68), channel_id=1, source_target_pairs={{0,136},{1,137},{2,138},{3,139},{4,140},{5,141},{6,142},{7,143},{8... | collective-permute-start | bytes 393224 | tf_op jit(solution)/shard_map/ppermute | solution.py:41

commit v4 on v3

--- a/solution.py
+++ b/solution.py
@@ -18,9 +18,10 @@
 H = 2816
 BLOCK = 88
 OWN = 11
-HALF = BLOCK // 2
-FIRST = 4 * HALF + 8
-SECOND = 4 * HALF
+DEVICES = (4, 8 - 4)
+UNITS = tuple(n * OWN for n in DEVICES)
+FIRST = 4 * UNITS[0] + 8
+SECOND = 4 * UNITS[1]
 PART = FIRST + SECOND
 LANES = 128
 MIB = 1 << 20
@@ -123,8 +124,8 @@
             shift[0:1, cols] = jnp.sum(upstream, axis=0, keepdims=True)
 
 
-def gradient(sums, other, shift, gain, out_grad, gelu, slope, wide, result, keep, cross, *scratch):
-    pre_grad, turned, gains, shifts, sems = scratch
+def gradient(sums, other, shift, gain, out_grad, gelu, slope, wide, pre_grad, keep, cross, *scratch):
+    turned, gains, shifts = scratch
     squares = sums[0:1, :] + other[0:1, :]
     response = sums[1:2, :] + other[1:2, :]
     channel_norm = jnp.sqrt(squares + 1e-06)
@@ -138,18 +139,13 @@
     of_gelu = norm_grad / channel_norm
     gain_term = sums[1:2, :] * scaled
     shift_term = shift[...]
-    copies = []
-    for p, (start, stop) in enumerate(zip(CUTS[:-1], CUTS[1:])):
-        for k in range(start, stop):
-            cols = slice(k * LANES, (k + 1) * LANES)
-            upstream = out_grad[:, cols].astype(jnp.float32)
-            act_grad = upstream * of_upstream[:, cols] + gelu[:, cols] * of_gelu[:, cols]
-            rounded = (act_grad * slope[:, cols]).astype(jnp.bfloat16)
-            pre_grad[:, cols] = rounded
-            turned[cols, :] = rounded.astype(jnp.float32).T
-        cols = pl.ds(start * LANES, (stop - start) * LANES)
-        copies.append(pltpu.make_async_copy(pre_grad.at[:, cols], result.at[:, cols], sems.at[p]))
-        copies[-1].start()
+    for k in range(H // LANES):
+        cols = slice(k * LANES, (k + 1) * LANES)
+        upstream = out_grad[:, cols].astype(jnp.float32)
+        act_grad = upstream * of_upstream[:, cols] + gelu[:, cols] * of_gelu[:, cols]
+        rounded = (act_grad * slope[:, cols]).astype(jnp.bfloat16)
+        pre_grad[:, cols] = rounded
+        turned[cols, :] = rounded.astype(jnp.float32).T
     both = jnp.concatenate([gain_term, shift_term, jnp.zeros((6, H), jnp.float32)], axis=0)
     for b in range(H // BLOCK):
         tile, start = divmod(b * BLOCK, LANES)
@@ -172,12 +168,25 @@
                 b = (block_y // 2) * 16 + to * 8 + block_x * 2 + lax.rem(block_y, 2)
                 start = pl.multiple_of(b * BLOCK, 8)
                 units = turned[pl.ds(start, BLOCK), :]
-                chunk[top + i * HALF : top + (i + 1) * HALF, :] = units[:HALF]
-                chunk[top + FIRST + i * HALF : top + FIRST + (i + 1) * HALF, :] = units[HALF:]
-                row = top + 4 * HALF + i
+                row = top + i * UNITS[0]
+                chunk[row : row + UNITS[0], :] = units[: UNITS[0]]
+                row = top + FIRST + i * UNITS[1]
+                chunk[row : row + UNITS[1], :] = units[UNITS[0] :]
+                row = top + 4 * UNITS[0] + i
                 chunk[row : row + 1, :] = gains[pl.ds(b, 1), :]
                 chunk[row + 4 : row + 5, :] = shifts[pl.ds(b, 1), :]
     cross[4 * PART :, :] = wide[...]
+
+
+def store(value, result, sems):
+    parts = sems.shape[0]
+    rows = ROWS // parts
+    copies = [
+        pltpu.make_async_copy(value.at[pl.ds(p * rows, rows)], result.at[pl.ds(p * rows, rows)], sems.at[p])
+        for p in range(parts)
+    ]
+    for copy in copies:
+        copy.start()
     for copy in copies:
         copy.wait()
 
@@ -191,13 +200,17 @@
             second[n * SECOND : (n + 1) * SECOND, :] = source[middle : middle + SECOND, :]
 
 
-def product(half, here, above, below, opposite, right_first, right_second, right_rest, *rest):
+def product(half, steps, here, *refs):
+    arrived = dict(zip(steps, refs[:3]))
+    above, below, opposite = arrived[1], arrived[-1], arrived[2]
+    (right_first, right_second, right_rest), rest = refs[3:6], refs[6:]
     if half == 0:
         outs, terms, lefts = rest[:4], rest[4], rest[5:]
     else:
         terms, outs, lefts = rest[0], rest[1:5], rest[5:]
     step = FIRST if half == 0 else SECOND
-    one, two = slice(0, 4 * HALF), slice(step, step + 4 * HALF)
+    units = UNITS[half]
+    one, two = slice(0, 4 * units), slice(step, step + 4 * units)
     sources = (
         (here[one, :], above[one, :], below[two, :]),
         (above[two, :], below[one, :]),
@@ -205,13 +218,15 @@
     )
     for left, values in zip(lefts, sources):
         for s, value in enumerate(values):
+            below_it = jnp.zeros((left.shape[0] - 4 * units, ROWS), jnp.float32)
+            value = jnp.concatenate([value, below_it], axis=0) if below_it.size else value
             left[:, s * ROWS : (s + 1) * ROWS] = value.astype(jnp.bfloat16)
     rights = (right_first, right_second, right_rest)
     across_pixels = (((1,), (1,)), ((), ()))
     if half == 0:
         small = jnp.zeros((8, LANES), jnp.float32)
         for pair in (here, above, below, opposite):
-            small = small + (pair[4 * HALF : FIRST, :] + pair[FIRST + 4 * HALF :, :])
+            small = small + (pair[4 * units : FIRST, :] + pair[FIRST + 4 * units :, :])
         terms[...] = small
     else:
         small = terms[...]
@@ -219,15 +234,16 @@
     for left in lefts:
         ones = jnp.ones((8, left.shape[1]), jnp.bfloat16)
         bias = bias + lax.dot_general(ones, left[...], across_pixels, preferred_element_type=jnp.float32)
-    bias = jnp.concatenate([bias, jnp.zeros((8, 3 * LANES - 4 * HALF), jnp.float32)], axis=1)
+    width = (4 * units // LANES + 2) * LANES
+    bias = jnp.concatenate([bias, jnp.zeros((8, width - bias.shape[1]), jnp.float32)], axis=1)
     rows = []
     for i in range(4):
-        tile, start = divmod(i * HALF, LANES)
+        tile, start = divmod(i * units, LANES)
         window = bias[:, tile * LANES : (tile + 2) * LANES]
         rows.append((pltpu.roll(window, 2 * LANES - start, 1) if start else window)[0:1, :LANES])
     bias = jnp.concatenate([*rows, *rows], axis=0)
-    for z in range(4):
-        skip = (4 * half + z) * OWN
+    for z in range(DEVICES[half]):
+        skip = (DEVICES[0] * half + z) * OWN
         turned = pltpu.roll(small, LANES - skip, 1) if skip else small
         turned_bias = pltpu.roll(bias, LANES - z * OWN, 1) if z else bias
         for i, out in enumerate(outs):
@@ -248,8 +264,8 @@
             last = jnp.concatenate([last, jnp.zeros((8, LANES), jnp.float32)], axis=0)
             left_half = lax.broadcasted_iota(jnp.int32, (6, LANES), 1) < 64
         for i, out in enumerate(outs):
-            for z in range(4):
-                unit = i * HALF + z * OWN
+            for z in range(DEVICES[half]):
+                unit = i * units + z * OWN
                 for k in range(2 * group, min(2 * group + 2, 5)):
                     row, col = z * PACKED + k * OWN, (k - 2 * group) * LANES
                     out[row : row + OWN, :] = total[unit : unit + OWN, col : col + LANES]
@@ -266,8 +282,8 @@
 
 
 def add_below(above, a, b, c, d, out):
-    out[:4] = above[...].reshape(4, PACKED, LANES)
-    out[4:] = ((a[...] + b[...]) + (c[...] + d[...])).reshape(4, PACKED, LANES)
+    out[: DEVICES[0]] = above[...].reshape(DEVICES[0], PACKED, LANES)
+    out[DEVICES[0] :] = ((a[...] + b[...]) + (c[...] + d[...])).reshape(DEVICES[1], PACKED, LANES)
 
 
 def finish(parts, weight, gain, shift, bias):
@@ -318,13 +334,10 @@
     pre_grad, keep, cross = call(
         gradient,
         [jax.ShapeDtypeStruct((ROWS, H), bf16), f32(4 * PART, LANES), f32(4 * PART + C, LANES)],
-        out_specs=[pl.BlockSpec(memory_space=pl.ANY)] + [pl.BlockSpec(memory_space=pltpu.VMEM)] * 2,
         scratch=[
-            pltpu.VMEM((ROWS, H), bf16),
             pltpu.VMEM((H, LANES), jnp.float32),
             pltpu.VMEM((H // BLOCK, LANES), jnp.float32),
             pltpu.VMEM((H // BLOCK, LANES), jnp.float32),
-            pltpu.SemaphoreType.DMA((4,)),
         ],
         flops=0,
         moved=6_000_000,
@@ -338,30 +351,40 @@
     far = send(from_below, along(1))
     far_across = send(above_across, along(-1))
     firsts, seconds = list(firsts_and_seconds[:4]), list(firsts_and_seconds[4:])
-    firsts[1], from_above, below_across = lax.optimization_barrier((firsts[1], from_above, below_across))
+    firsts[1], below_across, from_above = lax.optimization_barrier((firsts[1], below_across, from_above))
     right_second = right_of(below_across, from_above, flops=GUIDE)
     right_rest = right_of(arrived, far, far_across, flops=GUIDE)
 
-    def around(own, one, two, three):
-        return own, send(one, along(1)), send(three, along(-1)), send(two, along(2))
-
-    def multiply(half, parts, terms=(), flops=0):
-        outs = [f32(4 * PACKED, LANES)] * 4 + ([f32(8, LANES)] if half == 0 else [])
+    def around(steps, own, *away):
+        return own, *(send(away[(step - 1) % 4], along(step)) for step in steps)
+
+    def multiply(half, steps, parts, terms=(), flops=0):
+        outs = [f32(DEVICES[half] * PACKED, LANES)] * 4 + ([f32(8, LANES)] if half == 0 else [])
         return call(
-            functools.partial(product, half),
+            functools.partial(product, half, steps),
             outs,
-            scratch=[pltpu.VMEM((4 * HALF, n * ROWS), bf16) for n in (3, 2, 3)],
+            scratch=[pltpu.VMEM(((4 * UNITS[half] + 15) // 16 * 16, n * ROWS), bf16) for n in (3, 2, 3)],
             flops=flops,
             moved=4_000_000,
-        )(*parts, right_first, right_second, right_rest, *terms)
-
-    def reduce_beside(own, one, two, three):
-        return own, send(two, beside(2)), send(one, beside(1)), send(three, beside(-1))
-
-    *products, terms = multiply(0, around(*firsts), flops=GUIDE)
-    rows = reduce_beside(*products)
-    rows = call(add, f32(4 * PACKED, LANES), flops=GUIDE//10, moved=700_000)(*rows)
-    others = reduce_beside(*multiply(1, around(*seconds), (terms,), flops=GUIDE))
+        )(*around(steps, *parts), right_first, right_second, right_rest, *terms)
+
+    def reduce_beside(steps, own, *away):
+        return own, *(send(away[(step - 1) % 4], beside(step)) for step in steps)
+
+    *products, terms = multiply(0, (1, -1, 2), firsts, flops=GUIDE)
+    rows = reduce_beside((2, 1, -1), *products)
+    rows = call(add, f32(DEVICES[0] * PACKED, LANES), flops=GUIDE//10, moved=700_000)(*rows)
+    rows, pre_grad = lax.optimization_barrier((rows, pre_grad))
+    pre_grad = call(
+        store,
+        jax.ShapeDtypeStruct((ROWS, H), bf16),
+        scratch=[pltpu.SemaphoreType.DMA((4,))],
+        moved=1_440_000,
+        in_specs=[pl.BlockSpec(memory_space=pltpu.VMEM)],
+        out_specs=pl.BlockSpec(memory_space=pl.ANY),
+    )(pre_grad)
+    rows, pre_grad = lax.optimization_barrier((rows, pre_grad))
+    others = reduce_beside((2, 1, -1), *multiply(1, (1, -1, 2), seconds, (terms,), flops=GUIDE))
     rows = call(add_below, f32(8, PACKED, LANES), moved=1_000_000)(rows, *others)
     rows = lax.all_to_all(rows, "z", 0, 0, tiled=True)
     weight, gain, shift, bias = call(

time: 62.5 us -> 61.9 us (level)
    pallas_call x1, Pallas kernels: 1.77 us -> 0.88 us  [on_device(): call(gradient, [jax.ShapeDtypeStruct((ROWS, H), bf16), f32(4 * PART, LANE...]
    pallas_call x3 -> x4, Pallas kernels: 1.66 us -> 2.54 us  [the longest x2 1.62 us: multiply(): call(functools.partial(product, half, steps), outs, scratch=[pltpu.VMEM((...]
where the time goes in v4:
time: 61.9 us; the launch traced here: 61.7 us
  starting transfers between devices  24.8 us (40%)
  blocking collectives  17.8 us (29%)
  waiting for transfers between devices  10.8 us (17%)
  Pallas kernels  7.47 us (12%)
  between operations  0.75 us (1%)
    ppermute x20, starting transfers between devices, send(): return lax.ppermute(value, AXES, pairs(target))  24.8 us
    all_to_all x1, blocking collectives, on_device(): rows = lax.all_to_all(rows, 'z', 0, 0, tiled=True)  17.8 us
    ppermute x20, waiting for transfers between devices, send(): return lax.ppermute(value, AXES, pairs(target))  10.8 us
    pallas_call x1, Pallas kernels, on_device(): call(statistics, [f32(2, H), f32(1, H), f32(ROWS, H), f32(ROWS, H), jax.S...  2.06 us
    pallas_call x2, Pallas kernels, multiply(): call(functools.partial(product, half, steps), outs, scratch=[pltpu.VMEM((...  1.62 us
  transfers between devices with their start and end apart: 20, of which 8 were waited for; matrix products, arithmetic and copies ran while one was open for 0% of the time, Pallas kernels for 9%

profile of v4, /device:TPU:8, one launch (start us, length us, event | category | flops | bytes accessed | tf_op | source)
XLA Modules:
  0.0 61.7 jit_solution(11073129794579696910)
XLA Ops:
  0.6 1.0 %shard_map.84.wide.refs_0_ = f32[704,128]{1,0:T(8,128)S(1)} custom-call(bf16[704,128]{1,0:T(8,128)(2,1)} %bitcast.4), custom_call_target="tpu_custom_call" | custom-call | bytes 540000 | tf_op jit(solution)/shard_map/pallas_call | solution.py:308
  1.7 1.6 %collective-permute-start.2 = (f32[704,128]{1,0:T(8,128)S(1)}, f32[704,128]{1,0:T(8,128)S(1)}, u32[]{:S(2)}, u32[]{:S(2)}) collective-permute-start(f32[704,128]{1,0:T(8,128)S(1)} %shard_map.84.wide.refs_0_), channel_id=1, source_target_pairs={{0,16},{1,17},{2,18},{3,19},{4,20},{5,21},{6,22},{7,23},{8,24},{9,... | collective-permute-start | bytes 1081352 | tf_op jit(solution)/shard_map/ppermute | solution.py:42
  3.3 2.1 %shard_map.83 = (f32[2,2816]{1,0:T(2,128)S(1)}, f32[1,2816]{1,0:T(1,128)S(1)}, f32[128,2816]{1,0:T(8,128)S(1)}, f32[128,2816]{1,0:T(8,128)S(1)}, bf16[128,2816]{1,0:T(8,128)(2,1)S(1)}) custom-call(bf16[128,2816]{1,0:T(8,128)(2,1)} %pre_gelu_hbm.1, bf16[128,2816]{1,0:T(8,128)(2,1)} %out_grad_hbm.1), custom_call_target="tpu_custom_call" | custom-call | bytes 4400000 | tf_op jit(solution)/shard_map/pallas_call | solution.py:315
  5.3 2.0 %collective-permute-start = (f32[2,2816]{1,0:T(2,128)S(1)}, f32[2,2816]{1,0:T(2,128)S(1)}, u32[]{:S(2)}, u32[]{:S(2)}) collective-permute-start(f32[2,2816]{1,0:T(2,128)S(1)} %get-tuple-element.43.sums), channel_id=1, source_target_pairs={{0,1},{1,0},{2,3},{3,2},{4,5},{5,4},{6,7},{7,6},{8,9},{9,8},{10,11... | collective-permute-start | bytes 67592 | tf_op jit(solution)/shard_map/ppermute | solution.py:42
  7.4 3.2 %collective-permute-start.4 = (f32[704,128]{1,0:T(8,128)S(1)}, f32[704,128]{1,0:T(8,128)S(1)}, u32[]{:S(2)}, u32[]{:S(2)}) collective-permute-start(f32[704,128]{1,0:T(8,128)S(1)} %shard_map.84.wide.refs_0_), channel_id=1, source_target_pairs={{0,72},{1,73},{2,74},{3,75},{4,76},{5,77},{6,78},{7,79},{8,192},{9... | collective-permute-start | bytes 1081352 | tf_op jit(solution)/shard_map/ppermute | solution.py:42
  10.5 0.8 %collective-permute-start.5 = (f32[704,128]{1,0:T(8,128)S(1)}, f32[704,128]{1,0:T(8,128)S(1)}, u32[]{:S(2)}, u32[]{:S(2)}) collective-permute-start(f32[704,128]{1,0:T(8,128)S(1)} %shard_map.84.wide.refs_0_), channel_id=1, source_target_pairs={{0,48},{1,49},{2,50},{3,51},{4,52},{5,53},{6,54},{7,55},{8,56},{9,... | collective-permute-start | bytes 1081352 | tf_op jit(solution)/shard_map/ppermute | solution.py:42
  11.4 0.9 %shard_map.85 = (bf16[128,2816]{1,0:T(8,128)(2,1)S(1)}, f32[1440,128]{1,0:T(8,128)S(1)}, f32[2144,128]{1,0:T(8,128)S(1)}) custom-call(f32[2,2816]{1,0:T(2,128)S(1)} %get-tuple-element.43.sums, f32[2,2816]{1,0:T(2,128)S(1)} %collective-permute-done.other, f32[1,2816]{1,0:T(1,128)S(1)} %get-tuple-element.44.shift, f32[1,2816]{1,0:T(1,128)S(1)} %reshape.22.gain, ...), custom_call_target="tpu_custom_call" | custom-call | bytes 6000000 | tf_op jit(solution)/shard_map/pallas_call | solution.py:334
  12.5 1.7 %collective-permute-start.10 = (f32[704,128]{1,0:T(8,128)S(1)}, f32[704,128]{1,0:T(8,128)S(1)}, u32[]{:S(2)}, u32[]{:S(2)}) collective-permute-start(f32[704,128]{1,0:T(8,128)S(1)} %collective-permute-done.3.refs_2_), channel_id=1, source_target_pairs={{0,48},{1,49},{2,50},{3,51},{4,52},{5,53},{6,54},{7,55},{8,56},{9,... | collective-permute-start | bytes 1081352 | tf_op jit(solution)/shard_map/ppermute | solution.py:42
  16.0 2.0 %collective-permute-done.5.refs_1_ = f32[704,128]{1,0:T(8,128)S(1)} collective-permute-done((f32[704,128]{1,0:T(8,128)S(1)}, f32[704,128]{1,0:T(8,128)S(1)}, u32[]{:S(2)}, u32[]{:S(2)}) %collective-permute-start.5) | collective-permute-done | bytes 360480 | tf_op jit(solution)/shard_map/ppermute | solution.py:42
  18.0 3.2 %collective-permute-start.7 = (f32[368,128]{1,0:T(8,128)S(1)}, f32[368,128]{1,0:T(8,128)S(1)}, u32[]{:S(2)}, u32[]{:S(2)}) collective-permute-start(f32[368,128]{1,0:T(8,128)S(1)} %get-tuple-element.54), channel_id=1, source_target_pairs={{0,48},{1,49},{2,50},{3,51},{4,52},{5,53},{6,54},{7,55},{8,56},{9,... | collective-permute-start | bytes 565256 | tf_op jit(solution)/shard_map/ppermute | solution.py:42
  21.8 1.2 %collective-permute-start.14 = (f32[352,128]{1,0:T(8,128)S(1)}, f32[352,128]{1,0:T(8,128)S(1)}, u32[]{:S(2)}, u32[]{:S(2)}) collective-permute-start(f32[352,128]{1,0:T(8,128)S(1)} %get-tuple-element.69), channel_id=1, source_target_pairs={{0,16},{1,17},{2,18},{3,19},{4,20},{5,21},{6,22},{7,23},{8,24},{9,... | collective-permute-start | bytes 540680 | tf_op jit(solution)/shard_map/ppermute | solution.py:42
  23.0 2.0 %collective-permute-start.15 = (f32[352,128]{1,0:T(8,128)S(1)}, f32[352,128]{1,0:T(8,128)S(1)}, u32[]{:S(2)}, u32[]{:S(2)}) collective-permute-start(f32[352,128]{1,0:T(8,128)S(1)} %get-tuple-element.70), channel_id=1, source_target_pairs={{0,48},{1,49},{2,50},{3,51},{4,52},{5,53},{6,54},{7,55},{8,56},{9,... | collective-permute-start | bytes 540680 | tf_op jit(solution)/shard_map/ppermute | solution.py:42
  25.2 2.1 %collective-permute-start.16 = (f32[352,128]{1,0:T(8,128)S(1)}, f32[352,128]{1,0:T(8,128)S(1)}, u32[]{:S(2)}, u32[]{:S(2)}) collective-permute-start(f32[352,128]{1,0:T(8,128)S(1)} %get-tuple-element.71), channel_id=1, source_target_pairs={{0,32},{1,33},{2,34},{3,35},{4,36},{5,37},{6,38},{7,39},{8,40},{9,... | collective-permute-start | bytes 540680 | tf_op jit(solution)/shard_map/ppermute | solution.py:42
  27.3 1.1 %collective-permute-done.8.refs_2_ = f32[368,128]{1,0:T(8,128)S(1)} collective-permute-done((f32[368,128]{1,0:T(8,128)S(1)}, f32[368,128]{1,0:T(8,128)S(1)}, u32[]{:S(2)}, u32[]{:S(2)}) %collective-permute-start.8) | collective-permute-done | bytes 188448 | tf_op jit(solution)/shard_map/ppermute | solution.py:42
  28.4 0.8 %shard_map.90 = (f32[256,128]{1,0:T(8,128)S(1)}, f32[256,128]{1,0:T(8,128)S(1)}, f32[256,128]{1,0:T(8,128)S(1)}, f32[256,128]{1,0:T(8,128)S(1)}, f32[8,128]{1,0:T(8,128)S(1)}) custom-call(f32[368,128]{1,0:T(8,128)S(1)} %get-tuple-element.51.here, f32[368,128]{1,0:T(8,128)S(1)} %collective-permute-done.6.refs_0_, ...), custom_call_target="tpu_custom_call" | custom-call | flops 20000000000 | bytes 4000000 | tf_op jit(solution)/shard_map/pallas_call | solution.py:363
  29.2 1.3 %collective-permute-start.11 = (f32[256,128]{1,0:T(8,128)S(1)}, f32[256,128]{1,0:T(8,128)S(1)}, u32[]{:S(2)}, u32[]{:S(2)}) collective-permute-start(f32[256,128]{1,0:T(8,128)S(1)} %get-tuple-element.60), channel_id=1, source_target_pairs={{0,128},{1,129},{2,130},{3,131},{4,132},{5,133},{6,134},{7,135},{8... | collective-permute-start | bytes 393224 | tf_op jit(solution)/shard_map/ppermute | solution.py:42
  30.5 1.0 %collective-permute-start.12 = (f32[256,128]{1,0:T(8,128)S(1)}, f32[256,128]{1,0:T(8,128)S(1)}, u32[]{:S(2)}, u32[]{:S(2)}) collective-permute-start(f32[256,128]{1,0:T(8,128)S(1)} %get-tuple-element.61), channel_id=1, source_target_pairs={{0,8},{1,9},{2,10},{3,11},{4,12},{5,13},{6,14},{7,15},{8,128},{9,1... | collective-permute-start | bytes 393224 | tf_op jit(solution)/shard_map/ppermute | solution.py:42
  31.5 1.1 %collective-permute-start.13 = (f32[256,128]{1,0:T(8,128)S(1)}, f32[256,128]{1,0:T(8,128)S(1)}, u32[]{:S(2)}, u32[]{:S(2)}) collective-permute-start(f32[256,128]{1,0:T(8,128)S(1)} %get-tuple-element.62), channel_id=1, source_target_pairs={{0,136},{1,137},{2,138},{3,139},{4,140},{5,141},{6,142},{7,143},{8... | collective-permute-start | bytes 393224 | tf_op jit(solution)/shard_map/ppermute | solution.py:42
  32.6 1.8 %collective-permute-done.16.refs_2_ = f32[352,128]{1,0:T(8,128)S(1)} collective-permute-done((f32[352,128]{1,0:T(8,128)S(1)}, f32[352,128]{1,0:T(8,128)S(1)}, u32[]{:S(2)}, u32[]{:S(2)}) %collective-permute-start.16) | collective-permute-done | bytes 180256 | tf_op jit(solution)/shard_map/ppermute | solution.py:42
  35.8 1.5 %collective-permute-start.18 = (f32[256,128]{1,0:T(8,128)S(1)}, f32[256,128]{1,0:T(8,128)S(1)}, u32[]{:S(2)}, u32[]{:S(2)}) collective-permute-start(f32[256,128]{1,0:T(8,128)S(1)} %get-tuple-element.75), channel_id=1, source_target_pairs={{0,8},{1,9},{2,10},{3,11},{4,12},{5,13},{6,14},{7,15},{8,128},{9,1... | collective-permute-start | bytes 393224 | tf_op jit(solution)/shard_map/ppermute | solution.py:42
  37.9 0.9 %shard_map.92 = bf16[128,2816]{1,0:T(8,128)(2,1)} custom-call(bf16[128,2816]{1,0:T(8,128)(2,1)S(1)} %get-tuple-element.65.value), custom_call_target="tpu_custom_call" | custom-call | bytes 1440000 | tf_op jit(solution)/shard_map/pallas_call | solution.py:378
  38.7 3.1 %collective-permute-done.17.b = f32[256,128]{1,0:T(8,128)S(1)} collective-permute-done((f32[256,128]{1,0:T(8,128)S(1)}, f32[256,128]{1,0:T(8,128)S(1)}, u32[]{:S(2)}, u32[]{:S(2)}) %collective-permute-start.17) | collective-permute-done | bytes 131104 | tf_op jit(solution)/shard_map/ppermute | solution.py:42
  41.8 1.3 %collective-permute-done.19.d = f32[256,128]{1,0:T(8,128)S(1)} collective-permute-done((f32[256,128]{1,0:T(8,128)S(1)}, f32[256,128]{1,0:T(8,128)S(1)}, u32[]{:S(2)}, u32[]{:S(2)}) %collective-permute-start.19) | collective-permute-done | bytes 131104 | tf_op jit(solution)/shard_map/ppermute | solution.py:42
  43.2 17.8 %all_to_all.5.parts = f32[8,64,128]{2,1,0:T(8,128)S(1)} all-to-all(f32[8,64,128]{2,1,0:T(8,128)S(1)} %shard_map.94), channel_id=1, replica_groups=mesh['yh'=2,'core'=2,'x'=4,'yl'=2,'z'=8] {'z'}, dimensions={0} | all-to-all | bytes 524288 | tf_op jit(solution)/shard_map/all_to_all | solution.py:389
  (33 shorter events, 5.5 us)
Async XLA Ops:
  0.6 10.7 %copy-start = (f32[2816]{0:T(1024)S(1)}, f32[2816]{0:T(1024)}, u32[]{:S(2)}) copy-start(f32[2816]{0:T(1024)} %param.7) | copy-start | bytes 33796
  1.6 10.9 %collective-permute-start.3 = (f32[704,128]{1,0:T(8,128)S(1)}, f32[704,128]{1,0:T(8,128)S(1)}, u32[]{:S(2)}, u32[]{:S(2)}) collective-permute-start(f32[704,128]{1,0:T(8,128)S(1)} %shard_map.84.wide.refs_0_), channel_id=1, source_target_pairs={{0,200},{1,201},{2,202},{3,203},{4,204},{5,205},{6,206},{7,207},{8... | collective-permute-start | bytes 1081352 | tf_op jit(solution)/shard_map/ppermute | solution.py:42
  1.7 12.5 %collective-permute-start.2 = (f32[704,128]{1,0:T(8,128)S(1)}, f32[704,128]{1,0:T(8,128)S(1)}, u32[]{:S(2)}, u32[]{:S(2)}) collective-permute-start(f32[704,128]{1,0:T(8,128)S(1)} %shard_map.84.wide.refs_0_), channel_id=1, source_target_pairs={{0,16},{1,17},{2,18},{3,19},{4,20},{5,21},{6,22},{7,23},{8,24},{9,... | collective-permute-start | bytes 1081352 | tf_op jit(solution)/shard_map/ppermute | solution.py:42
  5.3 6.0 %collective-permute-start = (f32[2,2816]{1,0:T(2,128)S(1)}, f32[2,2816]{1,0:T(2,128)S(1)}, u32[]{:S(2)}, u32[]{:S(2)}) collective-permute-start(f32[2,2816]{1,0:T(2,128)S(1)} %get-tuple-element.43.sums), channel_id=1, source_target_pairs={{0,1},{1,0},{2,3},{3,2},{4,5},{5,4},{6,7},{7,6},{8,9},{9,8},{10,11... | collective-permute-start | bytes 67592 | tf_op jit(solution)/shard_map/ppermute | solution.py:42
  7.4 8.7 %collective-permute-start.4 = (f32[704,128]{1,0:T(8,128)S(1)}, f32[704,128]{1,0:T(8,128)S(1)}, u32[]{:S(2)}, u32[]{:S(2)}) collective-permute-start(f32[704,128]{1,0:T(8,128)S(1)} %shard_map.84.wide.refs_0_), channel_id=1, source_target_pairs={{0,72},{1,73},{2,74},{3,75},{4,76},{5,77},{6,78},{7,79},{8,192},{9... | collective-permute-start | bytes 1081352 | tf_op jit(solution)/shard_map/ppermute | solution.py:42
  10.5 7.4 %collective-permute-start.5 = (f32[704,128]{1,0:T(8,128)S(1)}, f32[704,128]{1,0:T(8,128)S(1)}, u32[]{:S(2)}, u32[]{:S(2)}) collective-permute-start(f32[704,128]{1,0:T(8,128)S(1)} %shard_map.84.wide.refs_0_), channel_id=1, source_target_pairs={{0,48},{1,49},{2,50},{3,51},{4,52},{5,53},{6,54},{7,55},{8,56},{9,... | collective-permute-start | bytes 1081352 | tf_op jit(solution)/shard_map/ppermute | solution.py:42
  12.3 2.8 %collective-permute-start.1 = (f32[2144,128]{1,0:T(8,128)S(1)}, f32[2144,128]{1,0:T(8,128)S(1)}, u32[]{:S(2)}, u32[]{:S(2)}) collective-permute-start(f32[2144,128]{1,0:T(8,128)S(1)} %get-tuple-element.49), channel_id=1, source_target_pairs={{0,64},{1,65},{2,66},{3,67},{4,68},{5,69},{6,70},{7,71},{8,72},{9,... | collective-permute-start | bytes 3293192 | tf_op jit(solution)/shard_map/ppermute | solution.py:42
  12.5 9.3 %collective-permute-start.10 = (f32[704,128]{1,0:T(8,128)S(1)}, f32[704,128]{1,0:T(8,128)S(1)}, u32[]{:S(2)}, u32[]{:S(2)}) collective-permute-start(f32[704,128]{1,0:T(8,128)S(1)} %collective-permute-done.3.refs_2_), channel_id=1, source_target_pairs={{0,48},{1,49},{2,50},{3,51},{4,52},{5,53},{6,54},{7,55},{8,56},{9,... | collective-permute-start | bytes 1081352 | tf_op jit(solution)/shard_map/ppermute | solution.py:42
  14.3 8.7 %collective-permute-start.9 = (f32[704,128]{1,0:T(8,128)S(1)}, f32[704,128]{1,0:T(8,128)S(1)}, u32[]{:S(2)}, u32[]{:S(2)}) collective-permute-start(f32[704,128]{1,0:T(8,128)S(1)} %collective-permute-done.2.refs_1_), channel_id=1, source_target_pairs={{0,16},{1,17},{2,18},{3,19},{4,20},{5,21},{6,22},{7,23},{8,24},{9,... | collective-permute-start | bytes 1081352 | tf_op jit(solution)/shard_map/ppermute | solution.py:42
  18.0 7.2 %collective-permute-start.6 = (f32[368,128]{1,0:T(8,128)S(1)}, f32[368,128]{1,0:T(8,128)S(1)}, u32[]{:S(2)}, u32[]{:S(2)}) collective-permute-start(f32[368,128]{1,0:T(8,128)S(1)} %get-tuple-element.53), channel_id=1, source_target_pairs={{0,16},{1,17},{2,18},{3,19},{4,20},{5,21},{6,22},{7,23},{8,24},{9,... | collective-permute-start | bytes 565256 | tf_op jit(solution)/shard_map/ppermute | solution.py:42
  18.0 9.3 %collective-permute-start.7 = (f32[368,128]{1,0:T(8,128)S(1)}, f32[368,128]{1,0:T(8,128)S(1)}, u32[]{:S(2)}, u32[]{:S(2)}) collective-permute-start(f32[368,128]{1,0:T(8,128)S(1)} %get-tuple-element.54), channel_id=1, source_target_pairs={{0,48},{1,49},{2,50},{3,51},{4,52},{5,53},{6,54},{7,55},{8,56},{9,... | collective-permute-start | bytes 565256 | tf_op jit(solution)/shard_map/ppermute | solution.py:42
  21.2 7.2 %collective-permute-start.8 = (f32[368,128]{1,0:T(8,128)S(1)}, f32[368,128]{1,0:T(8,128)S(1)}, u32[]{:S(2)}, u32[]{:S(2)}) collective-permute-start(f32[368,128]{1,0:T(8,128)S(1)} %get-tuple-element.55), channel_id=1, source_target_pairs={{0,32},{1,33},{2,34},{3,35},{4,36},{5,37},{6,38},{7,39},{8,40},{9,... | collective-permute-start | bytes 565256 | tf_op jit(solution)/shard_map/ppermute | solution.py:42
  21.8 9.7 %collective-permute-start.14 = (f32[352,128]{1,0:T(8,128)S(1)}, f32[352,128]{1,0:T(8,128)S(1)}, u32[]{:S(2)}, u32[]{:S(2)}) collective-permute-start(f32[352,128]{1,0:T(8,128)S(1)} %get-tuple-element.69), channel_id=1, source_target_pairs={{0,16},{1,17},{2,18},{3,19},{4,20},{5,21},{6,22},{7,23},{8,24},{9,... | collective-permute-start | bytes 540680 | tf_op jit(solution)/shard_map/ppermute | solution.py:42
  23.0 9.5 %collective-permute-start.15 = (f32[352,128]{1,0:T(8,128)S(1)}, f32[352,128]{1,0:T(8,128)S(1)}, u32[]{:S(2)}, u32[]{:S(2)}) collective-permute-start(f32[352,128]{1,0:T(8,128)S(1)} %get-tuple-element.70), channel_id=1, source_target_pairs={{0,48},{1,49},{2,50},{3,51},{4,52},{5,53},{6,54},{7,55},{8,56},{9,... | collective-permute-start | bytes 540680 | tf_op jit(solution)/shard_map/ppermute | solution.py:42
  25.2 9.2 %collective-permute-start.16 = (f32[352,128]{1,0:T(8,128)S(1)}, f32[352,128]{1,0:T(8,128)S(1)}, u32[]{:S(2)}, u32[]{:S(2)}) collective-permute-start(f32[352,128]{1,0:T(8,128)S(1)} %get-tuple-element.71), channel_id=1, source_target_pairs={{0,32},{1,33},{2,34},{3,35},{4,36},{5,37},{6,38},{7,39},{8,40},{9,... | collective-permute-start | bytes 540680 | tf_op jit(solution)/shard_map/ppermute | solution.py:42
  29.2 8.1 %collective-permute-start.11 = (f32[256,128]{1,0:T(8,128)S(1)}, f32[256,128]{1,0:T(8,128)S(1)}, u32[]{:S(2)}, u32[]{:S(2)}) collective-permute-start(f32[256,128]{1,0:T(8,128)S(1)} %get-tuple-element.60), channel_id=1, source_target_pairs={{0,128},{1,129},{2,130},{3,131},{4,132},{5,133},{6,134},{7,135},{8... | collective-permute-start | bytes 393224 | tf_op jit(solution)/shard_map/ppermute | solution.py:42
  30.5 7.3 %collective-permute-start.12 = (f32[256,128]{1,0:T(8,128)S(1)}, f32[256,128]{1,0:T(8,128)S(1)}, u32[]{:S(2)}, u32[]{:S(2)}) collective-permute-start(f32[256,128]{1,0:T(8,128)S(1)} %get-tuple-element.61), channel_id=1, source_target_pairs={{0,8},{1,9},{2,10},{3,11},{4,12},{5,13},{6,14},{7,15},{8,128},{9,1... | collective-permute-start | bytes 393224 | tf_op jit(solution)/shard_map/ppermute | solution.py:42
  31.5 6.3 %collective-permute-start.13 = (f32[256,128]{1,0:T(8,128)S(1)}, f32[256,128]{1,0:T(8,128)S(1)}, u32[]{:S(2)}, u32[]{:S(2)}) collective-permute-start(f32[256,128]{1,0:T(8,128)S(1)} %get-tuple-element.62), channel_id=1, source_target_pairs={{0,136},{1,137},{2,138},{3,139},{4,140},{5,141},{6,142},{7,143},{8... | collective-permute-start | bytes 393224 | tf_op jit(solution)/shard_map/ppermute | solution.py:42
  35.2 6.6 %collective-permute-start.17 = (f32[256,128]{1,0:T(8,128)S(1)}, f32[256,128]{1,0:T(8,128)S(1)}, u32[]{:S(2)}, u32[]{:S(2)}) collective-permute-start(f32[256,128]{1,0:T(8,128)S(1)} %get-tuple-element.74), channel_id=1, source_target_pairs={{0,128},{1,129},{2,130},{3,131},{4,132},{5,133},{6,134},{7,135},{8... | collective-permute-start | bytes 393224 | tf_op jit(solution)/shard_map/ppermute | solution.py:42
  35.8 6.0 %collective-permute-start.18 = (f32[256,128]{1,0:T(8,128)S(1)}, f32[256,128]{1,0:T(8,128)S(1)}, u32[]{:S(2)}, u32[]{:S(2)}) collective-permute-start(f32[256,128]{1,0:T(8,128)S(1)} %get-tuple-element.75), channel_id=1, source_target_pairs={{0,8},{1,9},{2,10},{3,11},{4,12},{5,13},{6,14},{7,15},{8,128},{9,1... | collective-permute-start | bytes 393224 | tf_op jit(solution)/shard_map/ppermute | solution.py:42
  37.3 5.9 %collective-permute-start.19 = (f32[256,128]{1,0:T(8,128)S(1)}, f32[256,128]{1,0:T(8,128)S(1)}, u32[]{:S(2)}, u32[]{:S(2)}) collective-permute-start(f32[256,128]{1,0:T(8,128)S(1)} %get-tuple-element.76), channel_id=1, source_target_pairs={{0,136},{1,137},{2,138},{3,139},{4,140},{5,141},{6,142},{7,143},{8... | collective-permute-start | bytes 393224 | tf_op jit(solution)/shard_map/ppermute | solution.py:42

commit v5 on v4

--- a/solution.py
+++ b/solution.py
@@ -18,10 +18,9 @@
 H = 2816
 BLOCK = 88
 OWN = 11
-DEVICES = (4, 8 - 4)
-UNITS = tuple(n * OWN for n in DEVICES)
-FIRST = 4 * UNITS[0] + 8
-SECOND = 4 * UNITS[1]
+STEPS = ((1, 2), (3, 0))
+FIRST = len(STEPS[0]) * BLOCK + 8
+SECOND = len(STEPS[1]) * BLOCK
 PART = FIRST + SECOND
 LANES = 128
 MIB = 1 << 20
@@ -168,11 +167,10 @@
                 b = (block_y // 2) * 16 + to * 8 + block_x * 2 + lax.rem(block_y, 2)
                 start = pl.multiple_of(b * BLOCK, 8)
                 units = turned[pl.ds(start, BLOCK), :]
-                row = top + i * UNITS[0]
-                chunk[row : row + UNITS[0], :] = units[: UNITS[0]]
-                row = top + FIRST + i * UNITS[1]
-                chunk[row : row + UNITS[1], :] = units[UNITS[0] :]
-                row = top + 4 * UNITS[0] + i
+                part = 0 if i in STEPS[0] else 1
+                row = top + part * FIRST + STEPS[part].index(i) * BLOCK
+                chunk[row : row + BLOCK, :] = units
+                row = top + FIRST - 8 + i
                 chunk[row : row + 1, :] = gains[pl.ds(b, 1), :]
                 chunk[row + 4 : row + 5, :] = shifts[pl.ds(b, 1), :]
     cross[4 * PART :, :] = wide[...]
@@ -204,13 +202,14 @@
     arrived = dict(zip(steps, refs[:3]))
     above, below, opposite = arrived[1], arrived[-1], arrived[2]
     (right_first, right_second, right_rest), rest = refs[3:6], refs[6:]
+    blocks = STEPS[half]
+    count, height = len(blocks), len(blocks) * BLOCK
     if half == 0:
-        outs, terms, lefts = rest[:4], rest[4], rest[5:]
+        outs, terms, lefts = rest[:count], rest[count], rest[count + 1 :]
     else:
-        terms, outs, lefts = rest[0], rest[1:5], rest[5:]
+        terms, outs, lefts = rest[0], rest[1 : count + 1], rest[count + 1 :]
     step = FIRST if half == 0 else SECOND
-    units = UNITS[half]
-    one, two = slice(0, 4 * units), slice(step, step + 4 * units)
+    one, two = slice(0, height), slice(step, step + height)
     sources = (
         (here[one, :], above[one, :], below[two, :]),
         (above[two, :], below[one, :]),
@@ -218,7 +217,7 @@
     )
     for left, values in zip(lefts, sources):
         for s, value in enumerate(values):
-            below_it = jnp.zeros((left.shape[0] - 4 * units, ROWS), jnp.float32)
+            below_it = jnp.zeros((left.shape[0] - height, ROWS), jnp.float32)
             value = jnp.concatenate([value, below_it], axis=0) if below_it.size else value
             left[:, s * ROWS : (s + 1) * ROWS] = value.astype(jnp.bfloat16)
     rights = (right_first, right_second, right_rest)
@@ -226,7 +225,7 @@
     if half == 0:
         small = jnp.zeros((8, LANES), jnp.float32)
         for pair in (here, above, below, opposite):
-            small = small + (pair[4 * units : FIRST, :] + pair[FIRST + 4 * units :, :])
+            small = small + (pair[height:FIRST, :] + pair[FIRST + height :, :])
         terms[...] = small
     else:
         small = terms[...]
@@ -234,21 +233,19 @@
     for left in lefts:
         ones = jnp.ones((8, left.shape[1]), jnp.bfloat16)
         bias = bias + lax.dot_general(ones, left[...], across_pixels, preferred_element_type=jnp.float32)
-    width = (4 * units // LANES + 2) * LANES
+    width = (height // LANES + 2) * LANES
     bias = jnp.concatenate([bias, jnp.zeros((8, width - bias.shape[1]), jnp.float32)], axis=1)
     rows = []
-    for i in range(4):
-        tile, start = divmod(i * units, LANES)
+    for n in range(count):
+        tile, start = divmod(n * BLOCK, LANES)
         window = bias[:, tile * LANES : (tile + 2) * LANES]
         rows.append((pltpu.roll(window, 2 * LANES - start, 1) if start else window)[0:1, :LANES])
-    bias = jnp.concatenate([*rows, *rows], axis=0)
-    for z in range(DEVICES[half]):
-        skip = (DEVICES[0] * half + z) * OWN
-        turned = pltpu.roll(small, LANES - skip, 1) if skip else small
-        turned_bias = pltpu.roll(bias, LANES - z * OWN, 1) if z else bias
-        for i, out in enumerate(outs):
+    small = jnp.concatenate([small, *rows, *[rows[0]] * (8 - count)], axis=0)
+    for z in range(8):
+        turned = pltpu.roll(small, LANES - z * OWN, 1) if z else small
+        for n, (i, out) in enumerate(zip(blocks, outs)):
             row = z * PACKED + 61
-            out[row : row + 1, :] = turned_bias[i : i + 1, :]
+            out[row : row + 1, :] = turned[8 + n : 9 + n, :]
             out[row + 1 : row + 2, :] = turned[i : i + 1, :]
             out[row + 2 : row + 3, :] = turned[4 + i : 5 + i, :]
     for group in range(3):
@@ -263,9 +260,9 @@
             last = jnp.concatenate([last, last], axis=1)
             last = jnp.concatenate([last, jnp.zeros((8, LANES), jnp.float32)], axis=0)
             left_half = lax.broadcasted_iota(jnp.int32, (6, LANES), 1) < 64
-        for i, out in enumerate(outs):
-            for z in range(DEVICES[half]):
-                unit = i * units + z * OWN
+        for n, out in enumerate(outs):
+            for z in range(8):
+                unit = n * BLOCK + z * OWN
                 for k in range(2 * group, min(2 * group + 2, 5)):
                     row, col = z * PACKED + k * OWN, (k - 2 * group) * LANES
                     out[row : row + OWN, :] = total[unit : unit + OWN, col : col + LANES]
@@ -277,13 +274,12 @@
 PACKED = 64
 
 
-def add(a, b, c, d, out):
-    out[...] = (a[...] + b[...]) + (c[...] + d[...])
-
-
-def add_below(above, a, b, c, d, out):
-    out[: DEVICES[0]] = above[...].reshape(DEVICES[0], PACKED, LANES)
-    out[DEVICES[0] :] = ((a[...] + b[...]) + (c[...] + d[...])).reshape(DEVICES[1], PACKED, LANES)
+def add(*refs):
+    *parts, out = refs
+    total = parts[0][...]
+    for part in parts[1:]:
+        total = total + part[...]
+    out[...] = total
 
 
 def finish(parts, weight, gain, shift, bias):
@@ -359,21 +355,25 @@
         return own, *(send(away[(step - 1) % 4], along(step)) for step in steps)
 
     def multiply(half, steps, parts, terms=(), flops=0):
-        outs = [f32(DEVICES[half] * PACKED, LANES)] * 4 + ([f32(8, LANES)] if half == 0 else [])
+        count = len(STEPS[half])
+        outs = [f32(8 * PACKED, LANES)] * count + ([f32(8, LANES)] if half == 0 else [])
+        height = (count * BLOCK + 15) // 16 * 16
         return call(
             functools.partial(product, half, steps),
             outs,
-            scratch=[pltpu.VMEM(((4 * UNITS[half] + 15) // 16 * 16, n * ROWS), bf16) for n in (3, 2, 3)],
+            scratch=[pltpu.VMEM((height, n * ROWS), bf16) for n in (3, 2, 3)],
             flops=flops,
             moved=4_000_000,
         )(*around(steps, *parts), right_first, right_second, right_rest, *terms)
 
-    def reduce_beside(steps, own, *away):
-        return own, *(send(away[(step - 1) % 4], beside(step)) for step in steps)
+    def reduce_beside(half, products):
+        return [value if i == 0 else send(value, beside(-1 if i == 3 else i)) for i, value in zip(STEPS[half], products)]
+
+    def add_up(*values, flops=0):
+        return call(add, f32(8 * PACKED, LANES), flops=flops, moved=700_000)(*values)
 
     *products, terms = multiply(0, (1, -1, 2), firsts, flops=GUIDE)
-    rows = reduce_beside((2, 1, -1), *products)
-    rows = call(add, f32(DEVICES[0] * PACKED, LANES), flops=GUIDE//10, moved=700_000)(*rows)
+    rows = add_up(*reduce_beside(0, products), flops=GUIDE // 10)
     rows, pre_grad = lax.optimization_barrier((rows, pre_grad))
     pre_grad = call(
         store,
@@ -384,9 +384,9 @@
         out_specs=pl.BlockSpec(memory_space=pl.ANY),
     )(pre_grad)
     rows, pre_grad = lax.optimization_barrier((rows, pre_grad))
-    others = reduce_beside((2, 1, -1), *multiply(1, (1, -1, 2), seconds, (terms,), flops=GUIDE))
-    rows = call(add_below, f32(8, PACKED, LANES), moved=1_000_000)(rows, *others)
-    rows = lax.all_to_all(rows, "z", 0, 0, tiled=True)
+    others = multiply(1, (1, -1, 2), seconds, (terms,), flops=GUIDE)
+    rows = add_up(rows, *reduce_beside(1, others))
+    rows = lax.all_to_all(rows.reshape(8, PACKED, LANES), "z", 0, 0, tiled=True)
     weight, gain, shift, bias = call(
         finish, [f32(OWN, C), f32(1, OWN), f32(1, OWN), f32(1, OWN)], moved=330_000
     )(rows)

time: 61.9 us -> 60.4 us (0.976)
  starting transfers between devices: 24.8 us -> 21.9 us
  waiting for transfers between devices: 10.8 us -> 12.2 us
    ppermute x20 -> x17, starting transfers between devices: 24.8 us -> 21.9 us  [send(): return lax.ppermute(value, AXES, pairs(target))]
    ppermute x20 -> x17, waiting for transfers between devices: 10.8 us -> 12.2 us  [send(): return lax.ppermute(value, AXES, pairs(target))]
  transfers between devices with their start and end apart: 20 -> 17, of which waited for: 8 -> 10; matrix products, arithmetic and copies ran while one was open for 0% -> 0% of each run, Pallas kernels for 9% -> 10%
where the time goes in v5:
time: 60.4 us; the launch traced here: 60.2 us
  starting transfers between devices  21.9 us (36%)
  blocking collectives  17.8 us (29%)
  waiting for transfers between devices  12.2 us (20%)
  Pallas kernels  7.47 us (12%)
  between operations  0.74 us (1%)
    ppermute x17, starting transfers between devices, send(): return lax.ppermute(value, AXES, pairs(target))  21.9 us
    all_to_all x1, blocking collectives, on_device(): rows = lax.all_to_all(rows.reshape(8, PACKED, LANES), 'z', 0, 0, tiled=True)  17.8 us
    ppermute x17, waiting for transfers between devices, send(): return lax.ppermute(value, AXES, pairs(target))  12.2 us
    pallas_call x1, Pallas kernels, on_device(): call(statistics, [f32(2, H), f32(1, H), f32(ROWS, H), f32(ROWS, H), jax.S...  2.06 us
    pallas_call x2, Pallas kernels, multiply(): call(functools.partial(product, half, steps), outs, scratch=[pltpu.VMEM((...  1.61 us
  transfers between devices with their start and end apart: 17, of which 10 were waited for; matrix products, arithmetic and copies ran while one was open for 0% of the time, Pallas kernels for 10%

profile of v5, /device:TPU:8, one launch (start us, length us, event | category | flops | bytes accessed | tf_op | source)
XLA Modules:
  0.0 60.2 jit_solution(11708572701095471075)
XLA Ops:
  0.6 1.0 %shard_map.84.wide.refs_0_ = f32[704,128]{1,0:T(8,128)S(1)} custom-call(bf16[704,128]{1,0:T(8,128)(2,1)} %bitcast.6), custom_call_target="tpu_custom_call" | custom-call | bytes 540000 | tf_op jit(solution)/shard_map/pallas_call | solution.py:304
  1.7 1.6 %collective-permute-start.2 = (f32[704,128]{1,0:T(8,128)S(1)}, f32[704,128]{1,0:T(8,128)S(1)}, u32[]{:S(2)}, u32[]{:S(2)}) collective-permute-start(f32[704,128]{1,0:T(8,128)S(1)} %shard_map.84.wide.refs_0_), channel_id=1, source_target_pairs={{0,16},{1,17},{2,18},{3,19},{4,20},{5,21},{6,22},{7,23},{8,24},{9,... | collective-permute-start | bytes 1081352 | tf_op jit(solution)/shard_map/ppermute | solution.py:41
  3.3 2.1 %shard_map.83 = (f32[2,2816]{1,0:T(2,128)S(1)}, f32[1,2816]{1,0:T(1,128)S(1)}, f32[128,2816]{1,0:T(8,128)S(1)}, f32[128,2816]{1,0:T(8,128)S(1)}, bf16[128,2816]{1,0:T(8,128)(2,1)S(1)}) custom-call(bf16[128,2816]{1,0:T(8,128)(2,1)} %pre_gelu_hbm.1, bf16[128,2816]{1,0:T(8,128)(2,1)} %out_grad_hbm.1), custom_call_target="tpu_custom_call" | custom-call | bytes 4400000 | tf_op jit(solution)/shard_map/pallas_call | solution.py:311
  5.3 2.0 %collective-permute-start = (f32[2,2816]{1,0:T(2,128)S(1)}, f32[2,2816]{1,0:T(2,128)S(1)}, u32[]{:S(2)}, u32[]{:S(2)}) collective-permute-start(f32[2,2816]{1,0:T(2,128)S(1)} %get-tuple-element.39.sums), channel_id=1, source_target_pairs={{0,1},{1,0},{2,3},{3,2},{4,5},{5,4},{6,7},{7,6},{8,9},{9,8},{10,11... | collective-permute-start | bytes 67592 | tf_op jit(solution)/shard_map/ppermute | solution.py:41
  7.4 3.2 %collective-permute-start.4 = (f32[704,128]{1,0:T(8,128)S(1)}, f32[704,128]{1,0:T(8,128)S(1)}, u32[]{:S(2)}, u32[]{:S(2)}) collective-permute-start(f32[704,128]{1,0:T(8,128)S(1)} %shard_map.84.wide.refs_0_), channel_id=1, source_target_pairs={{0,72},{1,73},{2,74},{3,75},{4,76},{5,77},{6,78},{7,79},{8,192},{9... | collective-permute-start | bytes 1081352 | tf_op jit(solution)/shard_map/ppermute | solution.py:41
  10.5 0.8 %collective-permute-start.5 = (f32[704,128]{1,0:T(8,128)S(1)}, f32[704,128]{1,0:T(8,128)S(1)}, u32[]{:S(2)}, u32[]{:S(2)}) collective-permute-start(f32[704,128]{1,0:T(8,128)S(1)} %shard_map.84.wide.refs_0_), channel_id=1, source_target_pairs={{0,48},{1,49},{2,50},{3,51},{4,52},{5,53},{6,54},{7,55},{8,56},{9,... | collective-permute-start | bytes 1081352 | tf_op jit(solution)/shard_map/ppermute | solution.py:41
  11.4 0.9 %shard_map.85 = (bf16[128,2816]{1,0:T(8,128)(2,1)S(1)}, f32[1440,128]{1,0:T(8,128)S(1)}, f32[2144,128]{1,0:T(8,128)S(1)}) custom-call(f32[2,2816]{1,0:T(2,128)S(1)} %get-tuple-element.39.sums, f32[2,2816]{1,0:T(2,128)S(1)} %collective-permute-done.other, f32[1,2816]{1,0:T(1,128)S(1)} %get-tuple-element.40.shift, f32[1,2816]{1,0:T(1,128)S(1)} %reshape.25.gain, ...), custom_call_target="tpu_custom_call" | custom-call | bytes 6000000 | tf_op jit(solution)/shard_map/pallas_call | solution.py:330
  12.5 1.7 %collective-permute-start.10 = (f32[704,128]{1,0:T(8,128)S(1)}, f32[704,128]{1,0:T(8,128)S(1)}, u32[]{:S(2)}, u32[]{:S(2)}) collective-permute-start(f32[704,128]{1,0:T(8,128)S(1)} %collective-permute-done.3.refs_2_), channel_id=1, source_target_pairs={{0,48},{1,49},{2,50},{3,51},{4,52},{5,53},{6,54},{7,55},{8,56},{9,... | collective-permute-start | bytes 1081352 | tf_op jit(solution)/shard_map/ppermute | solution.py:41
  15.2 0.8 %collective-permute-done.4.refs_0_ = f32[704,128]{1,0:T(8,128)S(1)} collective-permute-done((f32[704,128]{1,0:T(8,128)S(1)}, f32[704,128]{1,0:T(8,128)S(1)}, u32[]{:S(2)}, u32[]{:S(2)}) %collective-permute-start.4) | collective-permute-done | bytes 360480 | tf_op jit(solution)/shard_map/ppermute | solution.py:41
  16.0 2.0 %collective-permute-done.5.refs_1_ = f32[704,128]{1,0:T(8,128)S(1)} collective-permute-done((f32[704,128]{1,0:T(8,128)S(1)}, f32[704,128]{1,0:T(8,128)S(1)}, u32[]{:S(2)}, u32[]{:S(2)}) %collective-permute-start.5) | collective-permute-done | bytes 360480 | tf_op jit(solution)/shard_map/ppermute | solution.py:41
  18.0 3.2 %collective-permute-start.7 = (f32[368,128]{1,0:T(8,128)S(1)}, f32[368,128]{1,0:T(8,128)S(1)}, u32[]{:S(2)}, u32[]{:S(2)}) collective-permute-start(f32[368,128]{1,0:T(8,128)S(1)} %get-tuple-element.50), channel_id=1, source_target_pairs={{0,48},{1,49},{2,50},{3,51},{4,52},{5,53},{6,54},{7,55},{8,56},{9,... | collective-permute-start | bytes 565256 | tf_op jit(solution)/shard_map/ppermute | solution.py:41
  21.8 1.2 %collective-permute-start.13 = (f32[352,128]{1,0:T(8,128)S(1)}, f32[352,128]{1,0:T(8,128)S(1)}, u32[]{:S(2)}, u32[]{:S(2)}) collective-permute-start(f32[352,128]{1,0:T(8,128)S(1)} %get-tuple-element.63), channel_id=1, source_target_pairs={{0,16},{1,17},{2,18},{3,19},{4,20},{5,21},{6,22},{7,23},{8,24},{9,... | collective-permute-start | bytes 540680 | tf_op jit(solution)/shard_map/ppermute | solution.py:41
  23.0 2.0 %collective-permute-start.14 = (f32[352,128]{1,0:T(8,128)S(1)}, f32[352,128]{1,0:T(8,128)S(1)}, u32[]{:S(2)}, u32[]{:S(2)}) collective-permute-start(f32[352,128]{1,0:T(8,128)S(1)} %get-tuple-element.64), channel_id=1, source_target_pairs={{0,48},{1,49},{2,50},{3,51},{4,52},{5,53},{6,54},{7,55},{8,56},{9,... | collective-permute-start | bytes 540680 | tf_op jit(solution)/shard_map/ppermute | solution.py:41
  25.2 2.1 %collective-permute-start.15 = (f32[352,128]{1,0:T(8,128)S(1)}, f32[352,128]{1,0:T(8,128)S(1)}, u32[]{:S(2)}, u32[]{:S(2)}) collective-permute-start(f32[352,128]{1,0:T(8,128)S(1)} %get-tuple-element.65), channel_id=1, source_target_pairs={{0,32},{1,33},{2,34},{3,35},{4,36},{5,37},{6,38},{7,39},{8,40},{9,... | collective-permute-start | bytes 540680 | tf_op jit(solution)/shard_map/ppermute | solution.py:41
  27.3 1.1 %collective-permute-done.8.refs_2_ = f32[368,128]{1,0:T(8,128)S(1)} collective-permute-done((f32[368,128]{1,0:T(8,128)S(1)}, f32[368,128]{1,0:T(8,128)S(1)}, u32[]{:S(2)}, u32[]{:S(2)}) %collective-permute-start.8) | collective-permute-done | bytes 188448 | tf_op jit(solution)/shard_map/ppermute | solution.py:41
  28.4 0.8 %shard_map.90 = (f32[512,128]{1,0:T(8,128)S(1)}, f32[512,128]{1,0:T(8,128)S(1)}, f32[8,128]{1,0:T(8,128)S(1)}) custom-call(f32[368,128]{1,0:T(8,128)S(1)} %get-tuple-element.47.here, f32[368,128]{1,0:T(8,128)S(1)} %collective-permute-done.6.refs_0_, f32[368,128]{1,0:T(8,128)S(1)} %collective-permute-done.7.refs_1_, ...), custom_call_target="tpu_custom_call" | custom-call | flops 20000000000 | bytes 4000000 | tf_op jit(solution)/shard_map/pallas_call | solution.py:361
  29.6 2.5 %collective-permute-start.12 = (f32[512,128]{1,0:T(8,128)S(1)}, f32[512,128]{1,0:T(8,128)S(1)}, u32[]{:S(2)}, u32[]{:S(2)}) collective-permute-start(f32[512,128]{1,0:T(8,128)S(1)} %get-tuple-element.56), channel_id=1, source_target_pairs={{0,128},{1,129},{2,130},{3,131},{4,132},{5,133},{6,134},{7,135},{8... | collective-permute-start | bytes 786440 | tf_op jit(solution)/shard_map/ppermute | solution.py:41
  32.1 1.2 %collective-permute-done.14.refs_1_ = f32[352,128]{1,0:T(8,128)S(1)} collective-permute-done((f32[352,128]{1,0:T(8,128)S(1)}, f32[352,128]{1,0:T(8,128)S(1)}, u32[]{:S(2)}, u32[]{:S(2)}) %collective-permute-start.14) | collective-permute-done | bytes 180256 | tf_op jit(solution)/shard_map/ppermute | solution.py:41
  33.3 1.0 %collective-permute-done.15.refs_2_ = f32[352,128]{1,0:T(8,128)S(1)} collective-permute-done((f32[352,128]{1,0:T(8,128)S(1)}, f32[352,128]{1,0:T(8,128)S(1)}, u32[]{:S(2)}, u32[]{:S(2)}) %collective-permute-start.15) | collective-permute-done | bytes 180256 | tf_op jit(solution)/shard_map/ppermute | solution.py:41
  34.4 0.8 %shard_map.93 = (f32[512,128]{1,0:T(8,128)S(1)}, f32[512,128]{1,0:T(8,128)S(1)}) custom-call(f32[352,128]{1,0:T(8,128)S(1)} %get-tuple-element.62.here, f32[352,128]{1,0:T(8,128)S(1)} %collective-permute-done.13.refs_0_, f32[352,128]{1,0:T(8,128)S(1)} %collective-permute-done.14.refs_1_, f32[352,128]{1,0:T(8,128)S(1)} %collective-permute-done.15.refs_2_, ...), custom_call_target="tpu_custom_call" | custom-call | flops 20000000000 | bytes 4000000 | tf_op jit(solution)/shard_map/pallas_call | solution.py:361
  35.7 1.8 %collective-permute-done.12.refs_1_ = f32[512,128]{1,0:T(8,128)S(1)} collective-permute-done((f32[512,128]{1,0:T(8,128)S(1)}, f32[512,128]{1,0:T(8,128)S(1)}, u32[]{:S(2)}, u32[]{:S(2)}) %collective-permute-start.12) | collective-permute-done | bytes 262176 | tf_op jit(solution)/shard_map/ppermute | solution.py:41
  37.5 0.9 %shard_map.92 = bf16[128,2816]{1,0:T(8,128)(2,1)} custom-call(bf16[128,2816]{1,0:T(8,128)(2,1)S(1)} %get-tuple-element.59.value), custom_call_target="tpu_custom_call" | custom-call | bytes 1440000 | tf_op jit(solution)/shard_map/pallas_call | solution.py:378
  38.4 3.2 %collective-permute-done.16.refs_1_ = f32[512,128]{1,0:T(8,128)S(1)} collective-permute-done((f32[512,128]{1,0:T(8,128)S(1)}, f32[512,128]{1,0:T(8,128)S(1)}, u32[]{:S(2)}, u32[]{:S(2)}) %collective-permute-start.16) | collective-permute-done | bytes 262176 | tf_op jit(solution)/shard_map/ppermute | solution.py:41
  41.7 17.8 %all_to_all.5.parts = f32[8,64,128]{2,1,0:T(8,128)S(1)} all-to-all(f32[8,64,128]{2,1,0:T(8,128)S(1)} %bitcast.5), channel_id=1, replica_groups=mesh['yh'=2,'core'=2,'x'=4,'yl'=2,'z'=8] {'z'}, dimensions={0} | all-to-all | bytes 524288 | tf_op jit(solution)/shard_map/all_to_all | solution.py:389
  (27 shorter events, 3.6 us)
Async XLA Ops:
  0.6 10.7 %copy-start = (f32[2816]{0:T(1024)S(1)}, f32[2816]{0:T(1024)}, u32[]{:S(2)}) copy-start(f32[2816]{0:T(1024)} %param.7) | copy-start | bytes 33796
  1.6 10.9 %collective-permute-start.3 = (f32[704,128]{1,0:T(8,128)S(1)}, f32[704,128]{1,0:T(8,128)S(1)}, u32[]{:S(2)}, u32[]{:S(2)}) collective-permute-start(f32[704,128]{1,0:T(8,128)S(1)} %shard_map.84.wide.refs_0_), channel_id=1, source_target_pairs={{0,200},{1,201},{2,202},{3,203},{4,204},{5,205},{6,206},{7,207},{8... | collective-permute-start | bytes 1081352 | tf_op jit(solution)/shard_map/ppermute | solution.py:41
  1.7 12.5 %collective-permute-start.2 = (f32[704,128]{1,0:T(8,128)S(1)}, f32[704,128]{1,0:T(8,128)S(1)}, u32[]{:S(2)}, u32[]{:S(2)}) collective-permute-start(f32[704,128]{1,0:T(8,128)S(1)} %shard_map.84.wide.refs_0_), channel_id=1, source_target_pairs={{0,16},{1,17},{2,18},{3,19},{4,20},{5,21},{6,22},{7,23},{8,24},{9,... | collective-permute-start | bytes 1081352 | tf_op jit(solution)/shard_map/ppermute | solution.py:41
  5.3 6.0 %collective-permute-start = (f32[2,2816]{1,0:T(2,128)S(1)}, f32[2,2816]{1,0:T(2,128)S(1)}, u32[]{:S(2)}, u32[]{:S(2)}) collective-permute-start(f32[2,2816]{1,0:T(2,128)S(1)} %get-tuple-element.39.sums), channel_id=1, source_target_pairs={{0,1},{1,0},{2,3},{3,2},{4,5},{5,4},{6,7},{7,6},{8,9},{9,8},{10,11... | collective-permute-start | bytes 67592 | tf_op jit(solution)/shard_map/ppermute | solution.py:41
  7.4 8.7 %collective-permute-start.4 = (f32[704,128]{1,0:T(8,128)S(1)}, f32[704,128]{1,0:T(8,128)S(1)}, u32[]{:S(2)}, u32[]{:S(2)}) collective-permute-start(f32[704,128]{1,0:T(8,128)S(1)} %shard_map.84.wide.refs_0_), channel_id=1, source_target_pairs={{0,72},{1,73},{2,74},{3,75},{4,76},{5,77},{6,78},{7,79},{8,192},{9... | collective-permute-start | bytes 1081352 | tf_op jit(solution)/shard_map/ppermute | solution.py:41
  10.5 7.4 %collective-permute-start.5 = (f32[704,128]{1,0:T(8,128)S(1)}, f32[704,128]{1,0:T(8,128)S(1)}, u32[]{:S(2)}, u32[]{:S(2)}) collective-permute-start(f32[704,128]{1,0:T(8,128)S(1)} %shard_map.84.wide.refs_0_), channel_id=1, source_target_pairs={{0,48},{1,49},{2,50},{3,51},{4,52},{5,53},{6,54},{7,55},{8,56},{9,... | collective-permute-start | bytes 1081352 | tf_op jit(solution)/shard_map/ppermute | solution.py:41
  12.3 2.8 %collective-permute-start.1 = (f32[2144,128]{1,0:T(8,128)S(1)}, f32[2144,128]{1,0:T(8,128)S(1)}, u32[]{:S(2)}, u32[]{:S(2)}) collective-permute-start(f32[2144,128]{1,0:T(8,128)S(1)} %get-tuple-element.45), channel_id=1, source_target_pairs={{0,64},{1,65},{2,66},{3,67},{4,68},{5,69},{6,70},{7,71},{8,72},{9,... | collective-permute-start | bytes 3293192 | tf_op jit(solution)/shard_map/ppermute | solution.py:41
  12.5 9.4 %collective-permute-start.10 = (f32[704,128]{1,0:T(8,128)S(1)}, f32[704,128]{1,0:T(8,128)S(1)}, u32[]{:S(2)}, u32[]{:S(2)}) collective-permute-start(f32[704,128]{1,0:T(8,128)S(1)} %collective-permute-done.3.refs_2_), channel_id=1, source_target_pairs={{0,48},{1,49},{2,50},{3,51},{4,52},{5,53},{6,54},{7,55},{8,56},{9,... | collective-permute-start | bytes 1081352 | tf_op jit(solution)/shard_map/ppermute | solution.py:41
  14.3 8.7 %collective-permute-start.9 = (f32[704,128]{1,0:T(8,128)S(1)}, f32[704,128]{1,0:T(8,128)S(1)}, u32[]{:S(2)}, u32[]{:S(2)}) collective-permute-start(f32[704,128]{1,0:T(8,128)S(1)} %collective-permute-done.2.refs_1_), channel_id=1, source_target_pairs={{0,16},{1,17},{2,18},{3,19},{4,20},{5,21},{6,22},{7,23},{8,24},{9,... | collective-permute-start | bytes 1081352 | tf_op jit(solution)/shard_map/ppermute | solution.py:41
  18.0 7.2 %collective-permute-start.6 = (f32[368,128]{1,0:T(8,128)S(1)}, f32[368,128]{1,0:T(8,128)S(1)}, u32[]{:S(2)}, u32[]{:S(2)}) collective-permute-start(f32[368,128]{1,0:T(8,128)S(1)} %get-tuple-element.49), channel_id=1, source_target_pairs={{0,16},{1,17},{2,18},{3,19},{4,20},{5,21},{6,22},{7,23},{8,24},{9,... | collective-permute-start | bytes 565256 | tf_op jit(solution)/shard_map/ppermute | solution.py:41
  18.0 9.3 %collective-permute-start.7 = (f32[368,128]{1,0:T(8,128)S(1)}, f32[368,128]{1,0:T(8,128)S(1)}, u32[]{:S(2)}, u32[]{:S(2)}) collective-permute-start(f32[368,128]{1,0:T(8,128)S(1)} %get-tuple-element.50), channel_id=1, source_target_pairs={{0,48},{1,49},{2,50},{3,51},{4,52},{5,53},{6,54},{7,55},{8,56},{9,... | collective-permute-start | bytes 565256 | tf_op jit(solution)/shard_map/ppermute | solution.py:41
  21.2 7.2 %collective-permute-start.8 = (f32[368,128]{1,0:T(8,128)S(1)}, f32[368,128]{1,0:T(8,128)S(1)}, u32[]{:S(2)}, u32[]{:S(2)}) collective-permute-start(f32[368,128]{1,0:T(8,128)S(1)} %get-tuple-element.51), channel_id=1, source_target_pairs={{0,32},{1,33},{2,34},{3,35},{4,36},{5,37},{6,38},{7,39},{8,40},{9,... | collective-permute-start | bytes 565256 | tf_op jit(solution)/shard_map/ppermute | solution.py:41
  21.8 10.3 %collective-permute-start.13 = (f32[352,128]{1,0:T(8,128)S(1)}, f32[352,128]{1,0:T(8,128)S(1)}, u32[]{:S(2)}, u32[]{:S(2)}) collective-permute-start(f32[352,128]{1,0:T(8,128)S(1)} %get-tuple-element.63), channel_id=1, source_target_pairs={{0,16},{1,17},{2,18},{3,19},{4,20},{5,21},{6,22},{7,23},{8,24},{9,... | collective-permute-start | bytes 540680 | tf_op jit(solution)/shard_map/ppermute | solution.py:41
  23.0 10.3 %collective-permute-start.14 = (f32[352,128]{1,0:T(8,128)S(1)}, f32[352,128]{1,0:T(8,128)S(1)}, u32[]{:S(2)}, u32[]{:S(2)}) collective-permute-start(f32[352,128]{1,0:T(8,128)S(1)} %get-tuple-element.64), channel_id=1, source_target_pairs={{0,48},{1,49},{2,50},{3,51},{4,52},{5,53},{6,54},{7,55},{8,56},{9,... | collective-permute-start | bytes 540680 | tf_op jit(solution)/shard_map/ppermute | solution.py:41
  25.2 9.2 %collective-permute-start.15 = (f32[352,128]{1,0:T(8,128)S(1)}, f32[352,128]{1,0:T(8,128)S(1)}, u32[]{:S(2)}, u32[]{:S(2)}) collective-permute-start(f32[352,128]{1,0:T(8,128)S(1)} %get-tuple-element.65), channel_id=1, source_target_pairs={{0,32},{1,33},{2,34},{3,35},{4,36},{5,37},{6,38},{7,39},{8,40},{9,... | collective-permute-start | bytes 540680 | tf_op jit(solution)/shard_map/ppermute | solution.py:41
  29.2 6.4 %collective-permute-start.11 = (f32[512,128]{1,0:T(8,128)S(1)}, f32[512,128]{1,0:T(8,128)S(1)}, u32[]{:S(2)}, u32[]{:S(2)}) collective-permute-start(f32[512,128]{1,0:T(8,128)S(1)} %get-tuple-element.55), channel_id=1, source_target_pairs={{0,8},{1,9},{2,10},{3,11},{4,12},{5,13},{6,14},{7,15},{8,128},{9,1... | collective-permute-start | bytes 786440 | tf_op jit(solution)/shard_map/ppermute | solution.py:41
  29.6 7.9 %collective-permute-start.12 = (f32[512,128]{1,0:T(8,128)S(1)}, f32[512,128]{1,0:T(8,128)S(1)}, u32[]{:S(2)}, u32[]{:S(2)}) collective-permute-start(f32[512,128]{1,0:T(8,128)S(1)} %get-tuple-element.56), channel_id=1, source_target_pairs={{0,128},{1,129},{2,130},{3,131},{4,132},{5,133},{6,134},{7,135},{8... | collective-permute-start | bytes 786440 | tf_op jit(solution)/shard_map/ppermute | solution.py:41
  35.2 6.4 %collective-permute-start.16 = (f32[512,128]{1,0:T(8,128)S(1)}, f32[512,128]{1,0:T(8,128)S(1)}, u32[]{:S(2)}, u32[]{:S(2)}) collective-permute-start(f32[512,128]{1,0:T(8,128)S(1)} %get-tuple-element.67), channel_id=1, source_target_pairs={{0,136},{1,137},{2,138},{3,139},{4,140},{5,141},{6,142},{7,143},{8... | collective-permute-start | bytes 786440 | tf_op jit(solution)/shard_map/ppermute | solution.py:41

commit v6 on v5

--- a/solution.py
+++ b/solution.py
@@ -80,7 +80,7 @@
     *wides, out = refs
     for s, wide in enumerate(wides):
         top = wide.shape[0] - C
-        out[:, s * ROWS : (s + 1) * ROWS] = wide[top:, :].astype(jnp.bfloat16)
+        out[s * ROWS : (s + 1) * ROWS, :] = wide[top:, :].T.astype(jnp.bfloat16)
 
 
 CUTS = (0, 6, 12, 17, 22)
@@ -198,18 +198,19 @@
             second[n * SECOND : (n + 1) * SECOND, :] = source[middle : middle + SECOND, :]
 
 
-def product(half, steps, here, *refs):
+def product(half, blocks, steps, here, *refs):
     arrived = dict(zip(steps, refs[:3]))
     above, below, opposite = arrived[1], arrived[-1], arrived[2]
     (right_first, right_second, right_rest), rest = refs[3:6], refs[6:]
-    blocks = STEPS[half]
+    first = half == 0 and blocks[0] == STEPS[0][0]
     count, height = len(blocks), len(blocks) * BLOCK
-    if half == 0:
+    if first:
         outs, terms, lefts = rest[:count], rest[count], rest[count + 1 :]
     else:
         terms, outs, lefts = rest[0], rest[1 : count + 1], rest[count + 1 :]
     step = FIRST if half == 0 else SECOND
-    one, two = slice(0, height), slice(step, step + height)
+    top = STEPS[half].index(blocks[0]) * BLOCK
+    one, two = slice(top, top + height), slice(step + top, step + top + height)
     sources = (
         (here[one, :], above[one, :], below[two, :]),
         (above[two, :], below[one, :]),
@@ -222,10 +223,10 @@
             left[:, s * ROWS : (s + 1) * ROWS] = value.astype(jnp.bfloat16)
     rights = (right_first, right_second, right_rest)
     across_pixels = (((1,), (1,)), ((), ()))
-    if half == 0:
+    if first:
         small = jnp.zeros((8, LANES), jnp.float32)
         for pair in (here, above, below, opposite):
-            small = small + (pair[height:FIRST, :] + pair[FIRST + height :, :])
+            small = small + (pair[FIRST - 8 : FIRST, :] + pair[2 * FIRST - 8 :, :])
         terms[...] = small
     else:
         small = terms[...]
@@ -253,7 +254,7 @@
         total = 0.0
         for left, right in zip(lefts, rights):
             total = total + lax.dot_general(
-                left[...], right[cols, :], across_pixels, preferred_element_type=jnp.float32
+                left[...], right[:, cols], (((1,), (0,)), ((), ())), preferred_element_type=jnp.float32
             )
         if group == 2:
             last = total[:, LANES:]
@@ -324,7 +325,7 @@
     above_across = send(wide, across(-1))
 
     def right_of(*wides, flops=GUIDE):
-        shape = jax.ShapeDtypeStruct((C, len(wides) * ROWS), bf16)
+        shape = jax.ShapeDtypeStruct((len(wides) * ROWS, C), bf16)
         return call(narrow, shape, flops=flops, moved=4_400_000)(*wides)
 
     pre_grad, keep, cross = call(
@@ -354,17 +355,17 @@
     def around(steps, own, *away):
         return own, *(send(away[(step - 1) % 4], along(step)) for step in steps)
 
-    def multiply(half, steps, parts, terms=(), flops=0):
-        count = len(STEPS[half])
-        outs = [f32(8 * PACKED, LANES)] * count + ([f32(8, LANES)] if half == 0 else [])
+    def multiply(half, blocks, steps, parts, terms=(), flops=0):
+        count = len(blocks)
+        outs = [f32(8 * PACKED, LANES)] * count + ([] if terms else [f32(8, LANES)])
         height = (count * BLOCK + 15) // 16 * 16
         return call(
-            functools.partial(product, half, steps),
+            functools.partial(product, half, blocks, steps),
             outs,
             scratch=[pltpu.VMEM((height, n * ROWS), bf16) for n in (3, 2, 3)],
             flops=flops,
             moved=4_000_000,
-        )(*around(steps, *parts), right_first, right_second, right_rest, *terms)
+        )(*parts, right_first, right_second, right_rest, *terms)
 
     def reduce_beside(half, products):
         return [value if i == 0 else send(value, beside(-1 if i == 3 else i)) for i, value in zip(STEPS[half], products)]
@@ -372,7 +373,10 @@
     def add_up(*values, flops=0):
         return call(add, f32(8 * PACKED, LANES), flops=flops, moved=700_000)(*values)
 
-    *products, terms = multiply(0, (1, -1, 2), firsts, flops=GUIDE)
+    steps = (1, -1, 2)
+    parts = around(steps, *firsts)
+    one, terms = multiply(0, STEPS[0][:1], steps, parts, flops=GUIDE)
+    products = [one, *multiply(0, STEPS[0][1:], steps, parts, (terms,), flops=GUIDE)]
     rows = add_up(*reduce_beside(0, products), flops=GUIDE // 10)
     rows, pre_grad = lax.optimization_barrier((rows, pre_grad))
     pre_grad = call(
@@ -384,7 +388,9 @@
         out_specs=pl.BlockSpec(memory_space=pl.ANY),
     )(pre_grad)
     rows, pre_grad = lax.optimization_barrier((rows, pre_grad))
-    others = multiply(1, (1, -1, 2), seconds, (terms,), flops=GUIDE)
+    parts = around(steps, *seconds)
+    others = multiply(1, STEPS[1][:1], steps, parts, (terms,), flops=GUIDE)
+    others = [*others, *multiply(1, STEPS[1][1:], steps, parts, (terms,), flops=0)]
     rows = add_up(rows, *reduce_beside(1, others))
     rows = lax.all_to_all(rows.reshape(8, PACKED, LANES), "z", 0, 0, tiled=True)
     weight, gain, shift, bias = call(

time: 60.4 us -> 60.4 us (level)
  Pallas kernels: 7.47 us -> 8.47 us
    ppermute x17, starting transfers between devices: 21.9 us -> 21.3 us  [send(): return lax.ppermute(value, AXES, pairs(target))]
    pallas_call x2 -> x4, Pallas kernels: 1.61 us -> 2.14 us  [multiply(): call(functools.partial(product, half, blocks, steps), outs, scratch=[pltp...]
  transfers between devices with their start and end apart: 17 -> 17, of which waited for: 10 -> 10; matrix products, arithmetic and copies ran while one was open for 0% -> 0% of each run, Pallas kernels for 10% -> 11%
where the time goes in v6:
time: 60.4 us; the launch traced here: 60.2 us
  starting transfers between devices  21.3 us (35%)
  blocking collectives  17.8 us (29%)
  waiting for transfers between devices  11.8 us (20%)
  Pallas kernels  8.47 us (14%)
  between operations  0.77 us (1%)
    ppermute x17, starting transfers between devices, send(): return lax.ppermute(value, AXES, pairs(target))  21.3 us
    all_to_all x1, blocking collectives, on_device(): rows = lax.all_to_all(rows.reshape(8, PACKED, LANES), 'z', 0, 0, tiled=True)  17.8 us
    ppermute x17, waiting for transfers between devices, send(): return lax.ppermute(value, AXES, pairs(target))  11.8 us
    pallas_call x4, Pallas kernels, multiply(): call(functools.partial(product, half, blocks, steps), outs, scratch=[pltp...  2.14 us
    pallas_call x1, Pallas kernels, on_device(): call(statistics, [f32(2, H), f32(1, H), f32(ROWS, H), f32(ROWS, H), jax.S...  2.06 us
  transfers between devices with their start and end apart: 17, of which 10 were waited for; matrix products, arithmetic and copies ran while one was open for 0% of the time, Pallas kernels for 11%

profile of v6, /device:TPU:8, one launch (start us, length us, event | category | flops | bytes accessed | tf_op | source)
XLA Modules:
  0.0 60.2 jit_solution(17787609687221229711)
XLA Ops:
  0.6 1.0 %shard_map.84.wide.refs_0_ = f32[704,128]{1,0:T(8,128)S(1)} custom-call(bf16[704,128]{1,0:T(8,128)(2,1)} %bitcast.6), custom_call_target="tpu_custom_call" | custom-call | bytes 540000 | tf_op jit(solution)/shard_map/pallas_call | solution.py:305
  1.7 1.6 %collective-permute-start.2 = (f32[704,128]{1,0:T(8,128)S(1)}, f32[704,128]{1,0:T(8,128)S(1)}, u32[]{:S(2)}, u32[]{:S(2)}) collective-permute-start(f32[704,128]{1,0:T(8,128)S(1)} %shard_map.84.wide.refs_0_), channel_id=1, source_target_pairs={{0,16},{1,17},{2,18},{3,19},{4,20},{5,21},{6,22},{7,23},{8,24},{9,... | collective-permute-start | bytes 1081352 | tf_op jit(solution)/shard_map/ppermute | solution.py:41
  3.3 2.1 %shard_map.83 = (f32[2,2816]{1,0:T(2,128)S(1)}, f32[1,2816]{1,0:T(1,128)S(1)}, f32[128,2816]{1,0:T(8,128)S(1)}, f32[128,2816]{1,0:T(8,128)S(1)}, bf16[128,2816]{1,0:T(8,128)(2,1)S(1)}) custom-call(bf16[128,2816]{1,0:T(8,128)(2,1)} %pre_gelu_hbm.1, bf16[128,2816]{1,0:T(8,128)(2,1)} %out_grad_hbm.1), custom_call_target="tpu_custom_call" | custom-call | bytes 4400000 | tf_op jit(solution)/shard_map/pallas_call | solution.py:312
  5.3 2.0 %collective-permute-start = (f32[2,2816]{1,0:T(2,128)S(1)}, f32[2,2816]{1,0:T(2,128)S(1)}, u32[]{:S(2)}, u32[]{:S(2)}) collective-permute-start(f32[2,2816]{1,0:T(2,128)S(1)} %get-tuple-element.36.sums), channel_id=1, source_target_pairs={{0,1},{1,0},{2,3},{3,2},{4,5},{5,4},{6,7},{7,6},{8,9},{9,8},{10,11... | collective-permute-start | bytes 67592 | tf_op jit(solution)/shard_map/ppermute | solution.py:41
  7.4 3.2 %collective-permute-start.4 = (f32[704,128]{1,0:T(8,128)S(1)}, f32[704,128]{1,0:T(8,128)S(1)}, u32[]{:S(2)}, u32[]{:S(2)}) collective-permute-start(f32[704,128]{1,0:T(8,128)S(1)} %shard_map.84.wide.refs_0_), channel_id=1, source_target_pairs={{0,72},{1,73},{2,74},{3,75},{4,76},{5,77},{6,78},{7,79},{8,192},{9... | collective-permute-start | bytes 1081352 | tf_op jit(solution)/shard_map/ppermute | solution.py:41
  10.5 0.8 %collective-permute-start.5 = (f32[704,128]{1,0:T(8,128)S(1)}, f32[704,128]{1,0:T(8,128)S(1)}, u32[]{:S(2)}, u32[]{:S(2)}) collective-permute-start(f32[704,128]{1,0:T(8,128)S(1)} %shard_map.84.wide.refs_0_), channel_id=1, source_target_pairs={{0,48},{1,49},{2,50},{3,51},{4,52},{5,53},{6,54},{7,55},{8,56},{9,... | collective-permute-start | bytes 1081352 | tf_op jit(solution)/shard_map/ppermute | solution.py:41
  11.4 0.9 %shard_map.85 = (bf16[128,2816]{1,0:T(8,128)(2,1)S(1)}, f32[1440,128]{1,0:T(8,128)S(1)}, f32[2144,128]{1,0:T(8,128)S(1)}) custom-call(f32[2,2816]{1,0:T(2,128)S(1)} %get-tuple-element.36.sums, f32[2,2816]{1,0:T(2,128)S(1)} %collective-permute-done.other, f32[1,2816]{1,0:T(1,128)S(1)} %get-tuple-element.37.shift, f32[1,2816]{1,0:T(1,128)S(1)} %reshape.25.gain, ...), custom_call_target="tpu_custom_call" | custom-call | bytes 6000000 | tf_op jit(solution)/shard_map/pallas_call | solution.py:331
  12.5 1.7 %collective-permute-start.10 = (f32[704,128]{1,0:T(8,128)S(1)}, f32[704,128]{1,0:T(8,128)S(1)}, u32[]{:S(2)}, u32[]{:S(2)}) collective-permute-start(f32[704,128]{1,0:T(8,128)S(1)} %collective-permute-done.3.refs_2_), channel_id=1, source_target_pairs={{0,48},{1,49},{2,50},{3,51},{4,52},{5,53},{6,54},{7,55},{8,56},{9,... | collective-permute-start | bytes 1081352 | tf_op jit(solution)/shard_map/ppermute | solution.py:41
  15.8 2.1 %collective-permute-done.5.refs_1_ = f32[704,128]{1,0:T(8,128)S(1)} collective-permute-done((f32[704,128]{1,0:T(8,128)S(1)}, f32[704,128]{1,0:T(8,128)S(1)}, u32[]{:S(2)}, u32[]{:S(2)}) %collective-permute-start.5) | collective-permute-done | bytes 360480 | tf_op jit(solution)/shard_map/ppermute | solution.py:41
  18.0 3.2 %collective-permute-start.7 = (f32[368,128]{1,0:T(8,128)S(1)}, f32[368,128]{1,0:T(8,128)S(1)}, u32[]{:S(2)}, u32[]{:S(2)}) collective-permute-start(f32[368,128]{1,0:T(8,128)S(1)} %get-tuple-element.47), channel_id=1, source_target_pairs={{0,48},{1,49},{2,50},{3,51},{4,52},{5,53},{6,54},{7,55},{8,56},{9,... | collective-permute-start | bytes 565256 | tf_op jit(solution)/shard_map/ppermute | solution.py:41
  21.8 1.3 %collective-permute-start.13 = (f32[352,128]{1,0:T(8,128)S(1)}, f32[352,128]{1,0:T(8,128)S(1)}, u32[]{:S(2)}, u32[]{:S(2)}) collective-permute-start(f32[352,128]{1,0:T(8,128)S(1)} %get-tuple-element.60), channel_id=1, source_target_pairs={{0,16},{1,17},{2,18},{3,19},{4,20},{5,21},{6,22},{7,23},{8,24},{9,... | collective-permute-start | bytes 540680 | tf_op jit(solution)/shard_map/ppermute | solution.py:41
  23.2 1.9 %collective-permute-start.14 = (f32[352,128]{1,0:T(8,128)S(1)}, f32[352,128]{1,0:T(8,128)S(1)}, u32[]{:S(2)}, u32[]{:S(2)}) collective-permute-start(f32[352,128]{1,0:T(8,128)S(1)} %get-tuple-element.61), channel_id=1, source_target_pairs={{0,48},{1,49},{2,50},{3,51},{4,52},{5,53},{6,54},{7,55},{8,56},{9,... | collective-permute-start | bytes 540680 | tf_op jit(solution)/shard_map/ppermute | solution.py:41
  25.3 2.2 %collective-permute-start.15 = (f32[352,128]{1,0:T(8,128)S(1)}, f32[352,128]{1,0:T(8,128)S(1)}, u32[]{:S(2)}, u32[]{:S(2)}) collective-permute-start(f32[352,128]{1,0:T(8,128)S(1)} %get-tuple-element.62), channel_id=1, source_target_pairs={{0,32},{1,33},{2,34},{3,35},{4,36},{5,37},{6,38},{7,39},{8,40},{9,... | collective-permute-start | bytes 540680 | tf_op jit(solution)/shard_map/ppermute | solution.py:41
  27.6 0.8 %collective-permute-done.8.refs_2_ = f32[368,128]{1,0:T(8,128)S(1)} collective-permute-done((f32[368,128]{1,0:T(8,128)S(1)}, f32[368,128]{1,0:T(8,128)S(1)}, u32[]{:S(2)}, u32[]{:S(2)}) %collective-permute-start.8) | collective-permute-done | bytes 188448 | tf_op jit(solution)/shard_map/ppermute | solution.py:41
  29.5 1.3 %collective-permute-start.12 = (f32[512,128]{1,0:T(8,128)S(1)}, f32[512,128]{1,0:T(8,128)S(1)}, u32[]{:S(2)}, u32[]{:S(2)}) collective-permute-start(f32[512,128]{1,0:T(8,128)S(1)} %shard_map.91), channel_id=1, source_target_pairs={{0,128},{1,129},{2,130},{3,131},{4,132},{5,133},{6,134},{7,135},{8... | collective-permute-start | bytes 786440 | tf_op jit(solution)/shard_map/ppermute | solution.py:41
  30.8 1.0 %collective-permute-start.11 = (f32[512,128]{1,0:T(8,128)S(1)}, f32[512,128]{1,0:T(8,128)S(1)}, u32[]{:S(2)}, u32[]{:S(2)}) collective-permute-start(f32[512,128]{1,0:T(8,128)S(1)} %get-tuple-element.52), channel_id=1, source_target_pairs={{0,8},{1,9},{2,10},{3,11},{4,12},{5,13},{6,14},{7,15},{8,128},{9,1... | collective-permute-start | bytes 786440 | tf_op jit(solution)/shard_map/ppermute | solution.py:41
  31.8 1.4 %collective-permute-done.14.refs_1_ = f32[352,128]{1,0:T(8,128)S(1)} collective-permute-done((f32[352,128]{1,0:T(8,128)S(1)}, f32[352,128]{1,0:T(8,128)S(1)}, u32[]{:S(2)}, u32[]{:S(2)}) %collective-permute-start.14) | collective-permute-done | bytes 180256 | tf_op jit(solution)/shard_map/ppermute | solution.py:41
  33.1 1.5 %collective-permute-done.15.refs_2_ = f32[352,128]{1,0:T(8,128)S(1)} collective-permute-done((f32[352,128]{1,0:T(8,128)S(1)}, f32[352,128]{1,0:T(8,128)S(1)}, u32[]{:S(2)}, u32[]{:S(2)}) %collective-permute-start.15) | collective-permute-done | bytes 180256 | tf_op jit(solution)/shard_map/ppermute | solution.py:41
  35.8 1.6 %collective-permute-done.12.refs_1_ = f32[512,128]{1,0:T(8,128)S(1)} collective-permute-done((f32[512,128]{1,0:T(8,128)S(1)}, f32[512,128]{1,0:T(8,128)S(1)}, u32[]{:S(2)}, u32[]{:S(2)}) %collective-permute-start.12) | collective-permute-done | bytes 262176 | tf_op jit(solution)/shard_map/ppermute | solution.py:41
  37.4 1.7 %collective-permute-done.11.refs_0_ = f32[512,128]{1,0:T(8,128)S(1)} collective-permute-done((f32[512,128]{1,0:T(8,128)S(1)}, f32[512,128]{1,0:T(8,128)S(1)}, u32[]{:S(2)}, u32[]{:S(2)}) %collective-permute-start.11) | collective-permute-done | bytes 262176 | tf_op jit(solution)/shard_map/ppermute | solution.py:41
  39.2 0.9 %shard_map.93 = bf16[128,2816]{1,0:T(8,128)(2,1)} custom-call(bf16[128,2816]{1,0:T(8,128)(2,1)S(1)} %get-tuple-element.56.value), custom_call_target="tpu_custom_call" | custom-call | bytes 1440000 | tf_op jit(solution)/shard_map/pallas_call | solution.py:382
  40.1 1.6 %collective-permute-done.16.refs_1_ = f32[512,128]{1,0:T(8,128)S(1)} collective-permute-done((f32[512,128]{1,0:T(8,128)S(1)}, f32[512,128]{1,0:T(8,128)S(1)}, u32[]{:S(2)}, u32[]{:S(2)}) %collective-permute-start.16) | collective-permute-done | bytes 262176 | tf_op jit(solution)/shard_map/ppermute | solution.py:41
  41.7 17.8 %all_to_all.5.parts = f32[8,64,128]{2,1,0:T(8,128)S(1)} all-to-all(f32[8,64,128]{2,1,0:T(8,128)S(1)} %bitcast.5), channel_id=1, replica_groups=mesh['yh'=2,'core'=2,'x'=4,'yl'=2,'z'=8] {'z'}, dimensions={0} | all-to-all | bytes 524288 | tf_op jit(solution)/shard_map/all_to_all | solution.py:395
  59.5 0.7 %shard_map.97 = (f32[11,704]{1,0:T(8,128)}, f32[1,11]{1,0:T(1,128)}, f32[1,11]{1,0:T(1,128)}, f32[1,11]{1,0:T(1,128)}) custom-call(f32[8,64,128]{2,1,0:T(8,128)S(1)} %all_to_all.5.parts), custom_call_target="tpu_custom_call" | custom-call | bytes 330000 | tf_op jit(solution)/shard_map/pallas_call | solution.py:396
  (29 shorter events, 5.1 us)
Async XLA Ops:
  0.6 10.7 %copy-start = (f32[2816]{0:T(1024)S(1)}, f32[2816]{0:T(1024)}, u32[]{:S(2)}) copy-start(f32[2816]{0:T(1024)} %param.7) | copy-start | bytes 33796
  1.6 10.9 %collective-permute-start.3 = (f32[704,128]{1,0:T(8,128)S(1)}, f32[704,128]{1,0:T(8,128)S(1)}, u32[]{:S(2)}, u32[]{:S(2)}) collective-permute-start(f32[704,128]{1,0:T(8,128)S(1)} %shard_map.84.wide.refs_0_), channel_id=1, source_target_pairs={{0,200},{1,201},{2,202},{3,203},{4,204},{5,205},{6,206},{7,207},{8... | collective-permute-start | bytes 1081352 | tf_op jit(solution)/shard_map/ppermute | solution.py:41
  1.7 12.5 %collective-permute-start.2 = (f32[704,128]{1,0:T(8,128)S(1)}, f32[704,128]{1,0:T(8,128)S(1)}, u32[]{:S(2)}, u32[]{:S(2)}) collective-permute-start(f32[704,128]{1,0:T(8,128)S(1)} %shard_map.84.wide.refs_0_), channel_id=1, source_target_pairs={{0,16},{1,17},{2,18},{3,19},{4,20},{5,21},{6,22},{7,23},{8,24},{9,... | collective-permute-start | bytes 1081352 | tf_op jit(solution)/shard_map/ppermute | solution.py:41
  5.3 6.0 %collective-permute-start = (f32[2,2816]{1,0:T(2,128)S(1)}, f32[2,2816]{1,0:T(2,128)S(1)}, u32[]{:S(2)}, u32[]{:S(2)}) collective-permute-start(f32[2,2816]{1,0:T(2,128)S(1)} %get-tuple-element.36.sums), channel_id=1, source_target_pairs={{0,1},{1,0},{2,3},{3,2},{4,5},{5,4},{6,7},{7,6},{8,9},{9,8},{10,11... | collective-permute-start | bytes 67592 | tf_op jit(solution)/shard_map/ppermute | solution.py:41
  7.4 8.5 %collective-permute-start.4 = (f32[704,128]{1,0:T(8,128)S(1)}, f32[704,128]{1,0:T(8,128)S(1)}, u32[]{:S(2)}, u32[]{:S(2)}) collective-permute-start(f32[704,128]{1,0:T(8,128)S(1)} %shard_map.84.wide.refs_0_), channel_id=1, source_target_pairs={{0,72},{1,73},{2,74},{3,75},{4,76},{5,77},{6,78},{7,79},{8,192},{9... | collective-permute-start | bytes 1081352 | tf_op jit(solution)/shard_map/ppermute | solution.py:41
  10.5 7.4 %collective-permute-start.5 = (f32[704,128]{1,0:T(8,128)S(1)}, f32[704,128]{1,0:T(8,128)S(1)}, u32[]{:S(2)}, u32[]{:S(2)}) collective-permute-start(f32[704,128]{1,0:T(8,128)S(1)} %shard_map.84.wide.refs_0_), channel_id=1, source_target_pairs={{0,48},{1,49},{2,50},{3,51},{4,52},{5,53},{6,54},{7,55},{8,56},{9,... | collective-permute-start | bytes 1081352 | tf_op jit(solution)/shard_map/ppermute | solution.py:41
  12.3 2.8 %collective-permute-start.1 = (f32[2144,128]{1,0:T(8,128)S(1)}, f32[2144,128]{1,0:T(8,128)S(1)}, u32[]{:S(2)}, u32[]{:S(2)}) collective-permute-start(f32[2144,128]{1,0:T(8,128)S(1)} %get-tuple-element.42), channel_id=1, source_target_pairs={{0,64},{1,65},{2,66},{3,67},{4,68},{5,69},{6,70},{7,71},{8,72},{9,... | collective-permute-start | bytes 3293192 | tf_op jit(solution)/shard_map/ppermute | solution.py:41
  12.5 9.4 %collective-permute-start.10 = (f32[704,128]{1,0:T(8,128)S(1)}, f32[704,128]{1,0:T(8,128)S(1)}, u32[]{:S(2)}, u32[]{:S(2)}) collective-permute-start(f32[704,128]{1,0:T(8,128)S(1)} %collective-permute-done.3.refs_2_), channel_id=1, source_target_pairs={{0,48},{1,49},{2,50},{3,51},{4,52},{5,53},{6,54},{7,55},{8,56},{9,... | collective-permute-start | bytes 1081352 | tf_op jit(solution)/shard_map/ppermute | solution.py:41
  14.5 8.7 %collective-permute-start.9 = (f32[704,128]{1,0:T(8,128)S(1)}, f32[704,128]{1,0:T(8,128)S(1)}, u32[]{:S(2)}, u32[]{:S(2)}) collective-permute-start(f32[704,128]{1,0:T(8,128)S(1)} %collective-permute-done.2.refs_1_), channel_id=1, source_target_pairs={{0,16},{1,17},{2,18},{3,19},{4,20},{5,21},{6,22},{7,23},{8,24},{9,... | collective-permute-start | bytes 1081352 | tf_op jit(solution)/shard_map/ppermute | solution.py:41
  18.0 7.4 %collective-permute-start.6 = (f32[368,128]{1,0:T(8,128)S(1)}, f32[368,128]{1,0:T(8,128)S(1)}, u32[]{:S(2)}, u32[]{:S(2)}) collective-permute-start(f32[368,128]{1,0:T(8,128)S(1)} %get-tuple-element.46), channel_id=1, source_target_pairs={{0,16},{1,17},{2,18},{3,19},{4,20},{5,21},{6,22},{7,23},{8,24},{9,... | collective-permute-start | bytes 565256 | tf_op jit(solution)/shard_map/ppermute | solution.py:41
  18.0 9.6 %collective-permute-start.7 = (f32[368,128]{1,0:T(8,128)S(1)}, f32[368,128]{1,0:T(8,128)S(1)}, u32[]{:S(2)}, u32[]{:S(2)}) collective-permute-start(f32[368,128]{1,0:T(8,128)S(1)} %get-tuple-element.47), channel_id=1, source_target_pairs={{0,48},{1,49},{2,50},{3,51},{4,52},{5,53},{6,54},{7,55},{8,56},{9,... | collective-permute-start | bytes 565256 | tf_op jit(solution)/shard_map/ppermute | solution.py:41
  21.2 7.2 %collective-permute-start.8 = (f32[368,128]{1,0:T(8,128)S(1)}, f32[368,128]{1,0:T(8,128)S(1)}, u32[]{:S(2)}, u32[]{:S(2)}) collective-permute-start(f32[368,128]{1,0:T(8,128)S(1)} %get-tuple-element.48), channel_id=1, source_target_pairs={{0,32},{1,33},{2,34},{3,35},{4,36},{5,37},{6,38},{7,39},{8,40},{9,... | collective-permute-start | bytes 565256 | tf_op jit(solution)/shard_map/ppermute | solution.py:41
  21.8 9.9 %collective-permute-start.13 = (f32[352,128]{1,0:T(8,128)S(1)}, f32[352,128]{1,0:T(8,128)S(1)}, u32[]{:S(2)}, u32[]{:S(2)}) collective-permute-start(f32[352,128]{1,0:T(8,128)S(1)} %get-tuple-element.60), channel_id=1, source_target_pairs={{0,16},{1,17},{2,18},{3,19},{4,20},{5,21},{6,22},{7,23},{8,24},{9,... | collective-permute-start | bytes 540680 | tf_op jit(solution)/shard_map/ppermute | solution.py:41
  23.2 10.0 %collective-permute-start.14 = (f32[352,128]{1,0:T(8,128)S(1)}, f32[352,128]{1,0:T(8,128)S(1)}, u32[]{:S(2)}, u32[]{:S(2)}) collective-permute-start(f32[352,128]{1,0:T(8,128)S(1)} %get-tuple-element.61), channel_id=1, source_target_pairs={{0,48},{1,49},{2,50},{3,51},{4,52},{5,53},{6,54},{7,55},{8,56},{9,... | collective-permute-start | bytes 540680 | tf_op jit(solution)/shard_map/ppermute | solution.py:41
  25.3 9.3 %collective-permute-start.15 = (f32[352,128]{1,0:T(8,128)S(1)}, f32[352,128]{1,0:T(8,128)S(1)}, u32[]{:S(2)}, u32[]{:S(2)}) collective-permute-start(f32[352,128]{1,0:T(8,128)S(1)} %get-tuple-element.62), channel_id=1, source_target_pairs={{0,32},{1,33},{2,34},{3,35},{4,36},{5,37},{6,38},{7,39},{8,40},{9,... | collective-permute-start | bytes 540680 | tf_op jit(solution)/shard_map/ppermute | solution.py:41
  29.5 8.0 %collective-permute-start.12 = (f32[512,128]{1,0:T(8,128)S(1)}, f32[512,128]{1,0:T(8,128)S(1)}, u32[]{:S(2)}, u32[]{:S(2)}) collective-permute-start(f32[512,128]{1,0:T(8,128)S(1)} %shard_map.91), channel_id=1, source_target_pairs={{0,128},{1,129},{2,130},{3,131},{4,132},{5,133},{6,134},{7,135},{8... | collective-permute-start | bytes 786440 | tf_op jit(solution)/shard_map/ppermute | solution.py:41
  30.8 8.3 %collective-permute-start.11 = (f32[512,128]{1,0:T(8,128)S(1)}, f32[512,128]{1,0:T(8,128)S(1)}, u32[]{:S(2)}, u32[]{:S(2)}) collective-permute-start(f32[512,128]{1,0:T(8,128)S(1)} %get-tuple-element.52), channel_id=1, source_target_pairs={{0,8},{1,9},{2,10},{3,11},{4,12},{5,13},{6,14},{7,15},{8,128},{9,1... | collective-permute-start | bytes 786440 | tf_op jit(solution)/shard_map/ppermute | solution.py:41
  35.2 6.4 %collective-permute-start.16 = (f32[512,128]{1,0:T(8,128)S(1)}, f32[512,128]{1,0:T(8,128)S(1)}, u32[]{:S(2)}, u32[]{:S(2)}) collective-permute-start(f32[512,128]{1,0:T(8,128)S(1)} %shard_map.94), channel_id=1, source_target_pairs={{0,136},{1,137},{2,138},{3,139},{4,140},{5,141},{6,142},{7,143},{8... | collective-permute-start | bytes 786440 | tf_op jit(solution)/shard_map/ppermute | solution.py:41

commit v7 on v6

--- a/solution.py
+++ b/solution.py
@@ -348,7 +348,7 @@
     far = send(from_below, along(1))
     far_across = send(above_across, along(-1))
     firsts, seconds = list(firsts_and_seconds[:4]), list(firsts_and_seconds[4:])
-    firsts[1], below_across, from_above = lax.optimization_barrier((firsts[1], below_across, from_above))
+    firsts[3], below_across, from_above = lax.optimization_barrier((firsts[3], below_across, from_above))
     right_second = right_of(below_across, from_above, flops=GUIDE)
     right_rest = right_of(arrived, far, far_across, flops=GUIDE)
 

time: 60.4 us -> 61.9 us (1.025)
  waiting for transfers between devices: 11.8 us -> 13.8 us
    ppermute x17, waiting for transfers between devices: 11.8 us -> 13.8 us  [send(): return lax.ppermute(value, AXES, pairs(target))]
  transfers between devices with their start and end apart: 17 -> 17, of which waited for: 10 -> 9; matrix products, arithmetic and copies ran while one was open for 0% -> 0% of each run, Pallas kernels for 11% -> 11%
where the time goes in v7:
time: 61.9 us; the launch traced here: 61.7 us
  starting transfers between devices  20.8 us (34%)
  blocking collectives  17.8 us (29%)
  waiting for transfers between devices  13.8 us (22%)
  Pallas kernels  8.47 us (14%)
  between operations  0.77 us (1%)
    ppermute x17, starting transfers between devices, send(): return lax.ppermute(value, AXES, pairs(target))  20.8 us
    all_to_all x1, blocking collectives, on_device(): rows = lax.all_to_all(rows.reshape(8, PACKED, LANES), 'z', 0, 0, tiled=True)  17.8 us
    ppermute x17, waiting for transfers between devices, send(): return lax.ppermute(value, AXES, pairs(target))  13.8 us
    pallas_call x4, Pallas kernels, multiply(): call(functools.partial(product, half, blocks, steps), outs, scratch=[pltp...  2.15 us
    pallas_call x1, Pallas kernels, on_device(): call(statistics, [f32(2, H), f32(1, H), f32(ROWS, H), f32(ROWS, H), jax.S...  2.06 us
  transfers between devices with their start and end apart: 17, of which 9 were waited for; matrix products, arithmetic and copies ran while one was open for 0% of the time, Pallas kernels for 11%

profile of v7, /device:TPU:8, one launch (start us, length us, event | category | flops | bytes accessed | tf_op | source)
XLA Modules:
  0.0 61.7 jit_solution(9494492750405871084)
XLA Ops:
  0.6 1.0 %shard_map.84.wide.refs_0_ = f32[704,128]{1,0:T(8,128)S(1)} custom-call(bf16[704,128]{1,0:T(8,128)(2,1)} %bitcast.6), custom_call_target="tpu_custom_call" | custom-call | bytes 540000 | tf_op jit(solution)/shard_map/pallas_call | solution.py:305
  1.7 1.6 %collective-permute-start.2 = (f32[704,128]{1,0:T(8,128)S(1)}, f32[704,128]{1,0:T(8,128)S(1)}, u32[]{:S(2)}, u32[]{:S(2)}) collective-permute-start(f32[704,128]{1,0:T(8,128)S(1)} %shard_map.84.wide.refs_0_), channel_id=1, source_target_pairs={{0,16},{1,17},{2,18},{3,19},{4,20},{5,21},{6,22},{7,23},{8,24},{9,... | collective-permute-start | bytes 1081352 | tf_op jit(solution)/shard_map/ppermute | solution.py:41
  3.3 2.1 %shard_map.83 = (f32[2,2816]{1,0:T(2,128)S(1)}, f32[1,2816]{1,0:T(1,128)S(1)}, f32[128,2816]{1,0:T(8,128)S(1)}, f32[128,2816]{1,0:T(8,128)S(1)}, bf16[128,2816]{1,0:T(8,128)(2,1)S(1)}) custom-call(bf16[128,2816]{1,0:T(8,128)(2,1)} %pre_gelu_hbm.1, bf16[128,2816]{1,0:T(8,128)(2,1)} %out_grad_hbm.1), custom_call_target="tpu_custom_call" | custom-call | bytes 4400000 | tf_op jit(solution)/shard_map/pallas_call | solution.py:312
  5.3 2.0 %collective-permute-start = (f32[2,2816]{1,0:T(2,128)S(1)}, f32[2,2816]{1,0:T(2,128)S(1)}, u32[]{:S(2)}, u32[]{:S(2)}) collective-permute-start(f32[2,2816]{1,0:T(2,128)S(1)} %get-tuple-element.36.sums), channel_id=1, source_target_pairs={{0,1},{1,0},{2,3},{3,2},{4,5},{5,4},{6,7},{7,6},{8,9},{9,8},{10,11... | collective-permute-start | bytes 67592 | tf_op jit(solution)/shard_map/ppermute | solution.py:41
  7.4 3.2 %collective-permute-start.5 = (f32[704,128]{1,0:T(8,128)S(1)}, f32[704,128]{1,0:T(8,128)S(1)}, u32[]{:S(2)}, u32[]{:S(2)}) collective-permute-start(f32[704,128]{1,0:T(8,128)S(1)} %shard_map.84.wide.refs_0_), channel_id=1, source_target_pairs={{0,72},{1,73},{2,74},{3,75},{4,76},{5,77},{6,78},{7,79},{8,192},{9... | collective-permute-start | bytes 1081352 | tf_op jit(solution)/shard_map/ppermute | solution.py:41
  10.5 0.8 %collective-permute-start.6 = (f32[704,128]{1,0:T(8,128)S(1)}, f32[704,128]{1,0:T(8,128)S(1)}, u32[]{:S(2)}, u32[]{:S(2)}) collective-permute-start(f32[704,128]{1,0:T(8,128)S(1)} %shard_map.84.wide.refs_0_), channel_id=1, source_target_pairs={{0,48},{1,49},{2,50},{3,51},{4,52},{5,53},{6,54},{7,55},{8,56},{9,... | collective-permute-start | bytes 1081352 | tf_op jit(solution)/shard_map/ppermute | solution.py:41
  11.4 0.9 %shard_map.85 = (bf16[128,2816]{1,0:T(8,128)(2,1)S(1)}, f32[1440,128]{1,0:T(8,128)S(1)}, f32[2144,128]{1,0:T(8,128)S(1)}) custom-call(f32[2,2816]{1,0:T(2,128)S(1)} %get-tuple-element.36.sums, f32[2,2816]{1,0:T(2,128)S(1)} %collective-permute-done.other, f32[1,2816]{1,0:T(1,128)S(1)} %get-tuple-element.37.shift, f32[1,2816]{1,0:T(1,128)S(1)} %reshape.25.gain, ...), custom_call_target="tpu_custom_call" | custom-call | bytes 6000000 | tf_op jit(solution)/shard_map/pallas_call | solution.py:331
  12.5 1.7 %collective-permute-start.10 = (f32[704,128]{1,0:T(8,128)S(1)}, f32[704,128]{1,0:T(8,128)S(1)}, u32[]{:S(2)}, u32[]{:S(2)}) collective-permute-start(f32[704,128]{1,0:T(8,128)S(1)} %collective-permute-done.3.refs_2_), channel_id=1, source_target_pairs={{0,48},{1,49},{2,50},{3,51},{4,52},{5,53},{6,54},{7,55},{8,56},{9,... | collective-permute-start | bytes 1081352 | tf_op jit(solution)/shard_map/ppermute | solution.py:41
  15.2 0.7 %collective-permute-done.5.refs_0_ = f32[704,128]{1,0:T(8,128)S(1)} collective-permute-done((f32[704,128]{1,0:T(8,128)S(1)}, f32[704,128]{1,0:T(8,128)S(1)}, u32[]{:S(2)}, u32[]{:S(2)}) %collective-permute-start.5) | collective-permute-done | bytes 360480 | tf_op jit(solution)/shard_map/ppermute | solution.py:41
  15.8 2.1 %collective-permute-done.6.refs_1_ = f32[704,128]{1,0:T(8,128)S(1)} collective-permute-done((f32[704,128]{1,0:T(8,128)S(1)}, f32[704,128]{1,0:T(8,128)S(1)}, u32[]{:S(2)}, u32[]{:S(2)}) %collective-permute-start.6) | collective-permute-done | bytes 360480 | tf_op jit(solution)/shard_map/ppermute | solution.py:41
  18.0 2.0 %collective-permute-start.7 = (f32[368,128]{1,0:T(8,128)S(1)}, f32[368,128]{1,0:T(8,128)S(1)}, u32[]{:S(2)}, u32[]{:S(2)}) collective-permute-start(f32[368,128]{1,0:T(8,128)S(1)} %get-tuple-element.47), channel_id=1, source_target_pairs={{0,48},{1,49},{2,50},{3,51},{4,52},{5,53},{6,54},{7,55},{8,56},{9,... | collective-permute-start | bytes 565256 | tf_op jit(solution)/shard_map/ppermute | solution.py:41
  20.0 1.5 %collective-permute-start.8 = (f32[368,128]{1,0:T(8,128)S(1)}, f32[368,128]{1,0:T(8,128)S(1)}, u32[]{:S(2)}, u32[]{:S(2)}) collective-permute-start(f32[368,128]{1,0:T(8,128)S(1)} %get-tuple-element.48), channel_id=1, source_target_pairs={{0,32},{1,33},{2,34},{3,35},{4,36},{5,37},{6,38},{7,39},{8,40},{9,... | collective-permute-start | bytes 565256 | tf_op jit(solution)/shard_map/ppermute | solution.py:41
  21.8 2.5 %collective-permute-start.13 = (f32[352,128]{1,0:T(8,128)S(1)}, f32[352,128]{1,0:T(8,128)S(1)}, u32[]{:S(2)}, u32[]{:S(2)}) collective-permute-start(f32[352,128]{1,0:T(8,128)S(1)} %get-tuple-element.60), channel_id=1, source_target_pairs={{0,16},{1,17},{2,18},{3,19},{4,20},{5,21},{6,22},{7,23},{8,24},{9,... | collective-permute-start | bytes 540680 | tf_op jit(solution)/shard_map/ppermute | solution.py:41
  24.4 0.7 %collective-permute-start.14 = (f32[352,128]{1,0:T(8,128)S(1)}, f32[352,128]{1,0:T(8,128)S(1)}, u32[]{:S(2)}, u32[]{:S(2)}) collective-permute-start(f32[352,128]{1,0:T(8,128)S(1)} %get-tuple-element.61), channel_id=1, source_target_pairs={{0,48},{1,49},{2,50},{3,51},{4,52},{5,53},{6,54},{7,55},{8,56},{9,... | collective-permute-start | bytes 540680 | tf_op jit(solution)/shard_map/ppermute | solution.py:41
  25.3 1.7 %collective-permute-start.15 = (f32[352,128]{1,0:T(8,128)S(1)}, f32[352,128]{1,0:T(8,128)S(1)}, u32[]{:S(2)}, u32[]{:S(2)}) collective-permute-start(f32[352,128]{1,0:T(8,128)S(1)} %get-tuple-element.62), channel_id=1, source_target_pairs={{0,32},{1,33},{2,34},{3,35},{4,36},{5,37},{6,38},{7,39},{8,40},{9,... | collective-permute-start | bytes 540680 | tf_op jit(solution)/shard_map/ppermute | solution.py:41
  27.1 1.8 %collective-permute-done.4.refs_0_ = f32[368,128]{1,0:T(8,128)S(1)} collective-permute-done((f32[368,128]{1,0:T(8,128)S(1)}, f32[368,128]{1,0:T(8,128)S(1)}, u32[]{:S(2)}, u32[]{:S(2)}) %collective-permute-start.4) | collective-permute-done | bytes 188448 | tf_op jit(solution)/shard_map/ppermute | solution.py:41
  29.9 1.3 %collective-permute-start.12 = (f32[512,128]{1,0:T(8,128)S(1)}, f32[512,128]{1,0:T(8,128)S(1)}, u32[]{:S(2)}, u32[]{:S(2)}) collective-permute-start(f32[512,128]{1,0:T(8,128)S(1)} %shard_map.91), channel_id=1, source_target_pairs={{0,128},{1,129},{2,130},{3,131},{4,132},{5,133},{6,134},{7,135},{8... | collective-permute-start | bytes 786440 | tf_op jit(solution)/shard_map/ppermute | solution.py:41
  31.2 1.0 %collective-permute-start.11 = (f32[512,128]{1,0:T(8,128)S(1)}, f32[512,128]{1,0:T(8,128)S(1)}, u32[]{:S(2)}, u32[]{:S(2)}) collective-permute-start(f32[512,128]{1,0:T(8,128)S(1)} %get-tuple-element.52), channel_id=1, source_target_pairs={{0,8},{1,9},{2,10},{3,11},{4,12},{5,13},{6,14},{7,15},{8,128},{9,1... | collective-permute-start | bytes 786440 | tf_op jit(solution)/shard_map/ppermute | solution.py:41
  32.2 3.9 %collective-permute-done.13.refs_0_ = f32[352,128]{1,0:T(8,128)S(1)} collective-permute-done((f32[352,128]{1,0:T(8,128)S(1)}, f32[352,128]{1,0:T(8,128)S(1)}, u32[]{:S(2)}, u32[]{:S(2)}) %collective-permute-start.13) | collective-permute-done | bytes 180256 | tf_op jit(solution)/shard_map/ppermute | solution.py:41
  37.9 1.7 %collective-permute-done.11.refs_0_ = f32[512,128]{1,0:T(8,128)S(1)} collective-permute-done((f32[512,128]{1,0:T(8,128)S(1)}, f32[512,128]{1,0:T(8,128)S(1)}, u32[]{:S(2)}, u32[]{:S(2)}) %collective-permute-start.11) | collective-permute-done | bytes 262176 | tf_op jit(solution)/shard_map/ppermute | solution.py:41
  39.6 0.9 %shard_map.93 = bf16[128,2816]{1,0:T(8,128)(2,1)} custom-call(bf16[128,2816]{1,0:T(8,128)(2,1)S(1)} %get-tuple-element.56.value), custom_call_target="tpu_custom_call" | custom-call | bytes 1440000 | tf_op jit(solution)/shard_map/pallas_call | solution.py:382
  40.5 2.6 %collective-permute-done.16.refs_1_ = f32[512,128]{1,0:T(8,128)S(1)} collective-permute-done((f32[512,128]{1,0:T(8,128)S(1)}, f32[512,128]{1,0:T(8,128)S(1)}, u32[]{:S(2)}, u32[]{:S(2)}) %collective-permute-start.16) | collective-permute-done | bytes 262176 | tf_op jit(solution)/shard_map/ppermute | solution.py:41
  43.2 17.8 %all_to_all.5.parts = f32[8,64,128]{2,1,0:T(8,128)S(1)} all-to-all(f32[8,64,128]{2,1,0:T(8,128)S(1)} %bitcast.5), channel_id=1, replica_groups=mesh['yh'=2,'core'=2,'x'=4,'yl'=2,'z'=8] {'z'}, dimensions={0} | all-to-all | bytes 524288 | tf_op jit(solution)/shard_map/all_to_all | solution.py:395
  61.0 0.7 %shard_map.97 = (f32[11,704]{1,0:T(8,128)}, f32[1,11]{1,0:T(1,128)}, f32[1,11]{1,0:T(1,128)}, f32[1,11]{1,0:T(1,128)}) custom-call(f32[8,64,128]{2,1,0:T(8,128)S(1)} %all_to_all.5.parts), custom_call_target="tpu_custom_call" | custom-call | bytes 330000 | tf_op jit(solution)/shard_map/pallas_call | solution.py:396
  (29 shorter events, 4.8 us)
Async XLA Ops:
  0.6 10.7 %copy-start = (f32[2816]{0:T(1024)S(1)}, f32[2816]{0:T(1024)}, u32[]{:S(2)}) copy-start(f32[2816]{0:T(1024)} %param.7) | copy-start | bytes 33796
  1.6 10.9 %collective-permute-start.3 = (f32[704,128]{1,0:T(8,128)S(1)}, f32[704,128]{1,0:T(8,128)S(1)}, u32[]{:S(2)}, u32[]{:S(2)}) collective-permute-start(f32[704,128]{1,0:T(8,128)S(1)} %shard_map.84.wide.refs_0_), channel_id=1, source_target_pairs={{0,200},{1,201},{2,202},{3,203},{4,204},{5,205},{6,206},{7,207},{8... | collective-permute-start | bytes 1081352 | tf_op jit(solution)/shard_map/ppermute | solution.py:41
  1.7 12.5 %collective-permute-start.2 = (f32[704,128]{1,0:T(8,128)S(1)}, f32[704,128]{1,0:T(8,128)S(1)}, u32[]{:S(2)}, u32[]{:S(2)}) collective-permute-start(f32[704,128]{1,0:T(8,128)S(1)} %shard_map.84.wide.refs_0_), channel_id=1, source_target_pairs={{0,16},{1,17},{2,18},{3,19},{4,20},{5,21},{6,22},{7,23},{8,24},{9,... | collective-permute-start | bytes 1081352 | tf_op jit(solution)/shard_map/ppermute | solution.py:41
  5.3 6.0 %collective-permute-start = (f32[2,2816]{1,0:T(2,128)S(1)}, f32[2,2816]{1,0:T(2,128)S(1)}, u32[]{:S(2)}, u32[]{:S(2)}) collective-permute-start(f32[2,2816]{1,0:T(2,128)S(1)} %get-tuple-element.36.sums), channel_id=1, source_target_pairs={{0,1},{1,0},{2,3},{3,2},{4,5},{5,4},{6,7},{7,6},{8,9},{9,8},{10,11... | collective-permute-start | bytes 67592 | tf_op jit(solution)/shard_map/ppermute | solution.py:41
  7.4 8.5 %collective-permute-start.5 = (f32[704,128]{1,0:T(8,128)S(1)}, f32[704,128]{1,0:T(8,128)S(1)}, u32[]{:S(2)}, u32[]{:S(2)}) collective-permute-start(f32[704,128]{1,0:T(8,128)S(1)} %shard_map.84.wide.refs_0_), channel_id=1, source_target_pairs={{0,72},{1,73},{2,74},{3,75},{4,76},{5,77},{6,78},{7,79},{8,192},{9... | collective-permute-start | bytes 1081352 | tf_op jit(solution)/shard_map/ppermute | solution.py:41
  10.5 7.4 %collective-permute-start.6 = (f32[704,128]{1,0:T(8,128)S(1)}, f32[704,128]{1,0:T(8,128)S(1)}, u32[]{:S(2)}, u32[]{:S(2)}) collective-permute-start(f32[704,128]{1,0:T(8,128)S(1)} %shard_map.84.wide.refs_0_), channel_id=1, source_target_pairs={{0,48},{1,49},{2,50},{3,51},{4,52},{5,53},{6,54},{7,55},{8,56},{9,... | collective-permute-start | bytes 1081352 | tf_op jit(solution)/shard_map/ppermute | solution.py:41
  12.3 2.8 %collective-permute-start.1 = (f32[2144,128]{1,0:T(8,128)S(1)}, f32[2144,128]{1,0:T(8,128)S(1)}, u32[]{:S(2)}, u32[]{:S(2)}) collective-permute-start(f32[2144,128]{1,0:T(8,128)S(1)} %get-tuple-element.42), channel_id=1, source_target_pairs={{0,64},{1,65},{2,66},{3,67},{4,68},{5,69},{6,70},{7,71},{8,72},{9,... | collective-permute-start | bytes 3293192 | tf_op jit(solution)/shard_map/ppermute | solution.py:41
  12.5 9.4 %collective-permute-start.10 = (f32[704,128]{1,0:T(8,128)S(1)}, f32[704,128]{1,0:T(8,128)S(1)}, u32[]{:S(2)}, u32[]{:S(2)}) collective-permute-start(f32[704,128]{1,0:T(8,128)S(1)} %collective-permute-done.3.refs_2_), channel_id=1, source_target_pairs={{0,48},{1,49},{2,50},{3,51},{4,52},{5,53},{6,54},{7,55},{8,56},{9,... | collective-permute-start | bytes 1081352 | tf_op jit(solution)/shard_map/ppermute | solution.py:41
  14.5 9.9 %collective-permute-start.9 = (f32[704,128]{1,0:T(8,128)S(1)}, f32[704,128]{1,0:T(8,128)S(1)}, u32[]{:S(2)}, u32[]{:S(2)}) collective-permute-start(f32[704,128]{1,0:T(8,128)S(1)} %collective-permute-done.2.refs_1_), channel_id=1, source_target_pairs={{0,16},{1,17},{2,18},{3,19},{4,20},{5,21},{6,22},{7,23},{8,24},{9,... | collective-permute-start | bytes 1081352 | tf_op jit(solution)/shard_map/ppermute | solution.py:41
  18.0 7.4 %collective-permute-start.7 = (f32[368,128]{1,0:T(8,128)S(1)}, f32[368,128]{1,0:T(8,128)S(1)}, u32[]{:S(2)}, u32[]{:S(2)}) collective-permute-start(f32[368,128]{1,0:T(8,128)S(1)} %get-tuple-element.47), channel_id=1, source_target_pairs={{0,48},{1,49},{2,50},{3,51},{4,52},{5,53},{6,54},{7,55},{8,56},{9,... | collective-permute-start | bytes 565256 | tf_op jit(solution)/shard_map/ppermute | solution.py:41
  20.0 8.8 %collective-permute-start.4 = (f32[368,128]{1,0:T(8,128)S(1)}, f32[368,128]{1,0:T(8,128)S(1)}, u32[]{:S(2)}, u32[]{:S(2)}) collective-permute-start(f32[368,128]{1,0:T(8,128)S(1)} %get-tuple-element.45), channel_id=1, source_target_pairs={{0,16},{1,17},{2,18},{3,19},{4,20},{5,21},{6,22},{7,23},{8,24},{9,... | collective-permute-start | bytes 565256 | tf_op jit(solution)/shard_map/ppermute | solution.py:41
  20.0 8.8 %collective-permute-start.8 = (f32[368,128]{1,0:T(8,128)S(1)}, f32[368,128]{1,0:T(8,128)S(1)}, u32[]{:S(2)}, u32[]{:S(2)}) collective-permute-start(f32[368,128]{1,0:T(8,128)S(1)} %get-tuple-element.48), channel_id=1, source_target_pairs={{0,32},{1,33},{2,34},{3,35},{4,36},{5,37},{6,38},{7,39},{8,40},{9,... | collective-permute-start | bytes 565256 | tf_op jit(solution)/shard_map/ppermute | solution.py:41
  21.8 14.3 %collective-permute-start.13 = (f32[352,128]{1,0:T(8,128)S(1)}, f32[352,128]{1,0:T(8,128)S(1)}, u32[]{:S(2)}, u32[]{:S(2)}) collective-permute-start(f32[352,128]{1,0:T(8,128)S(1)} %get-tuple-element.60), channel_id=1, source_target_pairs={{0,16},{1,17},{2,18},{3,19},{4,20},{5,21},{6,22},{7,23},{8,24},{9,... | collective-permute-start | bytes 540680 | tf_op jit(solution)/shard_map/ppermute | solution.py:41
  24.4 11.7 %collective-permute-start.14 = (f32[352,128]{1,0:T(8,128)S(1)}, f32[352,128]{1,0:T(8,128)S(1)}, u32[]{:S(2)}, u32[]{:S(2)}) collective-permute-start(f32[352,128]{1,0:T(8,128)S(1)} %get-tuple-element.61), channel_id=1, source_target_pairs={{0,48},{1,49},{2,50},{3,51},{4,52},{5,53},{6,54},{7,55},{8,56},{9,... | collective-permute-start | bytes 540680 | tf_op jit(solution)/shard_map/ppermute | solution.py:41
  25.3 10.8 %collective-permute-start.15 = (f32[352,128]{1,0:T(8,128)S(1)}, f32[352,128]{1,0:T(8,128)S(1)}, u32[]{:S(2)}, u32[]{:S(2)}) collective-permute-start(f32[352,128]{1,0:T(8,128)S(1)} %get-tuple-element.62), channel_id=1, source_target_pairs={{0,32},{1,33},{2,34},{3,35},{4,36},{5,37},{6,38},{7,39},{8,40},{9,... | collective-permute-start | bytes 540680 | tf_op jit(solution)/shard_map/ppermute | solution.py:41
  29.9 8.0 %collective-permute-start.12 = (f32[512,128]{1,0:T(8,128)S(1)}, f32[512,128]{1,0:T(8,128)S(1)}, u32[]{:S(2)}, u32[]{:S(2)}) collective-permute-start(f32[512,128]{1,0:T(8,128)S(1)} %shard_map.91), channel_id=1, source_target_pairs={{0,128},{1,129},{2,130},{3,131},{4,132},{5,133},{6,134},{7,135},{8... | collective-permute-start | bytes 786440 | tf_op jit(solution)/shard_map/ppermute | solution.py:41
  31.2 8.3 %collective-permute-start.11 = (f32[512,128]{1,0:T(8,128)S(1)}, f32[512,128]{1,0:T(8,128)S(1)}, u32[]{:S(2)}, u32[]{:S(2)}) collective-permute-start(f32[512,128]{1,0:T(8,128)S(1)} %get-tuple-element.52), channel_id=1, source_target_pairs={{0,8},{1,9},{2,10},{3,11},{4,12},{5,13},{6,14},{7,15},{8,128},{9,1... | collective-permute-start | bytes 786440 | tf_op jit(solution)/shard_map/ppermute | solution.py:41
  36.7 6.4 %collective-permute-start.16 = (f32[512,128]{1,0:T(8,128)S(1)}, f32[512,128]{1,0:T(8,128)S(1)}, u32[]{:S(2)}, u32[]{:S(2)}) collective-permute-start(f32[512,128]{1,0:T(8,128)S(1)} %shard_map.94), channel_id=1, source_target_pairs={{0,136},{1,137},{2,138},{3,139},{4,140},{5,141},{6,142},{7,143},{8... | collective-permute-start | bytes 786440 | tf_op jit(solution)/shard_map/ppermute | solution.py:41
